TPU v7x, 32 devices: a whole 2x2x4 slice. The times are simulated.
32 devices in a mesh: dp: 8 (over z, y), chan: 4 (over x, core).
Axes of the slice: x: 2, y: 2, z: 4, core: 2. Of those that a mesh axis runs over, the one named last changes fastest.
Arguments:
- inputs: bfloat16 [32768, 1024], P('dp', 'chan'), may hold values from -6 to 6
- resolution: int32 [128], P('dp'), may hold values from 0 to 2, as said below
- reduce_weight: bfloat16 [1024, 256], replicated, may hold values from -0.1875 to 0.1875
- first_gain: float32 [256], P('chan'), may hold values from 0.5 to 1.5
- first_shift: float32 [256], P('chan'), may hold values from -3 to 3
- split_weight: bfloat16 [9, 128, 512], P(None, None, 'chan'), may hold values from -0.1875 to 0.1875
- second_gain: float32 [512], P('chan'), may hold values from 0.5 to 1.5
- second_shift: float32 [512], P('chan'), may hold values from -3 to 3
- gate_down: float32 [256, 128], replicated, may hold values from -0.375 to 0.375
- gate_gain: float32 [128], replicated, may hold values from 0.5 to 1.5
- gate_shift: float32 [128], replicated, may hold values from -3 to 3
- gate_up: float32 [128, 512], replicated, may hold values from -0.5 to 0.5
- gate_bias: float32 [512], replicated, may hold values from -3 to 3
- expand_weight: bfloat16 [256, 1024], P(None, 'chan'), may hold values from -0.375 to 0.375
- third_gain: float32 [1024], P('chan'), may hold values from 0.5 to 1.5
- third_shift: float32 [1024], P('chan'), may hold values from -3 to 3
- cotangent: bfloat16 [32768, 1024], P('dp', 'chan'), may hold values from -6 to 6
Outputs:
- block_out: bfloat16 [32768, 1024], P('dp', 'chan')
- inputs_grad: bfloat16 [32768, 1024], P('dp', 'chan')
- reduce_grad: float32 [1024, 256], P(None, 'chan')
- first_gain_grad: float32 [256], P('chan')
- first_shift_grad: float32 [256], P('chan')
- split_grad: float32 [9, 128, 512], P(None, None, 'chan')
- second_gain_grad: float32 [512], P('chan')
- second_shift_grad: float32 [512], P('chan')
- down_grad: float32 [256, 128], P(None, 'chan')
- gate_gain_grad: float32 [128], P('chan')
- gate_shift_grad: float32 [128], P('chan')
- up_grad: float32 [128, 512], P(None, 'chan')
- bias_grad: float32 [512], P('chan')
- expand_grad: float32 [256, 1024], P(None, 'chan')
- third_gain_grad: float32 [1024], P('chan')
- third_shift_grad: float32 [1024], P('chan')
Inputs may be any that keep to these rules, and one draw needn't show every extreme that they name: Image i has side 12 + 2 * resolution[i] pixels inside its 16 x 16 slot; group 2 fills the slot.
All inputs are finite; a program needn't handle non-finite values.
Results may differ from a plain program's by a relative error of at most 0.02.
Values may be sent and summed in bfloat16 or wider, within the bound.
A program may use at most 128 MiB of HBM per device.

v0:
```python
import jax
import jax.numpy as jnp
from jax import lax
from jax.sharding import PartitionSpec as P

SIDE = 16


eps = 1e-05
highest = lax.Precision.HIGHEST


def partner(value, axis, distance):
    return lax.ppermute(value, axis, [(i, i ^ 1 << distance) for i in range(lax.axis_size(axis))])


def silu_slope(values):
    sigma = jax.nn.sigmoid(values)
    return sigma * (1.0 + values * (1.0 - sigma))


def normalize(values, weight, gain, shift):
    count = jnp.sum(weight)
    first = jnp.sum(weight * values, 0)
    second = jnp.sum(weight * values * values, 0)
    count, first, second = lax.psum((count, first, second), "dp")
    mean = first / count
    scale = lax.rsqrt(second / count - mean * mean + eps)
    normed = (values - mean) * scale
    return (gain * normed + shift, (normed, scale, count))


def denormalize(grads, saved, gain, weight):
    normed, scale, count = saved
    total = jnp.sum(grads, 0)
    cross = jnp.sum(grads * normed, 0)
    total, cross = lax.psum((total, cross), "dp")
    result = gain * scale * (grads - total / count - normed * cross / count) * weight
    return (result, cross, total)


def radix_weights(logits, width):
    first = logits[:, :width]
    second = logits[:, width:]
    top = jnp.maximum(first, second)
    upper = jnp.exp(first - top)
    lower = jnp.exp(second - top)
    total = upper + lower
    return jnp.concatenate([upper / total, lower / total], 1)


def group_collect(piece, place, levels):
    for bit in range(levels):
        other = partner(piece, "chan", bit)
        high = place >> bit & 1 == 1
        piece = jnp.where(
            high, jnp.concatenate([other, piece], 1), jnp.concatenate([piece, other], 1)
        )
    return piece


def group_reduce(block, place, levels):
    for bit in reversed(range(levels)):
        size = block.shape[1] // 2
        lower = block[:, :size]
        upper = block[:, size:]
        high = place >> bit & 1 == 1
        outgoing = jnp.where(high, lower, upper)
        keeping = jnp.where(high, upper, lower)
        block = keeping + partner(outgoing.astype(jnp.bfloat16), "chan", bit).astype(outgoing.dtype)
    return block


def per_device(
    inputs,
    resolution,
    reduce_weight,
    first_gain,
    first_shift,
    split_weight,
    second_gain,
    second_shift,
    gate_down,
    gate_gain,
    gate_shift,
    gate_up,
    gate_bias,
    expand_weight,
    third_gain,
    third_shift,
    cotangent,
):
    parts = lax.axis_size("chan")
    place = lax.axis_index("chan")
    levels = (parts // 2).bit_length() - 1
    images = resolution.shape[0]
    rows = inputs.shape[0]
    cells = rows // images
    width = reduce_weight.shape[1]
    inner = gate_down.shape[1]
    half = width // 2
    mine_one = width // parts
    mine_two = 2 * width // parts
    mine_gate = inner // parts
    sides = 12 + 2 * resolution
    places = jnp.arange(SIDE)
    valid = (
        (places[None, :, None] < sides[:, None, None])
        & (places[None, None, :] < sides[:, None, None])
    ).astype(jnp.float32)
    pixel_mask = valid.reshape(rows, 1)
    pixels = (sides * sides).astype(jnp.float32)
    image_ones = jnp.ones((images, 1), jnp.float32)
    inputs_wide = inputs.astype(jnp.float32)
    features_all = lax.all_gather(inputs, "chan", axis=1, tiled=True)
    reduce_cols = lax.dynamic_slice_in_dim(reduce_weight, place * mine_one, mine_one, 1)
    reduced = jnp.dot(features_all, reduce_cols, preferred_element_type=jnp.float32)
    first_norm, first_saved = normalize(reduced, pixel_mask, first_gain, first_shift)
    first_act = (pixel_mask * jax.nn.silu(first_norm)).astype(jnp.bfloat16)
    group_act = group_collect(first_act, place, levels)
    padded_act = jnp.pad(
        group_act.reshape(images, SIDE, SIDE, half), ((0, 0), (1, 1), (1, 1), (0, 0))
    )
    splits = jnp.zeros((rows, mine_two), jnp.float32)
    for row_tap in range(3):
        for col_tap in range(3):
            shifted = padded_act[:, row_tap : row_tap + SIDE, col_tap : col_tap + SIDE, :].reshape(
                rows, half
            )
            splits = splits + jnp.dot(
                shifted, split_weight[row_tap * 3 + col_tap], preferred_element_type=jnp.float32
            )
    second_norm, second_saved = normalize(splits, pixel_mask, second_gain, second_shift)
    second_act = pixel_mask * jax.nn.silu(second_norm)
    per_image = second_act.reshape(images, cells, mine_two)
    pooled_mine = jnp.sum(per_image, 1) / pixels[:, None]
    pooled = lax.all_gather(pooled_mine, "chan", axis=1, tiled=True)
    summary = pooled[:, :width] + pooled[:, width:]
    squeezed_pre = jnp.dot(summary, gate_down, precision=highest)
    gate_norm, gate_saved = normalize(squeezed_pre, image_ones, gate_gain, gate_shift)
    squeezed = jax.nn.silu(gate_norm)
    logits = jnp.dot(squeezed, gate_up, precision=highest) + gate_bias
    attention = radix_weights(logits, width)
    attention_mine = lax.dynamic_slice_in_dim(attention, place * mine_two, mine_two, 1)
    weighted = (per_image * attention_mine[:, None, :]).astype(jnp.bfloat16).reshape(rows, mine_two)
    weighted_all = lax.all_gather(weighted, "chan", axis=1, tiled=True)
    merged = (
        weighted_all[:, :width].astype(jnp.float32) + weighted_all[:, width:].astype(jnp.float32)
    ).astype(jnp.bfloat16)
    expanded = jnp.dot(merged, expand_weight, preferred_element_type=jnp.float32)
    third_norm, third_saved = normalize(expanded, pixel_mask, third_gain, third_shift)
    before = third_norm + inputs_wide
    block_out = (pixel_mask * jax.nn.silu(before)).astype(jnp.bfloat16)
    grad_before = cotangent.astype(jnp.float32) * pixel_mask * silu_slope(before)
    grad_expanded, third_gain_grad, third_shift_grad = denormalize(
        grad_before, third_saved, third_gain, pixel_mask
    )
    grad_expanded = grad_expanded.astype(jnp.bfloat16)
    expand_grad = jnp.einsum("rp,rc->pc", merged, grad_expanded, preferred_element_type=jnp.float32)
    grad_merged = jnp.einsum(
        "rc,pc->rp", grad_expanded, expand_weight, preferred_element_type=jnp.float32
    )
    grad_weighted = lax.psum_scatter(
        jnp.concatenate([grad_merged, grad_merged], 1).astype(jnp.bfloat16),
        "chan",
        scatter_dimension=1,
        tiled=True,
    ).astype(jnp.float32)
    grad_image = grad_weighted.reshape(images, cells, mine_two)
    grad_attention_mine = jnp.sum(grad_image * per_image, 1)
    grad_second = grad_image * attention_mine[:, None, :]
    grad_attention = lax.all_gather(grad_attention_mine, "chan", axis=1, tiled=True)
    paired = (
        attention[:, :width] * grad_attention[:, :width]
        + attention[:, width:] * grad_attention[:, width:]
    )
    grad_logits = attention * (grad_attention - jnp.concatenate([paired, paired], 1))
    bias_full = jnp.sum(grad_logits, 0)
    up_full = jnp.dot(squeezed.T, grad_logits, precision=highest)
    grad_squeezed = jnp.dot(grad_logits, gate_up.T, precision=highest)
    grad_gate, gate_gain_full, gate_shift_full = denormalize(
        grad_squeezed * silu_slope(gate_norm), gate_saved, gate_gain, image_ones
    )
    down_full = jnp.dot(summary.T, grad_gate, precision=highest)
    grad_summary = jnp.dot(grad_gate, gate_down.T, precision=highest)
    summary_mine = lax.dynamic_slice_in_dim(grad_summary, place * mine_two % width, mine_two, 1)
    grad_second = grad_second + (summary_mine / pixels[:, None])[:, None, :]
    grad_second = grad_second.reshape(rows, mine_two) * pixel_mask * silu_slope(second_norm)
    grad_splits, second_gain_grad, second_shift_grad = denormalize(
        grad_second, second_saved, second_gain, pixel_mask
    )
    grad_splits = grad_splits.astype(jnp.bfloat16)
    padded_grad = jnp.pad(
        grad_splits.reshape(images, SIDE, SIDE, mine_two), ((0, 0), (1, 1), (1, 1), (0, 0))
    )
    kernel_parts = []
    grad_group = jnp.zeros((rows, half), jnp.float32)
    for row_tap in range(3):
        for col_tap in range(3):
            shifted = padded_act[:, row_tap : row_tap + SIDE, col_tap : col_tap + SIDE, :].reshape(
                rows, half
            )
            kernel_parts.append(
                jnp.einsum("rh,ro->ho", shifted, grad_splits, preferred_element_type=jnp.float32)
            )
            moved = padded_grad[
                :, 2 - row_tap : 2 - row_tap + SIDE, 2 - col_tap : 2 - col_tap + SIDE, :
            ].reshape(rows, mine_two)
            grad_group = grad_group + jnp.einsum(
                "ro,ho->rh",
                moved,
                split_weight[row_tap * 3 + col_tap],
                preferred_element_type=jnp.float32,
            )
    split_local = jnp.stack(kernel_parts)
    grad_first = group_reduce(grad_group, place, levels)
    grad_first = grad_first * pixel_mask * silu_slope(first_norm)
    grad_reduced, first_gain_grad, first_shift_grad = denormalize(
        grad_first, first_saved, first_gain, pixel_mask
    )
    grad_reduced = grad_reduced.astype(jnp.bfloat16)
    grad_features = jnp.einsum(
        "rp,cp->rc", grad_reduced, reduce_cols, preferred_element_type=jnp.float32
    )
    grad_inputs = lax.psum_scatter(
        grad_features.astype(jnp.bfloat16), "chan", scatter_dimension=1, tiled=True
    ).astype(jnp.float32)
    reduce_local = jnp.einsum(
        "rc,rp->cp", features_all, grad_reduced, preferred_element_type=jnp.float32
    )
    inputs_grad = (grad_before + grad_inputs).astype(jnp.bfloat16)
    down_mine = lax.dynamic_slice_in_dim(down_full, place * mine_gate, mine_gate, 1)
    up_mine = lax.dynamic_slice_in_dim(up_full, place * mine_two, mine_two, 1)
    bias_mine = lax.dynamic_slice_in_dim(bias_full, place * mine_two, mine_two, 0)
    summed = lax.psum((reduce_local, split_local, expand_grad, down_mine, up_mine, bias_mine), "dp")
    gate_gain_grad = lax.dynamic_slice_in_dim(gate_gain_full, place * mine_gate, mine_gate, 0)
    gate_shift_grad = lax.dynamic_slice_in_dim(gate_shift_full, place * mine_gate, mine_gate, 0)
    return (
        block_out,
        inputs_grad,
        summed[0],
        first_gain_grad,
        first_shift_grad,
        summed[1],
        second_gain_grad,
        second_shift_grad,
        summed[3],
        gate_gain_grad,
        gate_shift_grad,
        summed[4],
        summed[5],
        summed[2],
        third_gain_grad,
        third_shift_grad,
    )


def solution(mesh):
    placed = (
        P("dp", "chan"),
        P("dp"),
        P(),
        P("chan"),
        P("chan"),
        P(None, None, "chan"),
        P("chan"),
        P("chan"),
        P(),
        P(),
        P(),
        P(),
        P(),
        P(None, "chan"),
        P("chan"),
        P("chan"),
        P("dp", "chan"),
    )
    return jax.shard_map(
        per_device,
        mesh=mesh,
        in_specs=placed,
        out_specs=(
            P("dp", "chan"),
            P("dp", "chan"),
            P(None, "chan"),
            P("chan"),
            P("chan"),
            P(None, None, "chan"),
            P("chan"),
            P("chan"),
            P(None, "chan"),
            P("chan"),
            P("chan"),
            P(None, "chan"),
            P("chan"),
            P(None, "chan"),
            P("chan"),
            P("chan"),
        ),
        check_vma=False,
    )
```

profile of v0, /device:TPU:0, one launch (start us, length us, event | category | flops | bytes accessed | tf_op | source)
XLA Modules:
  0.0 590.8 jit_solution(4975399800963955082)
XLA Ops:
  8.3 0.7 fusion.22
  9.0 62.7 %all-gather.3.cloned.1.call-done = bf16[4096,1024]{1,0:T(8,128)(2,1)} async-done(((bf16[4096,256]{1,0:T(8,128)(2,1)}), bf16[4096,1024]{1,0:T(8,128)(2,1)}) %all-gather.3.cloned.1.call-update) | async-done | bytes 8388624 | tf_op jit(solution)/shard_map/all_gather | solution.py:115
  71.7 6.1 %fusion.17 = (f32[64]{0:T(128)S(1)}, f32[64]{0:T(128)S(1)}, f32[4096,64]{0,1:T(8,128)S(1)}) fusion(f32[4096]{0:T(1024)S(1)} %reshape.226, bf16[4096,1024]{1,0:T(8,128)(2,1)} %all-gather.3.cloned.1.call-done, bf16[1024,256]{1,0:T(8,128)(2,1)S(1)} %copy-done, s32[]{:T(128)S(6)} %select_n.49), kind=kOutput, calls=%fused_computation.89 | convolution fusion | flops 537919360 | bytes 9716228 | tf_op jit(solution)/shard_map/dot_general | solution.py:117
  77.8 22.0 %all-reduce.9 = (f32[64]{0:T(128)S(1)}, f32[]{:T(128)}, f32[64]{0:T(128)S(1)}) all-reduce(f32[64]{0:T(128)S(1)} %get-tuple-element.25, f32[]{:T(128)} %fusion.22, f32[64]{0:T(128)S(1)} %get-tuple-element.24), channel_id=1, replica_groups=mesh['dp'=8,'chan'=4] {'dp'}, use_global_device_ids=true, to_apply=%region_1.0 | all-reduce | flops 129 | bytes 1032 | tf_op jit(solution)/shard_map/psum | solution.py:26
  99.8 1.2 fusion.82
  102.1 1.5 collective-permute-done
  103.6 2.4 copy.40
  105.9 2.8 maximum_select_fusion
  108.7 2.4 pad_slice_fusion.8
  113.9 1.9 fusion
  116.7 0.7 fusion.2
  117.4 17.1 %all-reduce.8 = (f32[128]{0:T(128)S(1)}, f32[128]{0:T(128)S(1)}) all-reduce(f32[128]{0:T(128)S(1)} %get-tuple-element.21, f32[128]{0:T(128)S(1)} %get-tuple-element.20), channel_id=1, replica_groups=mesh['dp'=8,'chan'=4] {'dp'}, use_global_device_ids=true, to_apply=%region_7.8 | all-reduce | flops 256 | bytes 2048 | tf_op jit(solution)/shard_map/psum | solution.py:26
  134.6 1.2 fusion.85
  135.8 1.8 bitcast_reduce_fusion
  137.7 5.2 all_gather.13
  143.1 20.3 %all-reduce.7 = (f32[128]{0:T(128)S(1)}, f32[]{:T(128)}, f32[128]{0:T(128)S(1)}) all-reduce(f32[128]{0:T(128)S(1)} %get-tuple-element.31, f32[]{:T(128)} %constant.29.clone.1, f32[128]{0:T(128)S(1)} %get-tuple-element.30), channel_id=1, replica_groups=mesh['dp'=8,'chan'=4] {'dp'}, use_global_device_ids=true, to_apply=%region_12.13 | all-reduce | flops 257 | bytes 2056 | tf_op jit(solution)/shard_map/psum | solution.py:26
  163.4 1.2 fusion.87
  164.6 1.2 convolution_add_fusion.15
  165.8 2.7 fusion.3
  168.8 31.3 %all-gather.5.cloned.1.call-done = bf16[4096,512]{1,0:T(8,128)(2,1)} async-done(((bf16[4096,128]{1,0:T(8,128)(2,1)}), bf16[4096,512]{1,0:T(8,128)(2,1)}) %all-gather.5.cloned.1.call-update) | async-done | bytes 4194320 | tf_op jit(solution)/shard_map/all_gather | solution.py:146
  200.0 5.4 fusion.1
  205.4 21.3 %all-reduce.6 = (f32[256]{0:T(256)S(1)}, f32[256]{0:T(256)S(1)}) all-reduce(f32[256]{0:T(256)S(1)} %get-tuple-element.17, f32[256]{0:T(256)S(1)} %get-tuple-element.16), channel_id=1, replica_groups=mesh['dp'=8,'chan'=4] {'dp'}, use_global_device_ids=true, to_apply=%region_17.18 | all-reduce | flops 512 | bytes 4096 | tf_op jit(solution)/shard_map/psum | solution.py:26
  227.4 7.0 %fusion.78 = (f32[256]{0:T(256)S(1)}, f32[256]{0:T(256)S(1)}, f32[4096,256]{1,0:T(8,128)}, bf16[4096,256]{1,0:T(8,128)(2,1)}) fusion(f32[256]{0:T(256)S(1)} %get-tuple-element.70, f32[4096,256]{1,0:T(8,128)} %get-tuple-element.99, f32[256]{0:T(256)S(1)} %get-tuple-element.71, bf16[4096,256]{1,0:T(8,128)(2,1)} %param.17, f32[256]{0:T(256)S(1)} %copy-done.56, ...), kind=kLoop, calls=%fused_computation.199 | loop fusion | flops 23068160 | bytes 14702592 | tf_op jit(solution)/shard_map/reduce_sum | solution.py:35
  234.4 17.1 %all-reduce.5 = (f32[256]{0:T(256)S(1)}, f32[256]{0:T(256)S(1)}) all-reduce(f32[256]{0:T(256)S(1)} %get-tuple-element.19, f32[256]{0:T(256)S(1)} %get-tuple-element.18), channel_id=1, replica_groups=mesh['dp'=8,'chan'=4] {'dp'}, use_global_device_ids=true, to_apply=%region_23.24 | all-reduce | flops 512 | bytes 4096 | tf_op jit(solution)/shard_map/psum | solution.py:37
  252.2 4.8 multiply_convert_fusion
  257.0 1.3 copy-done.4
  258.3 0.7 convolution_convert_fusion.1
  259.1 2.5 maximum_bitcast_fusion
  261.7 42.4 %reduce-scatter.7.cloned.1.call-done = bf16[128,4096]{1,0:T(8,128)(2,1)} async-done(((bf16[512,4096]{1,0:T(8,128)(2,1)}), bf16[128,4096]{1,0:T(8,128)(2,1)}) %reduce-scatter.7.cloned.1.call-update) | async-done | bytes 1048592
  304.0 2.3 copy.44
  306.3 2.1 fusion.7
  308.4 5.2 all_gather.15
  314.6 21.3 %all-reduce.4 = (f32[128]{0:T(128)S(1)}, f32[128]{0:T(128)S(1)}) all-reduce(f32[128]{0:T(128)S(1)} %get-tuple-element.29, f32[128]{0:T(128)S(1)} %get-tuple-element.28), channel_id=1, replica_groups=mesh['dp'=8,'chan'=4] {'dp'}, use_global_device_ids=true, to_apply=%region_29.30 | all-reduce | flops 256 | bytes 2048 | tf_op jit(solution)/shard_map/psum | solution.py:37
  337.2 1.8 fusion.77
  339.0 0.7 dynamic-slice_divide_fusion
  339.7 3.4 fusion.79
  343.2 17.3 %all-reduce.3 = (f32[128]{0:T(128)S(1)}, f32[128]{0:T(128)S(1)}) all-reduce(f32[128]{0:T(128)S(1)} %get-tuple-element.23, f32[128]{0:T(128)S(1)} %get-tuple-element.22), channel_id=1, replica_groups=mesh['dp'=8,'chan'=4] {'dp'}, use_global_device_ids=true, to_apply=%region_33.34 | all-reduce | flops 256 | bytes 2048 | tf_op jit(solution)/shard_map/psum | solution.py:37
  361.2 3.2 multiply_convert_fusion.2
  364.4 2.4 pad_slice_fusion
  371.0 1.3 copy-done.5
  372.3 0.9 select_convert_fusion
  373.2 0.8 dynamic_slice.31
  373.9 1.6 fusion.68
  375.6 3.6 fusion.80
  379.2 35.8 %all-reduce.2 = (f32[64]{0:T(128)S(1)}, f32[64]{0:T(128)S(1)}, f32[256,32]{0,1:T(8,128)}, f32[128]{0:T(128)}) all-reduce(f32[64]{0:T(128)S(1)} %get-tuple-element.27, f32[64]{0:T(128)S(1)} %get-tuple-element.26, f32[256,32]{0,1:T(8,128)S(1)} %constant_dynamic-slice_fusion.1, ...), channel_id=1, replica_groups=mesh['dp'=8,'chan'=4] {'dp'}, use_global_device_ids=true, to_apply=%region_37.38 | all-reduce | flops 8448 | bytes 67584 | tf_op jit(solution)/shard_map/psum | solution.py:37
  415.8 7.7 %convolution_convert_fusion = bf16[4096,1024]{1,0:T(8,128)(2,1)} fusion(bf16[1024,256]{1,0:T(8,128)(2,1)S(1)} %copy-done, s32[]{:T(128)S(6)} %select_n.49, f32[4096,64]{0,1:T(8,128)} %get-tuple-element.61, f32[4096,64]{0,1:T(8,128)S(1)} %copy-done.3, f32[]{:T(128)} %get-tuple-element.50, f32[64]{0:T(128)S(1)} %get-tuple-element.104, ...), kind=kOutput, calls=%fused_computation | convolution fusion | flops 543424512 | bytes 10766856 | tf_op jit(solution)/shard_map/rp,cp->rc/dot_general | solution.py:222
  423.8 5.1 fusion.18
  430.0 1.1 fusion.16
  431.1 1.1 fusion.15
  432.2 1.1 fusion.14
  433.4 1.1 fusion.13
  434.5 2.4 fusion.12
  436.9 1.1 fusion.11
  438.1 1.1 fusion.10
  439.3 1.1 fusion.9
  440.4 1.1 fusion.8
  441.5 7.2 %convolution_bitcast_fusion.1 = f32[1024,64]{0,1:T(8,128)} fusion(bf16[4096,1024]{1,0:T(8,128)(2,1)} %all-gather.3.cloned.1.call-done, f32[4096,64]{0,1:T(8,128)S(1)} %copy-done.22, f32[4096,64]{0,1:T(8,128)S(1)} %copy-done.3, f32[]{:T(128)} %get-tuple-element.50, f32[64]{0:T(128)S(1)} %get-tuple-element.104, f32[64]{0:T(128)S(1)} %broadcast_divide_fusion.7, ...), kind=kOutput, calls=%fused_computation.68 | convolution fusion | flops 539230208 | bytes 10765572 | tf_op jit(solution)/shard_map/rc,rp->cp/dot_general | solution.py:228
  449.9 41.7 %reduce-scatter.5.cloned.1.call-done = bf16[4096,256]{1,0:T(8,128)(2,1)} async-done(((bf16[4096,1024]{1,0:T(8,128)(2,1)}), bf16[4096,256]{1,0:T(8,128)(2,1)}) %reduce-scatter.5.cloned.1.call-update) | async-done | bytes 2097168 | tf_op jit(solution)/shard_map/reduce_scatter | solution.py:225
  491.6 4.7 add_convert_fusion
  496.3 81.2 %all-reduce.13.cloned.1.call-done = (f32[1024,64]{0,1:T(8,128)}, f32[9,128,128]{2,1,0:T(8,128)}, f32[128,128]{1,0:T(8,128)}, f32[256,256]{1,0:T(8,128)}) async-done(((f32[1024,64]{0,1:T(8,128)}, f32[9,128,128]{2,1,0:T(8,128)}, f32[128,128]{1,0:T(8,128)}, f32[256,256]{1,0:T(8,128)}), (f32[1024,64]{0,1:T(8,128)}, f32[9,128,128]{2,1,0:T(8,128)}, f32[128,128]{1,0:T(8,128)}, ...) | async-done | bytes 1179664 | tf_op jit(solution)/shard_map/psum | solution.py:235
  577.5 1.7 copy.57
  579.2 1.9 copy.58
  581.1 1.5 copy.59
  582.6 1.7 copy.60
  (180 shorter events, 17.9 us)
Async XLA Ops:
  7.2 64.5 %copy-start = (bf16[1024,256]{1,0:T(8,128)(2,1)S(1)}, bf16[1024,256]{1,0:T(8,128)(2,1)}, u32[]{:S(2)}) copy-start(bf16[1024,256]{1,0:T(8,128)(2,1)} %param.19) | copy-start | bytes 1572868
  7.2 64.5 %all-gather.3.cloned.1.call-start = ((), (), s32[]{:S(2)}) async-start(), calls=%async_computation.2 | async-start | bytes 10485760 | tf_op jit(solution)/shard_map/all_gather | solution.py:115
  7.9 192.1 %all-gather.5.cloned.1.call-start = ((), (), s32[]{:S(2)}) async-start(), calls=%async_computation.3 | async-start | bytes 5242880 | tf_op jit(solution)/shard_map/all_gather | solution.py:146
  8.0 129.6 %copy-start.53 = (f32[16]{0:T(128)}, f32[16]{0:T(128)S(1)}, u32[]{:S(2)}) copy-start(f32[16]{0:T(128)S(1)} %get-tuple-element.94) | copy-start | bytes 196
  9.0 90.8 %copy-start.43 = (f32[64]{0:T(128)S(1)}, f32[64]{0:T(128)}, u32[]{:S(2)}) copy-start(f32[64]{0:T(128)} %param.20) | copy-start | bytes 772
  9.0 92.0 %copy-start.48 = (f32[64]{0:T(128)S(1)}, f32[64]{0:T(128)}, u32[]{:S(2)}) copy-start(f32[64]{0:T(128)} %param.21) | copy-start | bytes 772
  77.8 28.1 %copy-start.2 = (f32[4096,64]{0,1:T(8,128)}, f32[4096,64]{0,1:T(8,128)S(1)}, u32[]{:S(2)}) copy-start(f32[4096,64]{0,1:T(8,128)S(1)} %get-tuple-element.96) | copy-start | bytes 3145732
  101.5 2.1 collective-permute-start
  108.7 2.5 copy-start.23
  111.1 1.4 copy-start.16
  111.2 1.8 copy-start.14
  111.2 2.2 copy-start.18
  111.2 2.3 copy-start.12
  111.2 4.6 copy-start.8
  111.2 5.1 copy-start.6
  111.2 5.5 copy-start.20
  116.7 17.9 %copy-start.45 = (f32[128]{0:T(128)S(1)}, f32[128]{0:T(128)}, u32[]{:S(2)}) copy-start(f32[128]{0:T(128)} %param.23) | copy-start | bytes 1540
  116.7 19.1 %copy-start.55 = (f32[128]{0:T(128)S(1)}, f32[128]{0:T(128)}, u32[]{:S(2)}) copy-start(f32[128]{0:T(128)} %param.24) | copy-start | bytes 1540
  117.4 222.3 %copy-start.1 = (f32[4096,128]{1,0:T(8,128)}, f32[4096,128]{1,0:T(8,128)S(1)}, u32[]{:S(2)}) copy-start(f32[4096,128]{1,0:T(8,128)S(1)} %get-tuple-element.97) | copy-start | bytes 6291460
  135.7 1.9 copy-start.36
  135.7 1.9 copy-start.38
  135.7 7.1 %copy-start.25 = (f32[256,128]{1,0:T(8,128)S(1)}, f32[256,128]{1,0:T(8,128)}, u32[]{:S(2)}) copy-start(f32[256,128]{1,0:T(8,128)} %param.25) | copy-start | bytes 393220
  135.7 27.6 %copy-start.33 = (f32[128]{0:T(128)S(1)}, f32[128]{0:T(128)}, u32[]{:S(2)}) copy-start(f32[128]{0:T(128)} %param.26) | copy-start | bytes 1540
  135.8 28.8 %copy-start.40 = (f32[128]{0:T(128)S(1)}, f32[128]{0:T(128)}, u32[]{:S(2)}) copy-start(f32[128]{0:T(128)} %param.27) | copy-start | bytes 1540
  135.8 28.8 %copy-start.47 = (f32[512]{0:T(512)S(1)}, f32[512]{0:T(512)}, u32[]{:S(2)}) copy-start(f32[512]{0:T(512)} %param.29) | copy-start | bytes 6148
  142.9 21.7 %copy-start.27 = (f32[16,512]{1,0:T(8,128)}, f32[16,512]{1,0:T(8,128)S(1)}, u32[]{:S(2)}) copy-start(f32[16,512]{1,0:T(8,128)S(1)} %all_gather.13) | copy-start | bytes 98308
  168.5 58.2 %copy-start.46 = (f32[256]{0:T(256)S(1)}, f32[256]{0:T(256)}, u32[]{:S(2)}) copy-start(f32[256]{0:T(256)} %param.31) | copy-start | bytes 3076
  168.5 58.9 %copy-start.56 = (f32[256]{0:T(256)S(1)}, f32[256]{0:T(256)}, u32[]{:S(2)}) copy-start(f32[256]{0:T(256)} %param.32) | copy-start | bytes 3076
  168.6 135.5 %reduce-scatter.7.cloned.1.call-start = ((), (), s32[]{:S(2)}) async-start(), calls=%async_computation.5 | async-start | bytes 5242880
  251.5 5.5 copy-start.57
  251.5 5.5 copy-start.58
  252.2 6.2 %copy-start.26 = (bf16[256,256]{1,0:T(8,128)(2,1)S(1)}, bf16[256,256]{1,0:T(8,128)(2,1)}, u32[]{:S(2)}) copy-start(bf16[256,256]{1,0:T(8,128)(2,1)} %param.30) | copy-start | bytes 393220
  257.0 1.3 copy-start.4
  261.6 230.0 %reduce-scatter.5.cloned.1.call-start = ((), (), s32[]{:S(2)}) async-start(), calls=%async_computation.4 | async-start | bytes 10485760 | tf_op jit(solution)/shard_map/reduce_scatter | solution.py:225
  306.3 7.9 %copy-start.24 = (f32[128,512]{1,0:T(8,128)S(1)}, f32[128,512]{1,0:T(8,128)}, u32[]{:S(2)}) copy-start(f32[128,512]{1,0:T(8,128)} %param.28) | copy-start | bytes 786436
  306.3 7.9 %copy-start.34 = (f32[128]{0:T(128)S(1)}, f32[128]{0:T(128)}, u32[]{:S(2)}) copy-start(f32[128]{0:T(128)} %param.26) | copy-start | bytes 1540
  306.3 7.9 %copy-start.41 = (f32[128]{0:T(128)S(1)}, f32[128]{0:T(128)}, u32[]{:S(2)}) copy-start(f32[128]{0:T(128)} %param.27) | copy-start | bytes 1540
  335.9 3.0 copy-start.63
  339.7 21.5 %copy-start.37 = (f32[128]{0:T(128)S(1)}, f32[128]{0:T(128)}, u32[]{:S(2)}) copy-start(f32[128]{0:T(128)} %copy-done.36) | copy-start | bytes 1540
  339.7 21.5 %copy-start.39 = (f32[128]{0:T(128)S(1)}, f32[128]{0:T(128)}, u32[]{:S(2)}) copy-start(f32[128]{0:T(128)} %copy-done.38) | copy-start | bytes 1540
  339.7 21.5 %copy-start.54 = (f32[128]{0:T(128)S(1)}, f32[128]{0:T(128)}, u32[]{:S(2)}) copy-start(f32[128]{0:T(128)} %get-tuple-element.62) | copy-start | bytes 1540
  360.5 3.9 copy-start.59
  360.5 3.9 copy-start.62
  370.5 3.4 copy-start.28
  370.5 5.1 copy-start.30
  370.5 5.1 copy-start.32
  372.3 3.4 copy-start.3
  373.1 2.4 collective-permute-start.1
  375.6 40.2 %copy-start.44 = (f32[64]{0:T(128)S(1)}, f32[64]{0:T(128)}, u32[]{:S(2)}) copy-start(f32[64]{0:T(128)} %get-tuple-element.56) | copy-start | bytes 772
  415.1 8.3 %copy-start.61 = (f32[64]{0:T(128)}, f32[64]{0:T(128)S(1)}, u32[]{:S(2)}) copy-start(f32[64]{0:T(128)S(1)} %get-tuple-element.105) | copy-start | bytes 772
  415.1 26.4 %copy-start.51 = (f32[64]{0:T(128)}, f32[64]{0:T(128)S(1)}, u32[]{:S(2)}) copy-start(f32[64]{0:T(128)S(1)} %get-tuple-element.104) | copy-start | bytes 772
  423.4 5.4 copy-start.35
  423.5 5.4 copy-start.42
  423.5 154.0 %all-reduce.13.cloned.1.call-start = ((), (), s32[]{:S(2)}) async-start(), calls=%async_computation.6 | async-start | bytes 2359296 | tf_op jit(solution)/shard_map/psum | solution.py:235
  423.8 6.2 %copy-start.19 = (bf16[16,16,16,128]{3,2,1,0:T(8,128)(2,1)S(1)}, bf16[16,16,16,128]{3,2,1,0:T(8,128)(2,1)}, u32[]{:S(2)}) copy-start(bf16[16,16,16,128]{3,2,1,0:T(8,128)(2,1)} %copy-done.18) | copy-start | bytes 3145732
  428.9 2.2 copy-start.17
  430.0 2.3 copy-start.15
  431.1 2.2 copy-start.13
  434.5 2.4 copy-start.11
  436.9 2.3 copy-start.7
  438.1 2.2 copy-start.21
  439.3 2.2 copy-start.22
  441.5 7.2 %copy-start.64 = (f32[128]{0:T(128)S(1)}, f32[128]{0:T(128)}, u32[]{:S(2)}) copy-start(f32[128]{0:T(128)} %copy-done.63) | copy-start | bytes 1540
  441.5 7.8 %copy-start.50 = (f32[128]{0:T(128)S(1)}, f32[128]{0:T(128)}, u32[]{:S(2)}) copy-start(f32[128]{0:T(128)} %copy-done.49) | copy-start | bytes 1540
  (8 other events, 6.8 us)
Sparse Core Ops, SparseCore 0:
  9.6 62.0 all-gather.2
  168.6 31.3 all-gather.4
  261.7 42.2 reduce-scatter.6
  423.6 68.0 reduce-scatter.4
  496.5 81.0 all-reduce.12
where the time goes:
time: 592 us; the launch traced here: 591 us
  waiting for transfers between devices  262 us (44%)
  blocking collectives  183 us (31%)
  matrix products  58.5 us (10%)
  other arithmetic  49 us (8%)
  local copies, waits for them, and re-layouts  23.6 us (4%)
  between operations  14.6 us (2%)
    psum x4, blocking collectives, denormalize(): total, cross = lax.psum((total, cross), 'dp')  91.6 us
    psum x1, waiting for transfers between devices, per_device(): lax.psum((reduce_local, split_local, expand_grad, down_mine, up_mine, bia...  81.2 us
    psum x4, blocking collectives, normalize(): count, first, second = lax.psum((count, first, second), 'dp')  80.8 us
    all_gather x1, waiting for transfers between devices, per_device(): features_all = lax.all_gather(inputs, 'chan', axis=1, tiled=True)  62.7 us
    unnamed x6, waiting for transfers between devices  43.1 us
    reduce_scatter x1, waiting for transfers between devices, per_device(): lax.psum_scatter(grad_features.astype(jnp.bfloat16), 'chan', scatter_dime...  41.7 us
    all_gather x1, waiting for transfers between devices, per_device(): weighted_all = lax.all_gather(weighted, 'chan', axis=1, tiled=True)  31.3 us
    reduce_sum x3, other arithmetic, denormalize(): total = jnp.sum(grads, 0)  14 us
  transfers between devices with their start and end apart: 7, of which 6 were waited for; matrix products, arithmetic and copies ran while one was open for 6% of the time, Pallas kernels for 0%

commit v1 on v0

v1 whole, which is shorter than its diff:
```python
import functools
import types

import jax
import jax.numpy as jnp
from jax import lax
from jax.experimental import pallas as pl
from jax.experimental.pallas import tpu as pltpu
from jax.sharding import PartitionSpec as P

SIDE = 16
CELLS = SIDE * SIDE
TALL = CELLS + 2 * SIDE
LANES = 128
EPS = 1e-05
HIGHEST = lax.Precision.HIGHEST
F32 = jnp.float32
BF16 = jnp.bfloat16
MESH = pl.DeviceIdType.MESH
STRIP = 32


def wide(mask, width):
    return mask if width == LANES else jnp.concatenate([mask] * (width // LANES), axis=1)


def fold(values):
    return jnp.sum(values.reshape(values.shape[0] // 8, 8, values.shape[1]), axis=0)


def total(values):
    return jnp.sum(values, axis=0, keepdims=True)


def sigmoid(values):
    return 0.5 * jnp.tanh(0.5 * values) + 0.5


def dot(left, right):
    return jnp.dot(left, right, preferred_element_type=F32)


def exact(left, right):
    return jnp.dot(left, right, precision=HIGHEST, preferred_element_type=F32)


def exact_nt(left, right):
    return lax.dot_general(
        left, right, (((1,), (1,)), ((), ())), precision=HIGHEST, preferred_element_type=F32
    )


def exact_tn(left, right):
    return lax.dot_general(
        left, right, (((0,), (0,)), ((), ())), precision=HIGHEST, preferred_element_type=F32
    )


def flip(values):
    return values.astype(F32).T.astype(values.dtype)


def put(ref, row, vector):
    for part in range(vector.shape[1] // LANES):
        ref[0, row + part : row + part + 1, :] = vector[:, part * LANES : (part + 1) * LANES]


def get(block, row, width):
    parts = [block[row + q : row + q + 1, :] for q in range(width // LANES)]
    return parts[0] if len(parts) == 1 else jnp.concatenate(parts, axis=1)


def kernel(c, names, *refs):
    r = types.SimpleNamespace(**dict(zip(names, refs)))
    DP, CH, X, D, ipd, images = c.DP, c.CH, c.X, c.D, c.ipd, c.images
    width, cw, inner, m1, m2, mg = c.width, c.cw, c.inner, c.m1, c.m2, c.mg
    half, two = width // 2, 2 * width
    own_rows = ipd * CELLS
    taps = 9 * half
    dp = lax.axis_index("dp")
    ch = lax.axis_index("chan")
    core = ch % 2
    chip = ch // 2
    mate = (dp, ch + 1 - 2 * core)
    f0 = ((0, 0), (0, 0))

    def remote(src, dst, send, recv, device):
        return pltpu.make_async_remote_copy(
            src_ref=src, dst_ref=dst, send_sem=send, recv_sem=recv, device_id=device, device_id_type=MESH
        )

    def drain(ref, sem):
        pltpu.make_async_copy(ref, ref, sem).wait()

    def loop(count, body):
        def step(i, carry):
            body(i)
            return carry

        lax.fori_loop(0, count, step, 0)

    def peer(t):
        return (dp, ((chip + t) % X) * 2 + core)

    def across(d):
        return ((dp + d) % DP, ch)

    def block_of(t, same):
        return ((chip + t) % X) * 2 + (core if same else 1 - core)

    def rows_of(b, i):
        return pl.ds(pl.multiple_of((b * ipd + i) * CELLS, CELLS), CELLS)

    def block_rows(b):
        return pl.ds(pl.multiple_of(b * own_rows, own_rows), own_rows)

    def image(i):
        return pl.ds(pl.multiple_of(i * CELLS, CELLS), CELLS)

    def strips(base, body, carry, size=STRIP):
        def step(k, state):
            return body(pl.ds(pl.multiple_of(base + k * size, size), size), k, state)

        return lax.fori_loop(0, CELLS // size, step, carry)

    def everyone(buf, k, message=None):
        message = buf.at[0] if message is None else message

        def one(j, carry):
            d, q = j // CH, j % CH
            slot = ((DP - d) % DP) * CH + (CH - q) % CH
            remote(buf.at[0], buf.at[slot], r.all_send.at[k], r.all_recv.at[k], ((dp + d) % DP, (ch + q) % CH)).start()
            return carry

        lax.fori_loop(1, D, one, 0)

    def everyone_wait(buf, k):
        drain(buf.at[pl.ds(1, D - 1)], r.all_recv.at[k])

    def everyone_done(buf, k):
        drain(buf.at[pl.ds(1, D - 1)], r.all_send.at[k])

    def column(buf, k):
        for d in range(1, DP):
            remote(buf.at[0], buf.at[DP - d], r.col_send.at[k], r.col_recv.at[k], across(d)).start()

    def column_wait(buf, k):
        drain(buf.at[pl.ds(1, DP - 1)], r.col_recv.at[k])

    def column_done(buf, k):
        drain(buf.at[pl.ds(1, DP - 1)], r.col_send.at[k])

    class Scatter:
        def __init__(self, k, stage, inward, outward, landed, keep):
            self.k, self.stage, self.inward = k, stage, inward
            self.outward, self.landed, self.keep = outward, landed, keep

        def compute_mate(self, t, part):
            def body(i):
                self.stage[t, i] = part(block_of(t, False), i).astype(BF16)

            loop(ipd, body)

        def send_mate(self, t):
            def body(i):
                remote(
                    self.stage.at[t, i], self.inward.at[t, i],
                    r.rs_core_send.at[self.k], r.rs_core_recv.at[self.k, t, i], mate,
                ).start()

            loop(ipd, body)

        def to_mate(self, t, part):
            def body(i):
                self.stage[t, i] = part(block_of(t, False), i).astype(BF16)
                remote(
                    self.stage.at[t, i], self.inward.at[t, i],
                    r.rs_core_send.at[self.k], r.rs_core_recv.at[self.k, t, i], mate,
                ).start()

            loop(ipd, body)

        def to_peer(self, t, part):
            def body(i):
                value = part(block_of(t, True), i)
                drain(self.inward.at[t, i], r.rs_core_recv.at[self.k, t, i])
                self.outward[t - 1, i] = (value + self.inward[t, i].astype(F32)).astype(BF16)
                remote(
                    self.outward.at[t - 1, i], self.landed.at[X - t - 1, i],
                    r.rs_chip_send.at[self.k], r.rs_chip_recv.at[self.k, X - t, i], peer(t),
                ).start()

            loop(ipd, body)

        def own(self, part):
            def body(i):
                value = part(ch, i)
                drain(self.inward.at[0, i], r.rs_core_recv.at[self.k, 0, i])
                self.keep[image(i), :] = value + self.inward[0, i].astype(F32)

            loop(ipd, body)

        def arrive(self, i):
            for t in range(1, X):
                drain(self.landed.at[t - 1, i], r.rs_chip_recv.at[self.k, t, i])

        def extra(self, i, at, lanes):
            value = self.landed[0, i, at, lanes].astype(F32)
            for t in range(2, X):
                value = value + self.landed[t - 1, i, at, lanes].astype(F32)
            return value

        def done(self):
            drain(self.stage, r.rs_core_send.at[self.k])
            drain(self.outward, r.rs_chip_send.at[self.k])

    class Gather:
        def __init__(self, k, place, whole, pieces):
            self.k, self.place, self.whole, self.pieces = k, place, whole, pieces

        def send(self, i):
            src = self.place(ch, i)
            remote(src, src, r.ag_core_send.at[self.k], r.ag_core_recv.at[self.k, i], mate).start()
            for t in range(1, X):
                remote(src, src, r.ag_chip_send.at[self.k, t], r.ag_chip_recv.at[self.k, X - t, i], peer(t)).start()

        def from_mate(self, i):
            drain(self.place(block_of(0, False), i), r.ag_core_recv.at[self.k, i])

        def from_peer(self, t, i):
            ref = self.place(block_of(t, True), i)
            drain(ref, r.ag_chip_recv.at[self.k, t, i])
            remote(ref, ref, r.ag_pass_send.at[self.k, t], r.ag_pass_recv.at[self.k, t, i], mate).start()

        def from_pass(self, t, i):
            drain(self.place(block_of(t, False), i), r.ag_pass_recv.at[self.k, t, i])

        def done(self):
            drain(self.whole(ch), r.ag_core_send.at[self.k])
            for t in range(1, X):
                drain(self.whole(ch), r.ag_chip_send.at[self.k, t])
                drain(self.whole(block_of(t, True)), r.ag_pass_send.at[self.k, t])

    barrier = pltpu.get_barrier_semaphore()

    def greet(j, carry):
        pl.semaphore_signal(
            barrier, inc=1, device_id=((dp + j // CH) % DP, (ch + j % CH) % CH), device_id_type=MESH
        )
        return carry

    lax.fori_loop(1, D, greet, 0)

    load_w = pltpu.make_async_copy(
        r.reduce_weight.at[pl.ds(pl.multiple_of(ch * cw, cw), cw)], r.wr, r.load.at[0]
    )
    load_w.start()
    order = []
    for t in list(range(1, X)) + [0]:
        order += [block_of(t, False), block_of(t, True)]
    loads = []
    for k, b in enumerate(order):
        at = pl.ds(pl.multiple_of(b * own_rows, own_rows), own_rows)
        loads.append(pltpu.make_async_copy(r.inputs.at[at], r.xv.at[at], r.load.at[2 + k]))
        loads[-1].start()
    load_c = pltpu.make_async_copy(r.cotangent, r.cv, r.load.at[1])
    load_c.start()

    row_at = lax.broadcasted_iota(jnp.int32, (CELLS, LANES), 0)
    spot_r = lax.shift_right_logical(row_at, 4)
    spot_c = lax.bitwise_and(row_at, 15)

    def make_mask(j):
        side = 12 + 2 * r.resolution[j]
        mask = jnp.where(jnp.logical_and(spot_r < side, spot_c < side), 1.0, 0.0)
        r.area[pl.ds(j, 1), :] = jnp.full((1, LANES), side * side, jnp.int32).astype(F32)
        r.maskf[image(j), :] = mask
        r.maskb[image(j), :] = mask.astype(BF16)

    loop(images, make_mask)

    def selector(parts, mine):
        row = lax.broadcasted_iota(jnp.int32, (mine, mine * parts), 0)
        col = lax.broadcasted_iota(jnp.int32, (mine, mine * parts), 1)
        return jnp.where(col == row + ch * mine, 1.0, 0.0)

    pick1 = selector(CH, m1)
    pick2 = selector(CH, m2)
    pickg = selector(CH, mg)
    r.pbuf[0, 0:1, 0:width] = exact(r.first_gain[...], pick1)
    r.pbuf[0, 1:2, 0:width] = exact(r.first_shift[...], pick1)
    r.pbuf[0, 2:3, :] = exact(r.second_gain[...], pick2)
    r.pbuf[0, 3:4, :] = exact(r.second_shift[...], pick2)

    def part_reduce(b, i):
        at = rows_of(b, i)
        x = r.xv[at, :] * wide(r.maskb[at, :], cw)
        r.xv[at, :] = x
        return dot(x, r.wr[...])

    load_w.wait()
    rs1 = Scatter(0, r.stage, r.inward, r.outward, r.landed, r.red)
    loads[0].wait()
    rs1.compute_mate(1, part_reduce)
    pl.semaphore_wait(barrier, D - 1)
    rs1.send_mate(1)
    for t in range(1, X):
        if t > 1:
            loads[2 * t - 2].wait()
            rs1.to_mate(t, part_reduce)
        loads[2 * t - 1].wait()
        rs1.to_peer(t, part_reduce)
    loads[2 * X - 2].wait()
    rs1.to_mate(0, part_reduce)
    loads[2 * X - 1].wait()
    rs1.own(part_reduce)

    for q in range(1, CH):
        remote(r.pbuf.at[0], r.pbuf.at[CH - q], r.par_send.at[0], r.par_recv.at[CH - q], (dp, (ch + q) % CH)).start()
    r.wg[ch] = r.split_weight[...]
    gw = Gather(3, lambda b, i: r.wg.at[b], lambda b: r.wg.at[b], 1)
    gw.send(0)

    r.wrt[...] = flip(r.wr[...])
    r.wet[...] = flip(r.expand_weight[...])

    def turn_x(j):
        r.xt[j] = flip(r.xv[image(j), :])

    loop(images, turn_x)
    for g in range(2):
        for i in range(ipd):
            r.act[g, i, 0:SIDE, :] = jnp.zeros((SIDE, 3 * half), BF16)
            r.act[g, i, CELLS + SIDE : TALL, :] = jnp.zeros((SIDE, 3 * half), BF16)
            r.dsh[g, i, 0:SIDE, :] = jnp.zeros((SIDE, 3 * width), BF16)
            r.dsh[g, i, CELLS + SIDE : TALL, :] = jnp.zeros((SIDE, 3 * width), BF16)

    def finish_reduce(i, state):
        rs1.arrive(i)

        def body(at, k, state):
            first, second = state
            value = r.red[at, :] + rs1.extra(i, pl.ds(pl.multiple_of(k * STRIP, STRIP), STRIP), slice(None))
            r.red[at, :] = value
            return (first + fold(value), second + fold(value * value))

        return strips(i * CELLS, body, state)

    zero8 = jnp.zeros((8, width), F32)
    first, second = lax.fori_loop(0, ipd, finish_reduce, (zero8, zero8))

    pixels = lax.fori_loop(
        0, ipd, lambda i, count: count + r.area[pl.ds(ch * ipd + i, 1), :], jnp.zeros((1, LANES), F32)
    )
    r.g1[0] = jnp.zeros((8, LANES), F32)
    put(r.g1, 0, total(first))
    put(r.g1, width // LANES, total(second))
    r.g1[0, 6:7, :] = pixels
    everyone(r.g1, 0)

    everyone_wait(r.g1, 0)
    sums = jnp.sum(r.g1[...], axis=0)
    count = sums[6:7, 0:1]
    inverse = 1.0 / count
    params = r.pbuf[0]
    for q in range(1, CH):
        drain(r.pbuf.at[q], r.par_recv.at[q])
        params = params + r.pbuf[q]
    gain1, shift1 = params[0:1, 0:width], params[1:2, 0:width]
    gain2, shift2 = params[2:3, :], params[3:4, :]
    for t in range(1, X):
        gw.from_peer(t, 0)

    def moments(first, second):
        mean = first * inverse
        return mean, lax.rsqrt(second * inverse - mean * mean + EPS)

    mean1, scale1 = moments(get(sums, 0, width), get(sums, width // LANES, width))

    place_x = lambda b, i: r.xh1.at[rows_of(b, i)]
    gx = Gather(0, place_x, lambda b: r.xh1.at[block_rows(b)], ipd)

    strip_c = lax.bitwise_and(lax.broadcasted_iota(jnp.int32, (STRIP, LANES), 0), 15)
    not_first = strip_c != 0
    not_last = strip_c != 15

    def first_act(i):
        def body(at, k, carry):
            there = pl.ds(pl.multiple_of((ch * ipd + i) * CELLS + k * STRIP, STRIP), STRIP)
            put_at = pl.ds(pl.multiple_of(SIDE + k * STRIP, SIDE), STRIP)
            mask = r.maskf[there, :]
            for g in range(2):
                lanes = slice(g * half, (g + 1) * half)
                xh = (r.red[at, lanes] - mean1[:, lanes]) * scale1[:, lanes]
                h = gain1[:, lanes] * xh + shift1[:, lanes]
                s = sigmoid(h)
                y = h * s
                r.red[at, lanes] = xh
                r.xh1[there, lanes] = xh.astype(BF16)
                r.slope1[at, lanes] = mask * (s + y - y * s)
                a = mask * y
                before = jnp.where(not_first, pltpu.roll(a, 1, 0), 0.0)
                after = jnp.where(not_last, pltpu.roll(a, STRIP - 1, 0), 0.0)
                r.act[g, i, put_at, 0:half] = before.astype(BF16)
                r.act[g, i, put_at, half : 2 * half] = a.astype(BF16)
                r.act[g, i, put_at, 2 * half : 3 * half] = after.astype(BF16)
            return carry

        strips(i * CELLS, body, 0)
        gx.send(i)

    loop(ipd, first_act)

    gw.from_mate(0)
    for t in range(1, X):
        gw.from_pass(t, 0)
    for g in range(2):
        for q in range(CH // 2):
            r.wf[g, :, q * m2 : (q + 1) * m2] = r.wg[g * (CH // 2) + q]

    def conv(i, state):
        there = rows_of(ch, i)
        out = []
        for g in range(2):
            lanes = slice(g * width, (g + 1) * width)
            left = jnp.concatenate(
                [r.act[g, i, k * SIDE : k * SIDE + CELLS, :] for k in range(3)], axis=1
            )
            value = dot(left, r.wf[g]) * wide(r.maskf[there, :], width)
            r.sp[image(i), lanes] = value
            out.append((state[g][0] + fold(value), state[g][1] + fold(value * value)))
        return tuple(out)

    state = lax.fori_loop(0, ipd, conv, ((zero8, zero8), (zero8, zero8)))
    for g in range(2):
        put(r.g2, g * (width // LANES), total(state[g][0]))
        put(r.g2, (2 + g) * (width // LANES), total(state[g][1]))
    everyone(r.g2, 1)

    for g in range(2):
        for tap in range(9):
            r.wt[g, tap * width : (tap + 1) * width, :] = flip(r.wf[g, tap * half : (tap + 1) * half, :])

    everyone_wait(r.g2, 1)
    sums = jnp.sum(r.g2[...], axis=0)
    mean2, scale2 = moments(get(sums, 0, two), get(sums, two // LANES, two))

    r.g3[0] = jnp.zeros((8, LANES), F32)

    def second_act(i):
        def body(at, k, state):
            there = pl.ds(pl.multiple_of((ch * ipd + i) * CELLS + k * STRIP, STRIP), STRIP)
            mask = r.maskf[there, :]
            new = []
            for q in range(two // LANES):
                lanes = slice(q * LANES, (q + 1) * LANES)
                xh = (r.sp[at, lanes] - mean2[:, lanes]) * scale2[:, lanes]
                h = gain2[:, lanes] * xh + shift2[:, lanes]
                s = sigmoid(h)
                y = h * s
                r.sp[at, lanes] = xh
                r.slope2[at, lanes] = mask * (s + y - y * s)
                a = mask * y
                r.act2[at, lanes] = a
                new.append(state[q] + fold(a))
            return tuple(new)

        zero = jnp.zeros((8, LANES), F32)
        pooled = strips(i * CELLS, body, (zero,) * (two // LANES))
        share = 1.0 / r.area[pl.ds(ch * ipd + i, 1), :]
        r.share[pl.ds(i, 1), :] = share
        n = width // LANES
        for q in range(n):
            r.g3[0, pl.ds(4 * q + i, 1), :] = total(pooled[q] + pooled[n + q]) * share

    loop(ipd, second_act)
    everyone(r.g3, 2)

    gate_rows = min(D * 8, 2 * LANES)
    gate_blocks = D * 8 // gate_rows
    gate_at = lax.broadcasted_iota(jnp.int32, (gate_rows, LANES), 0)
    valid = lax.bitwise_and(gate_at, 7) < ipd
    every = 1.0 / (D * ipd)

    def gate_block(n):
        return pl.ds(pl.multiple_of(n * gate_rows, gate_rows), gate_rows)

    def lower_upper(buf, n):
        slots = gate_rows // 8
        both = buf[pl.ds(n * slots, slots)].reshape(gate_rows, LANES)
        return jnp.where(valid, both, 0.0), jnp.where(valid, pltpu.roll(both, gate_rows - 4, 0), 0.0)

    def gate_in(n, state):
        sum_lo, sum_hi = lower_upper(r.g3, n)
        pre = exact(sum_lo, r.gate_down[0:LANES, :]) + exact(sum_hi, r.gate_down[LANES:, :])
        r.gate_x[gate_block(n), :] = pre
        return state[0] + total(pre), state[1] + total(pre * pre)

    everyone_wait(r.g3, 2)
    zero1 = jnp.zeros((1, LANES), F32)
    first, second = lax.fori_loop(0, gate_blocks, gate_in, (zero1, zero1))
    gate_mean = first * every
    gate_scale = lax.rsqrt(second * every - gate_mean * gate_mean + EPS)

    def gate_out(n):
        at = gate_block(n)
        x = (r.gate_x[at, :] - gate_mean) * gate_scale
        h = r.gate_gain[...] * x + r.gate_shift[...]
        s = sigmoid(h)
        y = h * s
        r.gate_x[at, :] = x
        r.squeezed[at, :] = y
        r.gate_slope[at, :] = s + y - y * s

    loop(gate_blocks, gate_out)
    logits = exact(r.squeezed[0:8, :], r.gate_up[...]) + r.gate_bias[...]
    top = jnp.maximum(logits[:, :width], logits[:, width:])
    upper = jnp.exp(logits[:, :width] - top)
    lower = jnp.exp(logits[:, width:] - top)
    both = upper + lower
    r.att[:, 0:width] = upper / both
    r.att[:, width:two] = lower / both

    gm = Gather(1, lambda b, i: r.merged.at[rows_of(b, i)], lambda b: r.merged.at[block_rows(b)], ipd)

    def merge(i):
        att = r.att[pl.ds(i, 1), :]

        def body(at, k, carry):
            there = pl.ds(pl.multiple_of((ch * ipd + i) * CELLS + k * STRIP, STRIP), STRIP)
            left = (r.act2[at, 0:width] * att[:, 0:width]).astype(BF16)
            right = (r.act2[at, width:two] * att[:, width:two]).astype(BF16)
            r.merged[there, :] = (left.astype(F32) + right.astype(F32)).astype(BF16)
            return carry

        strips(i * CELLS, body, 0)
        gm.send(i)

    loop(ipd, merge)

    r.acc[...] = jnp.zeros((16, cw), F32)

    def expand(b, i):
        at = rows_of(b, i)
        value = dot(r.merged[at, :], r.expand_weight[...])
        r.ex[at, :] = value
        r.acc[0:8, :] += fold(value)
        r.acc[8:16, :] += fold(value * value)

    loop(ipd, lambda i: expand(ch, i))

    def expand_mate(i):
        gm.from_mate(i)
        expand(block_of(0, False), i)

    loop(ipd, expand_mate)
    for t in range(1, X):

        def expand_peer(i):
            gm.from_peer(t, i)
            expand(block_of(t, True), i)

        loop(ipd, expand_peer)
    for t in range(1, X):

        def expand_pass(i):
            gm.from_pass(t, i)
            expand(block_of(t, False), i)

        loop(ipd, expand_pass)
    put(r.c1, 0, total(r.acc[0:8, :]))
    put(r.c1, cw // LANES, total(r.acc[8:16, :]))
    column(r.c1, 0)
    load_c.wait()

    def turn_m(j):
        r.mt[j] = flip(r.merged[image(j), :])

    loop(images, turn_m)
    column_wait(r.c1, 0)
    sums = jnp.sum(r.c1[...], axis=0)
    mean3, scale3 = moments(get(sums, 0, cw), get(sums, cw // LANES, cw))
    gain3, shift3 = r.third_gain[...], r.third_shift[...]

    def outputs(j, state):
        def body(at, k, state):
            shift, cross = state
            mask = wide(r.maskf[at, :], cw)
            xh = (r.ex[at, :] - mean3) * scale3
            h = gain3 * xh + shift3 + r.xv[at, :].astype(F32)
            s = sigmoid(h)
            y = h * s
            d = r.cv[at, :].astype(F32) * mask * (s + y - y * s)
            r.cv[at, :] = (mask * y).astype(BF16)
            r.dpre[at, :] = d
            r.ex[at, :] = xh
            return (shift + fold(d), cross + fold(d * xh))

        state = strips(j * CELLS, body, state)
        pltpu.make_async_copy(r.cv.at[image(j)], r.block_out.at[image(j)], r.store.at[0]).start()
        return state

    zero_c = jnp.zeros((8, cw), F32)
    shift, cross = lax.fori_loop(0, images, outputs, (zero_c, zero_c))
    put(r.c2, 0, total(shift))
    put(r.c2, cw // LANES, total(cross))
    column(r.c2, 1)
    column_wait(r.c2, 1)
    sums = jnp.sum(r.c2[...], axis=0)
    shift_grad, gain_grad = get(sums, 0, cw), get(sums, cw // LANES, cw)
    r.third_gain_grad[...] = gain_grad
    r.third_shift_grad[...] = shift_grad
    lead3, base3, slant3 = gain3 * scale3, shift_grad * inverse, gain_grad * inverse

    def part_merged(b, i):
        def body(at, k, carry):
            mask = wide(r.maskf[at, :], cw)
            d = mask * lead3 * (r.dpre[at, :] - base3 - r.ex[at, :] * slant3)
            r.de[at, :] = d.astype(BF16)
            return carry

        strips((b * ipd + i) * CELLS, body, 0)
        return dot(r.de[rows_of(b, i), :], r.wet[...])

    rs1.done()
    rs2 = Scatter(1, r.stage, r.inward2, r.outward, r.landed2, r.dm)
    for t in range(1, X):
        rs2.to_mate(t, part_merged)
        rs2.to_peer(t, part_merged)
    rs2.to_mate(0, part_merged)
    rs2.own(part_merged)

    def grow(j):
        r.eg[...] += dot(r.mt[j], r.de[image(j), :])

    r.eg[...] = dot(r.mt[0], r.de[image(0), :])
    lax.fori_loop(1, images, lambda j, carry: (grow(j), carry)[1], 0)
    piece = width // DP
    et = r.es.dtype
    r.es[...] = r.eg[...].astype(et)

    def piece_rows(d):
        return pl.ds(pl.multiple_of(((dp + d) % DP) * piece, piece), piece)

    for d in range(1, DP):
        remote(r.es.at[piece_rows(d)], r.ebuf.at[DP - d], r.eg_send.at[0], r.eg_recv.at[0], across(d)).start()

    r.g4[0] = jnp.zeros((8, LANES), F32)

    def finish_merged(i):
        rs2.arrive(i)

        def body(at, k, state):
            here = pl.ds(pl.multiple_of(k * STRIP, STRIP), STRIP)
            value = r.dm[at, :] + rs2.extra(i, here, slice(None))
            r.dm[at, :] = value
            return state + fold(value * (r.act2[at, 0:width] - r.act2[at, width:two]))

        gap = total(strips(i * CELLS, body, zero8))
        att = r.att[pl.ds(i, 1), :]
        grad = att[:, 0:width] * att[:, width:two] * gap
        for q in range(width // LANES):
            r.g4[0, pl.ds(4 * q + i, 1), :] = grad[:, q * LANES : (q + 1) * LANES]

    loop(ipd, finish_merged)
    everyone(r.g4, 3)

    drain(r.ebuf.at[pl.ds(1, DP - 1)], r.eg_recv.at[0])
    value = r.eg[piece_rows(0), :]
    for d in range(1, DP):
        value = value + r.ebuf[d].astype(F32)
    r.eo[0] = value.astype(et)
    for d in range(1, DP):
        remote(r.eo.at[0], r.eo.at[DP - d], r.eg_send.at[1], r.eg_recv.at[1], across(d)).start()

    everyone_wait(r.g4, 3)
    up_gap = r.gate_up[:, 0:width] - r.gate_up[:, width:two]

    def gate_back(n, state):
        at = gate_block(n)
        grad_lo, grad_hi = lower_upper(r.g4, n)
        grad = exact_nt(grad_lo, up_gap[:, 0:LANES]) + exact_nt(grad_hi, up_gap[:, LANES:width])
        grad = grad * r.gate_slope[at, :]
        r.grad_down[at, :] = grad
        return state[0] + total(grad), state[1] + total(grad * r.gate_x[at, :])

    gate_shift_all, gate_gain_all = lax.fori_loop(0, gate_blocks, gate_back, (zero1, zero1))
    lead = r.gate_gain[...] * gate_scale

    def gate_norm_back(n):
        at = gate_block(n)
        grad = r.grad_down[at, :] - gate_shift_all * every - r.gate_x[at, :] * (gate_gain_all * every)
        r.grad_down[at, :] = jnp.where(valid, lead * grad, 0.0)

    loop(gate_blocks, gate_norm_back)
    r.grad_summary[...] = exact_nt(r.grad_down[0:8, :], r.gate_down[...])

    def second_back(i, state):
        att = r.att[pl.ds(i, 1), :]
        flat = r.grad_summary[pl.ds(i, 1), :] * wide(r.share[pl.ds(i, 1), :], width)

        def body(at, k, state):
            d = r.dm[at, :]
            new = []
            for g in range(2):
                lanes = slice(g * width, (g + 1) * width)
                value = (d * att[:, lanes] + flat) * r.slope2[at, lanes]
                r.act2[at, lanes] = value
                new.append((state[g][0] + fold(value), state[g][1] + fold(value * r.sp[at, lanes])))
            return tuple(new)

        return strips(i * CELLS, body, state, 16)

    state = lax.fori_loop(0, ipd, second_back, ((zero8, zero8), (zero8, zero8)))
    for g in range(2):
        put(r.g5, g * (width // LANES), total(state[g][0]))
        put(r.g5, (2 + g) * (width // LANES), total(state[g][1]))
    everyone(r.g5, 4)

    r.gate_gain_grad[...] = exact_nt(gate_gain_all, pickg)
    r.gate_shift_grad[...] = exact_nt(gate_shift_all, pickg)

    def gate_grads(n, state):
        at = gate_block(n)
        sum_lo, sum_hi = lower_upper(r.g3, n)
        grad_lo, grad_hi = lower_upper(r.g4, n)
        picked = exact_nt(r.grad_down[at, :], pickg)
        down = jnp.concatenate([exact_tn(sum_lo, picked), exact_tn(sum_hi, picked)], axis=0)
        squeezed = r.squeezed[at, :]
        up = jnp.concatenate([exact_tn(squeezed, grad_lo), exact_tn(squeezed, grad_hi)], axis=1)
        bias = jnp.concatenate([total(grad_lo), total(grad_hi)], axis=1)
        return state[0] + down, state[1] + up, state[2] + bias

    down, up, bias = lax.fori_loop(
        0, gate_blocks, gate_grads,
        (jnp.zeros((width, mg), F32), jnp.zeros((inner, width), F32), jnp.zeros((1, width), F32)),
    )
    r.down_grad[...] = down
    r.up_grad[...] = exact_nt(jnp.concatenate([up, -up], axis=1), pick2)
    r.bias_grad[...] = exact_nt(jnp.concatenate([bias, -bias], axis=1), pick2)

    everyone_wait(r.g5, 4)
    sums = jnp.sum(r.g5[...], axis=0)
    shift_grad, gain_grad = get(sums, 0, two), get(sums, two // LANES, two)
    r.second_gain_grad[...] = exact_nt(gain_grad, pick2)
    r.second_shift_grad[...] = exact_nt(shift_grad, pick2)
    lead2, base2, slant2 = gain2 * scale2, shift_grad * inverse, gain_grad * inverse

    def splits_back(i):
        def body(at, k, carry):
            there = pl.ds(pl.multiple_of((ch * ipd + i) * CELLS + k * STRIP, STRIP), STRIP)
            put_at = pl.ds(pl.multiple_of(SIDE + k * STRIP, SIDE), STRIP)
            mask = r.maskf[there, :]
            for q in range(two // LANES):
                g, p = q // (width // LANES), q % (width // LANES)
                lanes = slice(q * LANES, (q + 1) * LANES)
                d = mask * lead2[:, lanes] * (
                    r.act2[at, lanes] - base2[:, lanes] - r.sp[at, lanes] * slant2[:, lanes]
                )
                r.act2[at, lanes] = d
                before = jnp.where(not_first, pltpu.roll(d, 1, 0), 0.0)
                after = jnp.where(not_last, pltpu.roll(d, STRIP - 1, 0), 0.0)
                for n, value in enumerate((after, d, before)):
                    start = n * width + p * LANES
                    r.dsh[g, i, put_at, start : start + LANES] = value.astype(BF16)
            return carry

        strips(i * CELLS, body, 0)

    loop(ipd, splits_back)

    def first_back(i, state):
        out = []
        for g in range(2):
            lanes = slice(g * half, (g + 1) * half)
            left = jnp.concatenate(
                [r.dsh[g, i, (2 - k) * SIDE : (2 - k) * SIDE + CELLS, :] for k in range(3)], axis=1
            )
            value = dot(left, r.wt[g]) * r.slope1[image(i), lanes]
            r.dh1[rows_of(ch, i), lanes] = value.astype(BF16)
            out.append((state[g][0] + fold(value), state[g][1] + fold(value * r.red[image(i), lanes])))
        return tuple(out)

    zero_h = jnp.zeros((8, half), F32)
    state = lax.fori_loop(0, ipd, first_back, ((zero_h, zero_h), (zero_h, zero_h)))
    r.g6[0] = jnp.zeros((8, LANES), F32)
    for g in range(2):
        r.g6[0, g : g + 1, :] = total(state[g][0])
        r.g6[0, 2 + g : 3 + g, :] = total(state[g][1])
    everyone(r.g6, 5)
    gd = Gather(2, lambda b, i: r.dh1.at[rows_of(b, i)], lambda b: r.dh1.at[block_rows(b)], ipd)
    loop(ipd, gd.send)

    def pass_x(i):
        for t in range(1, X):
            gx.from_peer(t, i)

    loop(ipd, pass_x)

    def turn_d(i):
        for g in range(2):
            r.dst[g, :, image(i)] = r.act2[image(i), g * width : (g + 1) * width].T.astype(BF16)

    loop(ipd, turn_d)
    per = CH // 2
    for g in range(2):
        for k in range(3):
            lanes = slice(3 * k * half, 3 * (k + 1) * half)
            right = r.act[g, :, k * SIDE : k * SIDE + CELLS, :].reshape(own_rows, 3 * half)
            value = dot(r.dst[g], right)
            if c.split_inside:
                for q in range(per):
                    b = g * per + q
                    r.ss[b // 2, b % 2, :, lanes] = value[q * m2 : (q + 1) * m2, :].astype(BF16)
            else:
                r.split_part[g * width : (g + 1) * width, lanes] = value
    if c.split_inside:
        remote(r.ss.at[:, 1 - core], r.sin, r.sg_send.at[0], r.sg_recv.at[0], mate).start()

    everyone_wait(r.g6, 5)
    sums = jnp.sum(r.g6[...], axis=0)
    shift_grad, gain_grad = get(sums, 0, width), get(sums, 2, width)
    r.first_gain_grad[...] = exact_nt(gain_grad, pick1)
    r.first_shift_grad[...] = exact_nt(shift_grad, pick1)
    lead1, base1, slant1 = gain1 * scale1, shift_grad * inverse, gain_grad * inverse

    if c.split_inside:
        drain(r.sin, r.sg_recv.at[0])
        slab = m2 // DP

        def slab_rows(d):
            return pl.ds(pl.multiple_of(((dp + d) % DP) * slab, slab), slab)

        for t in range(X):
            r.sc[t] = (r.ss[t, core].astype(F32) + r.sin[t].astype(F32)).astype(BF16)
        for d in range(1, DP):
            for t in range(X):
                remote(
                    r.sc.at[t, slab_rows(d)], r.sp1.at[DP - d, t], r.sg_send.at[1], r.sg_recv.at[1], across(d)
                ).start()

    r.rg[...] = jnp.zeros((cw, width), F32)

    def from_x(i):
        gx.from_mate(i)
        for t in range(1, X):
            gx.from_pass(t, i)

    loop(ipd, from_x)
    gx.done()

    def reduced_back(b, i):
        def body(at, k, carry):
            mask = wide(r.maskf[at, :], width)
            d = mask * lead1 * (r.dh1[at, :].astype(F32) - base1 - r.xh1[at, :].astype(F32) * slant1)
            r.xh1[at, :] = d.astype(BF16)
            return carry

        strips((b * ipd + i) * CELLS, body, 0)
        r.rg[...] += dot(r.xt[b * ipd + i], r.xh1[rows_of(b, i), :])

    def input_back(b, i):
        at = rows_of(b, i)
        r.xv[at, :] = (r.dpre[at, :] + dot(r.xh1[at, :], r.wrt[...])).astype(BF16)
        pltpu.make_async_copy(r.xv.at[at], r.inputs_grad.at[at], r.store.at[1]).start()

    loop(ipd, lambda i: reduced_back(ch, i))

    def from_mate(i):
        gd.from_mate(i)
        reduced_back(block_of(0, False), i)

    loop(ipd, from_mate)
    loop(ipd, lambda i: input_back(ch, i))
    loop(ipd, lambda i: input_back(block_of(0, False), i))
    for t in range(1, X):

        def from_peer(i):
            gd.from_peer(t, i)
            reduced_back(block_of(t, True), i)

        loop(ipd, from_peer)
    for t in range(1, X):

        def from_pass(i):
            gd.from_pass(t, i)
            reduced_back(block_of(t, False), i)

        loop(ipd, from_pass)

    if c.reduce_inside:
        r.rs[...] = r.rg[...].T.astype(r.rs.dtype)
        for d in range(1, DP):
            remote(r.rs.at[piece_rows(d)], r.rbuf.at[DP - d], r.rg_send.at[0], r.rg_recv.at[0], across(d)).start()
    else:
        r.reduce_part[...] = r.rg[...].T
    if c.split_inside:
        drain(r.sp1.at[pl.ds(1, DP - 1)], r.sg_recv.at[1])
        for t in range(X):
            value = r.sc[(chip + t) % X, slab_rows(0), :].astype(F32)
            for d in range(1, DP):
                value = value + r.sp1[d, (chip + t) % X].astype(F32)
            r.sx[t] = value.astype(BF16)
            if t:
                remote(r.sx.at[t], r.sxin.at[X - t], r.sg_send.at[2], r.sg_recv.at[2], peer(t)).start()
    for t in range(1, X):
        loop(ipd, lambda i: input_back(block_of(t, True), i))
    if c.reduce_inside:
        groups = DP // CH
        goal = dp // groups
        drain(r.rbuf.at[pl.ds(1, DP - 1)], r.rg_recv.at[0])
        value = r.rs[piece_rows(0), :].astype(F32)
        for d in range(1, DP):
            value = value + r.rbuf[d].astype(F32)
        r.rsum[...] = value.astype(r.rsum.dtype)
        slot = r.rall.at[dp % groups, ch]
        for d in range(1, DP):
            remote(r.rsum, slot, r.rg_send.at[1], r.rg_recv.at[1], ((dp + d) % DP, goal)).start()

        @pl.when(goal == ch)
        def _():
            pltpu.make_async_copy(r.rsum, slot, r.rg_recv.at[1]).start()

        @pl.when(goal != ch)
        def _():
            remote(r.rsum, slot, r.rg_send.at[2], r.rg_recv.at[1], (dp, goal)).start()

    if c.split_inside:
        drain(r.sxin.at[pl.ds(1, X - 1)], r.sg_recv.at[2])
        value = r.sx[0].astype(F32)
        for t in range(1, X):
            value = value + r.sxin[t].astype(F32)
        r.so[0] = value.astype(BF16)
        for d in range(1, DP):
            remote(r.so.at[0], r.so.at[DP - d], r.sg_send.at[3], r.sg_recv.at[3], across(d)).start()
    for t in range(1, X):
        loop(ipd, lambda i: input_back(block_of(t, False), i))

    drain(r.eo.at[pl.ds(1, DP - 1)], r.eg_recv.at[1])
    for d in range(DP):
        r.expand_grad[piece_rows(d), :] = r.eo[d].astype(F32)
    if c.reduce_inside:
        drain(r.rall, r.rg_recv.at[1])
        r.tall[...] = jnp.zeros((LANES, CH * cw), F32)
        for s in range(groups):
            for q in range(CH):
                r.tall[s * piece : (s + 1) * piece, q * cw : (q + 1) * cw] = r.rall[s, q].astype(F32)
        for q in range(CH * cw // LANES):
            at = slice(q * LANES, (q + 1) * LANES)
            r.reduce_grad[at, :] = r.tall[:, at].T[:, 0:m1]
    if c.split_inside:
        drain(r.so.at[pl.ds(1, DP - 1)], r.sg_recv.at[3])
        for tap in range(9):
            at = slice(tap * half, (tap + 1) * half)
            block = jnp.concatenate([r.so[(d - dp + DP) % DP, :, at].astype(F32) for d in range(DP)], axis=0)
            r.split_grad[tap] = block.T

    for k, buf in enumerate((r.g1, r.g2, r.g3, r.g4, r.g5, r.g6)):
        everyone_done(buf, k)
    column_done(r.c1, 0)
    column_done(r.c2, 1)
    rs2.done()
    for gather in (gm, gd, gw):
        gather.done()
    drain(r.pbuf.at[pl.ds(1, CH - 1)], r.par_send.at[0])
    drain(r.ebuf.at[pl.ds(1, DP - 1)], r.eg_send.at[0])
    drain(r.ebuf.at[pl.ds(1, DP - 1)], r.eg_send.at[1])
    if c.reduce_inside:
        drain(r.rbuf.at[pl.ds(1, DP - 1)], r.rg_send.at[0])
        drain(r.rbuf.at[pl.ds(1, DP - 1)], r.rg_send.at[1])

        @pl.when(goal != ch)
        def _():
            drain(r.rsum, r.rg_send.at[2])

    if c.split_inside:
        drain(r.sin, r.sg_send.at[0])
        drain(r.sp1.at[pl.ds(1, DP - 1)], r.sg_send.at[1])
        drain(r.sxin.at[pl.ds(1, X - 1)], r.sg_send.at[2])
        drain(r.so.at[pl.ds(1, DP - 1)], r.sg_send.at[3])
    drain(r.cv, r.store.at[0])
    drain(r.xv, r.store.at[1])


ARGS = (
    "inputs", "resolution", "reduce_weight", "first_gain", "first_shift", "split_weight", "second_gain",
    "second_shift", "gate_down", "gate_gain", "gate_shift", "gate_up", "gate_bias", "expand_weight",
    "third_gain", "third_shift", "cotangent",
)


def per_device(*arrays):
    a = dict(zip(ARGS, arrays))
    c = types.SimpleNamespace()
    c.DP, c.CH = lax.axis_size("dp"), lax.axis_size("chan")
    c.X, c.D = c.CH // 2, c.DP * c.CH
    c.images = a["resolution"].shape[0]
    c.ipd = c.images // c.CH
    rows, c.cw = a["inputs"].shape
    c.width = a["reduce_weight"].shape[1]
    c.inner = a["gate_down"].shape[1]
    c.m1, c.m2, c.mg = c.width // c.CH, 2 * c.width // c.CH, c.inner // c.CH
    half, two = c.width // 2, 2 * c.width
    taps = 9 * half
    piece = c.width // c.DP
    piece_type = BF16 if piece % 16 == 0 else F32
    c.reduce_inside = c.DP % c.CH == 0 and piece % 8 == 0
    c.split_inside = c.m2 % (16 * c.DP) == 0
    own = c.ipd * CELLS
    DP, CH, X, D, ipd, cw, width = c.DP, c.CH, c.X, c.D, c.ipd, c.cw, c.width
    for name in ARGS:
        if a[name].ndim == 1 and name != "resolution":
            a[name] = a[name].reshape(1, -1)
    a["split_weight"] = a["split_weight"].reshape(taps, c.m2)
    sds = jax.ShapeDtypeStruct
    outs = dict(
        block_out=sds((rows, cw), BF16),
        inputs_grad=sds((rows, cw), BF16),
        first_gain_grad=sds((1, c.m1), F32),
        first_shift_grad=sds((1, c.m1), F32),
        second_gain_grad=sds((1, c.m2), F32),
        second_shift_grad=sds((1, c.m2), F32),
        down_grad=sds((width, c.mg), F32),
        gate_gain_grad=sds((1, c.mg), F32),
        gate_shift_grad=sds((1, c.mg), F32),
        up_grad=sds((c.inner, c.m2), F32),
        bias_grad=sds((1, c.m2), F32),
        expand_grad=sds((width, cw), F32),
        third_gain_grad=sds((1, cw), F32),
        third_shift_grad=sds((1, cw), F32),
    )
    if c.reduce_inside:
        outs["reduce_grad"] = sds((CH * cw, c.m1), F32)
    else:
        outs["reduce_part"] = sds((width, cw), F32)
    if c.split_inside:
        outs["split_grad"] = sds((9, half, c.m2), F32)
    else:
        outs["split_part"] = sds((two, taps), F32)
    V = pltpu.VMEM
    dma = lambda *shape: pltpu.SemaphoreType.DMA(shape)
    scratch = dict(
        xv=V((rows, cw), BF16), cv=V((rows, cw), BF16), wr=V((cw, width), BF16), wrt=V((width, cw), BF16),
        wet=V((cw, width), BF16), xt=V((c.images, cw, CELLS), BF16), mt=V((c.images, width, CELLS), BF16),
        maskf=V((rows, LANES), F32), area=V((c.images, LANES), F32), maskb=V((rows, LANES), BF16), pbuf=V((CH, 8, two), F32),
        red=V((own, width), F32), slope1=V((own, width), F32), xh1=V((rows, width), BF16),
        act=V((2, ipd, TALL, 3 * half), BF16), dsh=V((2, ipd, TALL, 3 * width), BF16),
        wg=V((CH, taps, c.m2), BF16), wf=V((2, taps, width), BF16), wt=V((2, 9 * width, half), BF16),
        sp=V((own, two), F32), slope2=V((own, two), F32), act2=V((own, two), F32), share=V((8, LANES), F32),
        gate_x=V((D * 8, LANES), F32), squeezed=V((D * 8, LANES), F32), gate_slope=V((D * 8, LANES), F32),
        grad_down=V((D * 8, LANES), F32), grad_summary=V((8, width), F32), att=V((8, two), F32),
        merged=V((rows, width), BF16), ex=V((rows, cw), F32), acc=V((16, cw), F32),
        dpre=V((rows, cw), F32), de=V((rows, cw), BF16), dm=V((own, width), F32), dh1=V((rows, width), BF16),

        dst=V((2, width, own), BF16),
        eg=V((width, cw), F32), es=V((width, cw), piece_type), ebuf=V((DP, piece, cw), piece_type),
        eo=V((DP, piece, cw), piece_type), rg=V((cw, width), F32),
        all_send=dma(6), all_recv=dma(6), col_send=dma(2), col_recv=dma(2),
        rs_core_send=dma(2), rs_core_recv=dma(2, X, ipd), rs_chip_send=dma(2), rs_chip_recv=dma(2, X, ipd),
        ag_core_send=dma(4), ag_core_recv=dma(4, ipd), ag_chip_send=dma(4, X), ag_chip_recv=dma(4, X, ipd),
        ag_pass_send=dma(4, X), ag_pass_recv=dma(4, X, ipd), par_send=dma(1), par_recv=dma(CH),
        eg_send=dma(2), eg_recv=dma(2), rg_send=dma(3), rg_recv=dma(2), sg_send=dma(4), sg_recv=dma(4),
        load=dma(2 + 2 * X), store=dma(2),
    )
    for name, count in (
        ("stage", X), ("inward", X), ("outward", X - 1), ("landed", X - 1), ("inward2", X), ("landed2", X - 1)
    ):
        scratch[name] = V((count, ipd, CELLS, width), BF16)
    for k in range(1, 7):
        scratch[f"g{k}"] = V((D, 8, LANES), F32)
    for k in range(1, 3):
        scratch[f"c{k}"] = V((DP, 8, LANES), F32)
    if c.reduce_inside:
        scratch.update(
            rs=V((width, cw), piece_type), rbuf=V((DP, piece, cw), piece_type), rsum=V((piece, cw), piece_type),
            rall=V((DP // CH, CH, piece, cw), piece_type), tall=V((LANES, CH * cw), F32),
        )
    if c.split_inside:
        slab = c.m2 // DP
        scratch.update(
            ss=V((X, 2, c.m2, taps), BF16), sin=V((X, c.m2, taps), BF16), sc=V((X, c.m2, taps), BF16),
            sp1=V((DP, X, slab, taps), BF16), sx=V((X, slab, taps), BF16), sxin=V((X, slab, taps), BF16),
            so=V((DP, slab, taps), BF16),
        )
    anywhere = pl.BlockSpec(memory_space=pl.ANY)
    vmem = pl.BlockSpec(memory_space=pltpu.VMEM)
    spec = dict(
        inputs=anywhere, cotangent=anywhere, reduce_weight=anywhere, block_out=anywhere, inputs_grad=anywhere,
        resolution=pl.BlockSpec(memory_space=pltpu.SMEM),
    )
    names = tuple(ARGS) + tuple(outs) + tuple(scratch)
    results = pl.pallas_call(
        functools.partial(kernel, c, names),
        out_shape=tuple(outs.values()),
        in_specs=[spec.get(name, vmem) for name in ARGS],
        out_specs=tuple(spec.get(name, vmem) for name in outs),
        scratch_shapes=list(scratch.values()),
        compiler_params=pltpu.CompilerParams(
            collective_id=0, has_side_effects=True, vmem_limit_bytes=62 * 2**20
        ),
        name="block",
    )(*[a[name] for name in ARGS])
    o = dict(zip(outs, results))
    if not c.reduce_inside:
        place = lax.axis_index("chan")
        part = lax.psum(o["reduce_part"], "dp")
        part = lax.all_gather(part, "chan", axis=1, tiled=True)
        o["reduce_grad"] = lax.dynamic_slice_in_dim(part, place * c.m1, c.m1, 0).T
    if not c.split_inside:
        place = lax.axis_index("chan")
        part = lax.psum(o["split_part"], ("dp", "chan"))
        part = lax.dynamic_slice_in_dim(part, place * c.m2, c.m2, 0)
        o["split_grad"] = part.T.reshape(9, half, c.m2)
    flat = lambda name: o[name].reshape(-1)
    return (
        o["block_out"], o["inputs_grad"], o["reduce_grad"], flat("first_gain_grad"), flat("first_shift_grad"),
        o["split_grad"], flat("second_gain_grad"), flat("second_shift_grad"), o["down_grad"],
        flat("gate_gain_grad"), flat("gate_shift_grad"), o["up_grad"], flat("bias_grad"), o["expand_grad"],
        flat("third_gain_grad"), flat("third_shift_grad"),
    )


def solution(mesh):
    placed = (
        P("dp", "chan"), P("dp"), P(), P("chan"), P("chan"), P(None, None, "chan"), P("chan"), P("chan"),
        P(), P(), P(), P(), P(), P(None, "chan"), P("chan"), P("chan"), P("dp", "chan"),
    )
    return jax.shard_map(
        per_device,
        mesh=mesh,
        in_specs=placed,
        out_specs=(
            P("dp", "chan"), P("dp", "chan"), P(None, "chan"), P("chan"), P("chan"), P(None, None, "chan"),
            P("chan"), P("chan"), P(None, "chan"), P("chan"), P("chan"), P(None, "chan"), P("chan"),
            P(None, "chan"), P("chan"), P("chan"),
        ),
        check_vma=False,
    )
```

time: 592 us -> 168 us (0.28)
  waiting for transfers between devices: 262 us -> 0 us
  blocking collectives: 183 us -> 0 us
  Pallas kernels: 0 us -> 152 us
  matrix products: 58.5 us -> 0 us
  other arithmetic: 49 us -> 0 us
  between operations: 14.6 us -> 0.75 us
  local copies, waits for them, and re-layouts: 23.6 us -> 14.9 us
    psum x8 -> x0, blocking collectives: 172 us -> none  [the longest x4 91.6 us: denormalize(): total, cross = lax.psum((total, cross), 'dp')]
    pallas_call x0 -> x1, Pallas kernels: none -> 152 us  [per_device(): pl.pallas_call(functools.partial(kernel, c, names), out_shape=tuple(outs....]
    all_gather x2 -> x0, waiting for transfers between devices: 94 us -> none  [the longest x1 62.7 us: per_device(): features_all = lax.all_gather(inputs, 'chan', axis=1, tiled=True)]
    psum x1 -> x0, waiting for transfers between devices: 81.2 us -> none  [per_device(): lax.psum((reduce_local, split_local, expand_grad, down_mine, up_mine, bia...]
    dot_general x39 -> x0, matrix products: 58.5 us -> none  [the longest x9 11.3 us: per_device(): jnp.einsum('rh,ro->ho', shifted, grad_splits, preferred_element_type=jnp....]
    unnamed x6 -> x0, waiting for transfers between devices: 43.1 us -> none
    reduce_scatter x1 -> x0, waiting for transfers between devices: 41.7 us -> none  [per_device(): lax.psum_scatter(grad_features.astype(jnp.bfloat16), 'chan', scatter_dime...]
    reduce_sum x7 -> x0, other arithmetic: 19.3 us -> none  [the longest x3 14 us: denormalize(): total = jnp.sum(grads, 0)]
  transfers between devices with their start and end apart: 7 -> 0, of which waited for: 6 -> 0; matrix products, arithmetic and copies ran while one was open for 6% -> 0% of each run, Pallas kernels for 0% -> 0%
where the time goes in v1:
time: 168 us
  Pallas kernels  152 us (90%)
  local copies, waits for them, and re-layouts  14.9 us (9%)
    pallas_call x1, Pallas kernels, per_device(): pl.pallas_call(functools.partial(kernel, c, names), out_shape=tuple(outs....  152 us
    unnamed x42, local copies, waits for them, and re-layouts  14.9 us

profile of v1, /device:TPU:0, one launch (start us, length us, event | category | flops | bytes accessed | tf_op | source)
XLA Modules:
  0.0 168.2 jit_solution(8009535523332523550)
XLA Ops:
  0.7 152.5 %block.1 = (bf16[4096,256]{1,0:T(8,128)(2,1)}, bf16[4096,256]{1,0:T(8,128)(2,1)}, f32[1,64]{1,0:T(1,128)}, f32[1,64]{1,0:T(1,128)}, f32[1,128]{1,0:T(1,128)}, /*...) custom-call(bf16[4096,256]{1,0:T(8,128)(2,1)} %refs_0_.1, ...), custom_call_target="tpu_custom_call" | custom-call | tf_op jit(solution)/shard_map/block/pallas_call | solution.py:1092
  153.1 1.6 copy.34
  154.7 1.9 %copy.33 = f32[1024,64]{0,1:T(8,128)} copy(f32[1024,64]{1,0:T(8,128)} %get-tuple-element.50) | data formatting | bytes 524288
  156.7 0.0 copy-start
  156.7 3.2 %copy.49 = bf16[4096,256]{1,0:T(8,128)(2,1)} copy(bf16[4096,256]{1,0:T(8,128)(2,1)} %get-tuple-element.80) | data formatting | bytes 4194304
  159.9 0.0 copy-done
  159.9 0.0 copy-start.12
  159.9 0.0 copy-start.11
  159.9 0.0 copy-start.1
  159.9 0.0 copy-start.10
  159.9 0.0 copy-start.9
  159.9 0.0 copy-start.8
  159.9 0.0 copy-start.7
  159.9 0.0 copy-start.3
  159.9 0.0 copy-start.6
  159.9 0.0 copy-start.2
  159.9 0.0 copy-start.5
  160.0 0.0 copy-start.4
  160.0 1.3 copy.50
  161.3 0.0 copy-done.12
  161.3 0.5 copy.51
  161.8 0.0 copy-done.11
  161.8 0.5 copy.52
  162.3 0.0 copy-done.1
  162.3 0.8 copy.53
  163.1 0.0 copy-done.10
  163.1 0.5 copy.54
  163.7 0.0 copy-done.9
  163.7 0.5 copy.55
  164.2 0.0 copy-done.8
  164.2 0.5 copy.56
  164.7 0.0 copy-done.7
  164.7 0.5 copy.57
  165.2 0.0 copy-done.3
  165.2 0.6 copy.58
  165.8 0.0 copy-done.6
  165.8 0.5 copy.59
  166.3 0.0 copy-done.2
  166.3 0.7 copy.60
  167.0 0.0 copy-done.5
  167.1 0.6 copy.61
  167.6 0.0 copy-done.4
  167.6 0.6 copy.62
Async XLA Ops:
  156.7 3.2 %copy-start = (bf16[4096,256]{1,0:T(8,128)(2,1)S(1)}, bf16[4096,256]{1,0:T(8,128)(2,1)}, u32[]{:S(2)}) copy-start(bf16[4096,256]{1,0:T(8,128)(2,1)} %get-tuple-element.81) | copy-start | bytes 6291460
  159.9 1.4 copy-start.12
  159.9 1.9 %copy-start.11 = (f32[1,64]{1,0:T(1,128)S(1)}, f32[1,64]{1,0:T(1,128)}, u32[]{:S(2)}) copy-start(f32[1,64]{1,0:T(1,128)} %get-tuple-element.36) | copy-start | bytes 772
  159.9 2.4 %copy-start.1 = (f32[9,128,128]{2,1,0:T(8,128)S(1)}, f32[9,128,128]{2,1,0:T(8,128)}, u32[]{:S(2)}) copy-start(f32[9,128,128]{2,1,0:T(8,128)} %get-tuple-element.85) | copy-start | bytes 1769476
  159.9 3.3 %copy-start.10 = (f32[1,128]{1,0:T(1,128)S(1)}, f32[1,128]{1,0:T(1,128)}, u32[]{:S(2)}) copy-start(f32[1,128]{1,0:T(1,128)} %get-tuple-element.38) | copy-start | bytes 1540
  159.9 3.8 %copy-start.9 = (f32[1,128]{1,0:T(1,128)S(1)}, f32[1,128]{1,0:T(1,128)}, u32[]{:S(2)}) copy-start(f32[1,128]{1,0:T(1,128)} %get-tuple-element.39) | copy-start | bytes 1540
  159.9 4.3 %copy-start.8 = (f32[1,32]{1,0:T(1,128)S(1)}, f32[1,32]{1,0:T(1,128)}, u32[]{:S(2)}) copy-start(f32[1,32]{1,0:T(1,128)} %get-tuple-element.41) | copy-start | bytes 388
  159.9 4.8 %copy-start.7 = (f32[1,32]{1,0:T(1,128)S(1)}, f32[1,32]{1,0:T(1,128)}, u32[]{:S(2)}) copy-start(f32[1,32]{1,0:T(1,128)} %get-tuple-element.42) | copy-start | bytes 388
  159.9 5.3 %copy-start.3 = (f32[128,128]{1,0:T(8,128)S(1)}, f32[128,128]{1,0:T(8,128)}, u32[]{:S(2)}) copy-start(f32[128,128]{1,0:T(8,128)} %get-tuple-element.91) | copy-start | bytes 196612
  159.9 5.9 %copy-start.6 = (f32[1,128]{1,0:T(1,128)S(1)}, f32[1,128]{1,0:T(1,128)}, u32[]{:S(2)}) copy-start(f32[1,128]{1,0:T(1,128)} %get-tuple-element.44) | copy-start | bytes 1540
  159.9 6.4 %copy-start.2 = (f32[256,256]{1,0:T(8,128)S(1)}, f32[256,256]{1,0:T(8,128)}, u32[]{:S(2)}) copy-start(f32[256,256]{1,0:T(8,128)} %get-tuple-element.93) | copy-start | bytes 786436
  159.9 7.1 %copy-start.5 = (f32[1,256]{1,0:T(1,128)S(1)}, f32[1,256]{1,0:T(1,128)}, u32[]{:S(2)}) copy-start(f32[1,256]{1,0:T(1,128)} %get-tuple-element.46) | copy-start | bytes 3076
  160.0 7.7 %copy-start.4 = (f32[1,256]{1,0:T(1,128)S(1)}, f32[1,256]{1,0:T(1,128)}, u32[]{:S(2)}) copy-start(f32[1,256]{1,0:T(1,128)} %get-tuple-element.47) | copy-start | bytes 3076

commit v2 on v1

--- a/solution.py
+++ b/solution.py
@@ -144,6 +144,18 @@
         for d in range(1, DP):
             remote(buf.at[0], buf.at[DP - d], r.col_send.at[k], r.col_recv.at[k], across(d)).start()
 
+    def row(buf, k, source=None):
+        for q in range(1, CH):
+            src = buf.at[0] if source is None else source.at[(ch + q) % CH]
+            remote(src, buf.at[CH - q], r.row_send.at[k], r.row_recv.at[k], (dp, (ch + q) % CH)).start()
+
+    def row_sum(buf, k, column_buf):
+        drain(buf.at[pl.ds(1, CH - 1)], r.row_recv.at[k])
+        column_buf[0] = jnp.sum(buf[...], axis=0)
+
+    def row_done(buf, k):
+        drain(buf.at[pl.ds(1, CH - 1)], r.row_send.at[k])
+
     def column_wait(buf, k):
         drain(buf.at[pl.ds(1, DP - 1)], r.col_recv.at[k])
 
@@ -240,6 +252,55 @@
             for t in range(1, X):
                 drain(self.whole(ch), r.ag_chip_send.at[self.k, t])
                 drain(self.whole(block_of(t, True)), r.ag_pass_send.at[self.k, t])
+
+    class Share:
+        def __init__(self, k, blocks, rows):
+            self.k, self.blocks, self.piece = k, blocks, rows // DP
+
+        def part(self, b, d):
+            at = pl.ds(pl.multiple_of(((dp + d) % DP) * self.piece, self.piece), self.piece)
+            return self.blocks.at[b, at]
+
+        def send(self):
+            own = self.blocks.at[ch]
+            remote(own, own, r.sh_core_send.at[self.k], r.sh_core_recv.at[self.k], mate).start()
+            for t in range(1, X):
+                src = self.part(ch, 0) if c.share else own
+                remote(src, src, r.sh_chip_send.at[self.k, t], r.sh_chip_recv.at[self.k, X - t], peer(t)).start()
+
+        def spread(self):
+            for t in range(1, X):
+                b = block_of(t, True)
+                src = self.part(b, 0) if c.share else self.blocks.at[b]
+                drain(src, r.sh_chip_recv.at[self.k, t])
+                if c.share:
+                    for d in range(1, DP):
+                        remote(src, src, r.sh_col_send.at[self.k, t], r.sh_col_recv.at[self.k, t, DP - d], across(d)).start()
+
+        def hand(self):
+            for t in range(1, X):
+                b = block_of(t, True)
+                if c.share:
+                    for d in range(1, DP):
+                        drain(self.part(b, d), r.sh_col_recv.at[self.k, t, d])
+                whole = self.blocks.at[b]
+                remote(whole, whole, r.sh_pass_send.at[self.k, t], r.sh_pass_recv.at[self.k, t], mate).start()
+
+        def take(self):
+            drain(self.blocks.at[block_of(0, False)], r.sh_core_recv.at[self.k])
+            for t in range(1, X):
+                drain(self.blocks.at[block_of(t, False)], r.sh_pass_recv.at[self.k, t])
+
+        def done(self):
+            own = self.blocks.at[ch]
+            drain(own, r.sh_core_send.at[self.k])
+            for t in range(1, X):
+                whole = self.blocks.at[block_of(t, True)]
+                drain(self.part(ch, 0) if c.share else own, r.sh_chip_send.at[self.k, t])
+                drain(whole, r.sh_pass_send.at[self.k, t])
+                if c.share:
+                    for d in range(1, DP):
+                        drain(self.part(block_of(t, True), 0), r.sh_col_send.at[self.k, t])
 
     barrier = pltpu.get_barrier_semaphore()
 
@@ -279,6 +340,37 @@
 
     loop(images, make_mask)
 
+    def part_reduce(b, i):
+        at = rows_of(b, i)
+        x = r.xv[at, :] * wide(r.maskb[at, :], cw)
+        r.xv[at, :] = x
+        return dot(x, r.wr[...])
+
+    r.wg[ch] = r.split_weight[...]
+    r.wx[ch] = r.expand_weight[...]
+    shares = (Share(0, r.wg, taps), Share(1, r.wx, width))
+
+    load_w.wait()
+    rs1 = Scatter(0, r.stage, r.inward, r.outward, r.landed, r.red)
+    loads[0].wait()
+    rs1.compute_mate(1, part_reduce)
+    pl.semaphore_wait(barrier, D - 1)
+    rs1.send_mate(1)
+    for share in shares:
+        share.send()
+    for t in range(1, X):
+        if t > 1:
+            loads[2 * t - 2].wait()
+            rs1.to_mate(t, part_reduce)
+        loads[2 * t - 1].wait()
+        rs1.to_peer(t, part_reduce)
+    for share in shares:
+        share.spread()
+    loads[2 * X - 2].wait()
+    rs1.to_mate(0, part_reduce)
+    loads[2 * X - 1].wait()
+    rs1.own(part_reduce)
+
     def selector(parts, mine):
         row = lax.broadcasted_iota(jnp.int32, (mine, mine * parts), 0)
         col = lax.broadcasted_iota(jnp.int32, (mine, mine * parts), 1)
@@ -292,34 +384,8 @@
     r.pbuf[0, 2:3, :] = exact(r.second_gain[...], pick2)
     r.pbuf[0, 3:4, :] = exact(r.second_shift[...], pick2)
 
-    def part_reduce(b, i):
-        at = rows_of(b, i)
-        x = r.xv[at, :] * wide(r.maskb[at, :], cw)
-        r.xv[at, :] = x
-        return dot(x, r.wr[...])
-
-    load_w.wait()
-    rs1 = Scatter(0, r.stage, r.inward, r.outward, r.landed, r.red)
-    loads[0].wait()
-    rs1.compute_mate(1, part_reduce)
-    pl.semaphore_wait(barrier, D - 1)
-    rs1.send_mate(1)
-    for t in range(1, X):
-        if t > 1:
-            loads[2 * t - 2].wait()
-            rs1.to_mate(t, part_reduce)
-        loads[2 * t - 1].wait()
-        rs1.to_peer(t, part_reduce)
-    loads[2 * X - 2].wait()
-    rs1.to_mate(0, part_reduce)
-    loads[2 * X - 1].wait()
-    rs1.own(part_reduce)
-
     for q in range(1, CH):
         remote(r.pbuf.at[0], r.pbuf.at[CH - q], r.par_send.at[0], r.par_recv.at[CH - q], (dp, (ch + q) % CH)).start()
-    r.wg[ch] = r.split_weight[...]
-    gw = Gather(3, lambda b, i: r.wg.at[b], lambda b: r.wg.at[b], 1)
-    gw.send(0)
 
     r.wrt[...] = flip(r.wr[...])
     r.wet[...] = flip(r.expand_weight[...])
@@ -357,7 +423,8 @@
     put(r.g1, width // LANES, total(second))
     r.g1[0, 6:7, :] = pixels
     everyone(r.g1, 0)
-
+    for share in shares:
+        share.hand()
     everyone_wait(r.g1, 0)
     sums = jnp.sum(r.g1[...], axis=0)
     count = sums[6:7, 0:1]
@@ -368,8 +435,6 @@
         params = params + r.pbuf[q]
     gain1, shift1 = params[0:1, 0:width], params[1:2, 0:width]
     gain2, shift2 = params[2:3, :], params[3:4, :]
-    for t in range(1, X):
-        gw.from_peer(t, 0)
 
     def moments(first, second):
         mean = first * inverse
@@ -407,13 +472,11 @@
             return carry
 
         strips(i * CELLS, body, 0)
-        gx.send(i)
 
     loop(ipd, first_act)
 
-    gw.from_mate(0)
-    for t in range(1, X):
-        gw.from_pass(t, 0)
+    for share in shares:
+        share.take()
     for g in range(2):
         for q in range(CH // 2):
             r.wf[g, :, q * m2 : (q + 1) * m2] = r.wg[g * (CH // 2) + q]
@@ -534,55 +597,42 @@
             return carry
 
         strips(i * CELLS, body, 0)
-        gm.send(i)
-
-    loop(ipd, merge)
-
+
+    merge(0)
+    gm.send(0)
+    lax.fori_loop(1, ipd, lambda i, carry: (merge(i), carry)[1], 0)
+
+    def expand_sums(k):
+        def body(i, state):
+            value = dot(r.merged[rows_of(ch, i), :], r.wx[k])
+            return (state[0] + fold(value), state[1] + fold(value * value))
+
+        first, second = lax.fori_loop(0, ipd, body, (zero_c, zero_c))
+        put(r.sums3.at[pl.ds(k, 1)], 0, total(first))
+        put(r.sums3.at[pl.ds(k, 1)], cw // LANES, total(second))
+
+    zero_c = jnp.zeros((8, cw), F32)
+    loop(CH, expand_sums)
+    r.r1[0] = r.sums3[ch]
+    row(r.r1, 0, r.sums3)
+    lax.fori_loop(1, ipd, lambda i, carry: (gm.send(i), carry)[1], 0)
+    load_c.wait()
     r.acc[...] = jnp.zeros((16, cw), F32)
-
-    def expand(b, i):
-        at = rows_of(b, i)
-        value = dot(r.merged[at, :], r.expand_weight[...])
-        r.ex[at, :] = value
-        r.acc[0:8, :] += fold(value)
-        r.acc[8:16, :] += fold(value * value)
-
-    loop(ipd, lambda i: expand(ch, i))
-
-    def expand_mate(i):
-        gm.from_mate(i)
-        expand(block_of(0, False), i)
-
-    loop(ipd, expand_mate)
-    for t in range(1, X):
-
-        def expand_peer(i):
-            gm.from_peer(t, i)
-            expand(block_of(t, True), i)
-
-        loop(ipd, expand_peer)
-    for t in range(1, X):
-
-        def expand_pass(i):
-            gm.from_pass(t, i)
-            expand(block_of(t, False), i)
-
-        loop(ipd, expand_pass)
-    put(r.c1, 0, total(r.acc[0:8, :]))
-    put(r.c1, cw // LANES, total(r.acc[8:16, :]))
+    row_sum(r.r1, 0, r.c1)
     column(r.c1, 0)
-    load_c.wait()
-
-    def turn_m(j):
-        r.mt[j] = flip(r.merged[image(j), :])
-
-    loop(images, turn_m)
+
+    def turn_own(j):
+        r.mt[ch * ipd + j] = flip(r.merged[rows_of(ch, j), :])
+
+    loop(ipd, turn_own)
     column_wait(r.c1, 0)
     sums = jnp.sum(r.c1[...], axis=0)
     mean3, scale3 = moments(get(sums, 0, cw), get(sums, cw // LANES, cw))
     gain3, shift3 = r.third_gain[...], r.third_shift[...]
 
-    def outputs(j, state):
+    def outputs(b, i):
+        r.ex[rows_of(b, i), :] = dot(r.merged[rows_of(b, i), :], r.expand_weight[...])
+
         def body(at, k, state):
             shift, cross = state
             mask = wide(r.maskf[at, :], cw)
@@ -596,15 +646,45 @@
             r.ex[at, :] = xh
             return (shift + fold(d), cross + fold(d * xh))
 
-        state = strips(j * CELLS, body, state)
-        pltpu.make_async_copy(r.cv.at[image(j)], r.block_out.at[image(j)], r.store.at[0]).start()
-        return state
-
-    zero_c = jnp.zeros((8, cw), F32)
-    shift, cross = lax.fori_loop(0, images, outputs, (zero_c, zero_c))
-    put(r.c2, 0, total(shift))
-    put(r.c2, cw // LANES, total(cross))
+        shift, cross = strips((b * ipd + i) * CELLS, body, (zero_c, zero_c))
+        r.acc[0:8, :] += shift
+        r.acc[8:16, :] += cross
+        at = rows_of(b, i)
+        pltpu.make_async_copy(r.cv.at[at], r.block_out.at[at], r.store.at[0]).start()
+
+    loop(ipd, lambda i: outputs(ch, i))
+
+    def outputs_mate(i):
+        gm.from_mate(i)
+        outputs(block_of(0, False), i)
+
+    loop(ipd, outputs_mate)
+    for t in range(1, X):
+
+        def outputs_peer(i):
+            gm.from_peer(t, i)
+            outputs(block_of(t, True), i)
+
+        loop(ipd, outputs_peer)
+    lax.fori_loop(1, ipd, lambda i, carry: (gx.send(i), carry)[1], 0)
+    for t in range(1, X):
+
+        def outputs_pass(i):
+            gm.from_pass(t, i)
+            outputs(block_of(t, False), i)
+
+        loop(ipd, outputs_pass)
+    put(r.c2, 0, total(r.acc[0:8, :]))
+    put(r.c2, cw // LANES, total(r.acc[8:16, :]))
     column(r.c2, 1)
+
+    def turn_other(j):
+        b = j // ipd
+        b = jnp.where(b < ch, b, b + 1)
+        at = b * ipd + j % ipd
+        r.mt[at] = flip(r.merged[image(at), :])
+
+    loop(images - ipd, turn_other)
     column_wait(r.c2, 1)
     sums = jnp.sum(r.c2[...], axis=0)
     shift_grad, gain_grad = get(sums, 0, cw), get(sums, cw // LANES, cw)
@@ -629,6 +709,7 @@
         rs2.to_peer(t, part_merged)
     rs2.to_mate(0, part_merged)
     rs2.own(part_merged)
+    gx.send(0)
 
     def grow(j):
         r.eg[...] += dot(r.mt[j], r.de[image(j), :])
@@ -725,7 +806,7 @@
         sum_lo, sum_hi = lower_upper(r.g3, n)
         grad_lo, grad_hi = lower_upper(r.g4, n)
         picked = exact_nt(r.grad_down[at, :], pickg)
-        down = jnp.concatenate([exact_tn(sum_lo, picked), exact_tn(sum_hi, picked)], axis=0)
+        down = jnp.concatenate([exact_tn(picked, sum_lo), exact_tn(picked, sum_hi)], axis=1)
         squeezed = r.squeezed[at, :]
         up = jnp.concatenate([exact_tn(squeezed, grad_lo), exact_tn(squeezed, grad_hi)], axis=1)
         bias = jnp.concatenate([total(grad_lo), total(grad_hi)], axis=1)
@@ -733,7 +814,7 @@
 
     down, up, bias = lax.fori_loop(
         0, gate_blocks, gate_grads,
-        (jnp.zeros((width, mg), F32), jnp.zeros((inner, width), F32), jnp.zeros((1, width), F32)),
+        (jnp.zeros((mg, width), F32), jnp.zeros((inner, width), F32), jnp.zeros((1, width), F32)),
     )
     r.down_grad[...] = down
     r.up_grad[...] = exact_nt(jnp.concatenate([up, -up], axis=1), pick2)
@@ -783,11 +864,10 @@
 
     zero_h = jnp.zeros((8, half), F32)
     state = lax.fori_loop(0, ipd, first_back, ((zero_h, zero_h), (zero_h, zero_h)))
-    r.g6[0] = jnp.zeros((8, LANES), F32)
     for g in range(2):
-        r.g6[0, g : g + 1, :] = total(state[g][0])
-        r.g6[0, 2 + g : 3 + g, :] = total(state[g][1])
-    everyone(r.g6, 5)
+        r.r3[0, g : g + 1, :] = total(state[g][0])
+        r.r3[0, 2 + g : 3 + g, :] = total(state[g][1])
+    row(r.r3, 1)
     gd = Gather(2, lambda b, i: r.dh1.at[rows_of(b, i)], lambda b: r.dh1.at[block_rows(b)], ipd)
     loop(ipd, gd.send)
 
@@ -803,41 +883,63 @@
 
     loop(ipd, turn_d)
     per = CH // 2
-    for g in range(2):
-        for k in range(3):
-            lanes = slice(3 * k * half, 3 * (k + 1) * half)
-            right = r.act[g, :, k * SIDE : k * SIDE + CELLS, :].reshape(own_rows, 3 * half)
+    wide3 = 3 * half
+    for k in range(3):
+        for g in range(2):
+            right = r.act[g, :, k * SIDE : k * SIDE + CELLS, :].reshape(own_rows, wide3)
             value = dot(r.dst[g], right)
             if c.split_inside:
                 for q in range(per):
                     b = g * per + q
-                    r.ss[b // 2, b % 2, :, lanes] = value[q * m2 : (q + 1) * m2, :].astype(BF16)
+                    r.ss[k, b % 2, b // 2] = value[q * m2 : (q + 1) * m2, :].astype(BF16)
             else:
-                r.split_part[g * width : (g + 1) * width, lanes] = value
-    if c.split_inside:
-        remote(r.ss.at[:, 1 - core], r.sin, r.sg_send.at[0], r.sg_recv.at[0], mate).start()
-
-    everyone_wait(r.g6, 5)
-    sums = jnp.sum(r.g6[...], axis=0)
+                r.split_part[g * width : (g + 1) * width, k * wide3 : (k + 1) * wide3] = value
+        if c.split_inside:
+            remote(r.ss.at[k, 1 - core], r.sin.at[k], r.sg_send.at[0, k], r.sg_recv.at[0, k], mate).start()
+    row_sum(r.r3, 1, r.c3)
+    column(r.c3, 2)
+    slab = m2 // DP
+
+    def split_spread(k):
+        drain(r.sin.at[k], r.sg_recv.at[0, k])
+        for t in range(X):
+            value = (r.ss[k, core, t].astype(F32) + r.sin[k, t].astype(F32)).astype(BF16)
+            r.sc[k, :, t] = value.reshape(DP, slab, wide3)
+        for d in range(1, DP):
+            remote(
+                r.sc.at[k, (dp + d) % DP], r.sp1.at[k, DP - d], r.sg_send.at[1, k], r.sg_recv.at[1, k], across(d)
+            ).start()
+
+    def split_chips(k):
+        drain(r.sp1.at[k, pl.ds(1, DP - 1)], r.sg_recv.at[1, k])
+        for t in range(X):
+            there = (chip + t) % X
+            value = r.sc[k, dp, there].astype(F32)
+            for d in range(1, DP):
+                value = value + r.sp1[k, d, there].astype(F32)
+            r.sx[k, t] = value.astype(BF16)
+            if t:
+                remote(r.sx.at[k, t], r.sxin.at[k, X - t], r.sg_send.at[2, k], r.sg_recv.at[2, k], peer(t)).start()
+
+    def split_out(k):
+        drain(r.sxin.at[k, pl.ds(1, X - 1)], r.sg_recv.at[2, k])
+        value = r.sx[k, 0].astype(F32)
+        for t in range(1, X):
+            value = value + r.sxin[k, t].astype(F32)
+        r.so[k, 0] = value.astype(BF16)
+        for d in range(1, DP):
+            remote(r.so.at[k, 0], r.so.at[k, DP - d], r.sg_send.at[3, k], r.sg_recv.at[3, k], across(d)).start()
+
+    def split_step(step, k):
+        if c.split_inside:
+            step(k)
+
+    for k in range(3):
+        split_step(split_spread, k)
+    column_wait(r.c3, 2)
+    sums = jnp.sum(r.c3[...], axis=0)
     shift_grad, gain_grad = get(sums, 0, width), get(sums, 2, width)
-    r.first_gain_grad[...] = exact_nt(gain_grad, pick1)
-    r.first_shift_grad[...] = exact_nt(shift_grad, pick1)
     lead1, base1, slant1 = gain1 * scale1, shift_grad * inverse, gain_grad * inverse
-
-    if c.split_inside:
-        drain(r.sin, r.sg_recv.at[0])
-        slab = m2 // DP
-
-        def slab_rows(d):
-            return pl.ds(pl.multiple_of(((dp + d) % DP) * slab, slab), slab)
-
-        for t in range(X):
-            r.sc[t] = (r.ss[t, core].astype(F32) + r.sin[t].astype(F32)).astype(BF16)
-        for d in range(1, DP):
-            for t in range(X):
-                remote(
-                    r.sc.at[t, slab_rows(d)], r.sp1.at[DP - d, t], r.sg_send.at[1], r.sg_recv.at[1], across(d)
-                ).start()
 
     r.rg[...] = jnp.zeros((cw, width), F32)
 
@@ -880,6 +982,7 @@
             reduced_back(block_of(t, True), i)
 
         loop(ipd, from_peer)
+    split_step(split_chips, 0)
     for t in range(1, X):
 
         def from_pass(i):
@@ -894,17 +997,10 @@
             remote(r.rs.at[piece_rows(d)], r.rbuf.at[DP - d], r.rg_send.at[0], r.rg_recv.at[0], across(d)).start()
     else:
         r.reduce_part[...] = r.rg[...].T
-    if c.split_inside:
-        drain(r.sp1.at[pl.ds(1, DP - 1)], r.sg_recv.at[1])
-        for t in range(X):
-            value = r.sc[(chip + t) % X, slab_rows(0), :].astype(F32)
-            for d in range(1, DP):
-                value = value + r.sp1[d, (chip + t) % X].astype(F32)
-            r.sx[t] = value.astype(BF16)
-            if t:
-                remote(r.sx.at[t], r.sxin.at[X - t], r.sg_send.at[2], r.sg_recv.at[2], peer(t)).start()
+    split_step(split_chips, 1)
     for t in range(1, X):
         loop(ipd, lambda i: input_back(block_of(t, True), i))
+    split_step(split_out, 0)
     if c.reduce_inside:
         groups = DP // CH
         goal = dp // groups
@@ -925,42 +1021,41 @@
         def _():
             remote(r.rsum, slot, r.rg_send.at[2], r.rg_recv.at[1], (dp, goal)).start()
 
-    if c.split_inside:
-        drain(r.sxin.at[pl.ds(1, X - 1)], r.sg_recv.at[2])
-        value = r.sx[0].astype(F32)
-        for t in range(1, X):
-            value = value + r.sxin[t].astype(F32)
-        r.so[0] = value.astype(BF16)
-        for d in range(1, DP):
-            remote(r.so.at[0], r.so.at[DP - d], r.sg_send.at[3], r.sg_recv.at[3], across(d)).start()
+    split_step(split_chips, 2)
+    split_step(split_out, 1)
     for t in range(1, X):
         loop(ipd, lambda i: input_back(block_of(t, False), i))
+    r.first_gain_grad[...] = exact_nt(gain_grad, pick1)
+    r.first_shift_grad[...] = exact_nt(shift_grad, pick1)
+    split_step(split_out, 2)
 
     drain(r.eo.at[pl.ds(1, DP - 1)], r.eg_recv.at[1])
     for d in range(DP):
         r.expand_grad[piece_rows(d), :] = r.eo[d].astype(F32)
     if c.reduce_inside:
         drain(r.rall, r.rg_recv.at[1])
-        r.tall[...] = jnp.zeros((LANES, CH * cw), F32)
         for s in range(groups):
             for q in range(CH):
-                r.tall[s * piece : (s + 1) * piece, q * cw : (q + 1) * cw] = r.rall[s, q].astype(F32)
-        for q in range(CH * cw // LANES):
-            at = slice(q * LANES, (q + 1) * LANES)
-            r.reduce_grad[at, :] = r.tall[:, at].T[:, 0:m1]
+                r.reduce_grad[s * piece : (s + 1) * piece, q * cw : (q + 1) * cw] = r.rall[s, q].astype(F32)
     if c.split_inside:
-        drain(r.so.at[pl.ds(1, DP - 1)], r.sg_recv.at[3])
-        for tap in range(9):
-            at = slice(tap * half, (tap + 1) * half)
-            block = jnp.concatenate([r.so[(d - dp + DP) % DP, :, at].astype(F32) for d in range(DP)], axis=0)
-            r.split_grad[tap] = block.T
-
-    for k, buf in enumerate((r.g1, r.g2, r.g3, r.g4, r.g5, r.g6)):
+        for k in range(3):
+            drain(r.so.at[k, pl.ds(1, DP - 1)], r.sg_recv.at[3, k])
+            for p in range(3):
+                at = slice(p * half, (p + 1) * half)
+                block = jnp.concatenate(
+                    [r.so[k, (d - dp + DP) % DP, :, at].astype(F32) for d in range(DP)], axis=0
+                )
+                r.split_grad[3 * k + p] = block.T
+
+    for k, buf in enumerate((r.g1, r.g2, r.g3, r.g4, r.g5)):
         everyone_done(buf, k)
     column_done(r.c1, 0)
+    column_done(r.c3, 2)
+    row_done(r.r1, 0)
+    row_done(r.r3, 1)
     column_done(r.c2, 1)
     rs2.done()
-    for gather in (gm, gd, gw):
+    for gather in (gm, gd) + shares:
         gather.done()
     drain(r.pbuf.at[pl.ds(1, CH - 1)], r.par_send.at[0])
     drain(r.ebuf.at[pl.ds(1, DP - 1)], r.eg_send.at[0])
@@ -974,12 +1069,33 @@
             drain(r.rsum, r.rg_send.at[2])
 
     if c.split_inside:
-        drain(r.sin, r.sg_send.at[0])
-        drain(r.sp1.at[pl.ds(1, DP - 1)], r.sg_send.at[1])
-        drain(r.sxin.at[pl.ds(1, X - 1)], r.sg_send.at[2])
-        drain(r.so.at[pl.ds(1, DP - 1)], r.sg_send.at[3])
+        for k in range(3):
+            drain(r.sin.at[k], r.sg_send.at[0, k])
+            drain(r.sp1.at[k, pl.ds(1, DP - 1)], r.sg_send.at[1, k])
+            drain(r.sxin.at[k, pl.ds(1, X - 1)], r.sg_send.at[2, k])
+            drain(r.so.at[k, pl.ds(1, DP - 1)], r.sg_send.at[3, k])
     drain(r.cv, r.store.at[0])
     drain(r.xv, r.store.at[1])
+
+
+def hand_over(*refs):
+    count = (len(refs) - 1) // 3
+    sources, results, places, sems = refs[:count], refs[count : 2 * count], refs[2 * count : -1], refs[-1]
+    copies = []
+    for source, result, place in zip(sources, results, places):
+        rows = source.shape[0]
+        parts = 2 if rows >= 1024 else 1
+        for p in range(parts):
+            at = pl.ds(p * (rows // parts), rows // parts)
+            k = len(copies)
+            inward = pltpu.make_async_copy(source.at[at], place.at[at], sems.at[k, 0])
+            copies.append((inward, pltpu.make_async_copy(place.at[at], result.at[at], sems.at[k, 1])))
+            inward.start()
+    for inward, outward in copies:
+        inward.wait()
+        outward.start()
+    for inward, outward in copies:
+        outward.wait()
 
 
 ARGS = (
@@ -1005,6 +1121,7 @@
     piece = c.width // c.DP
     piece_type = BF16 if piece % 16 == 0 else F32
     c.reduce_inside = c.DP % c.CH == 0 and piece % 8 == 0
+    c.share = taps % (16 * c.DP) == 0 and c.width % (16 * c.DP) == 0
     c.split_inside = c.m2 % (16 * c.DP) == 0
     own = c.ipd * CELLS
     DP, CH, X, D, ipd, cw, width = c.DP, c.CH, c.X, c.D, c.ipd, c.cw, c.width
@@ -1020,7 +1137,7 @@
         first_shift_grad=sds((1, c.m1), F32),
         second_gain_grad=sds((1, c.m2), F32),
         second_shift_grad=sds((1, c.m2), F32),
-        down_grad=sds((width, c.mg), F32),
+        down_grad=sds((c.mg, width), F32),
         gate_gain_grad=sds((1, c.mg), F32),
         gate_shift_grad=sds((1, c.mg), F32),
         up_grad=sds((c.inner, c.m2), F32),
@@ -1030,7 +1147,7 @@
         third_shift_grad=sds((1, cw), F32),
     )
     if c.reduce_inside:
-        outs["reduce_grad"] = sds((CH * cw, c.m1), F32)
+        outs["reduce_grad"] = sds((c.m1, CH * cw), F32)
     else:
         outs["reduce_part"] = sds((width, cw), F32)
     if c.split_inside:
@@ -1045,7 +1162,7 @@
         maskf=V((rows, LANES), F32), area=V((c.images, LANES), F32), maskb=V((rows, LANES), BF16), pbuf=V((CH, 8, two), F32),
         red=V((own, width), F32), slope1=V((own, width), F32), xh1=V((rows, width), BF16),
         act=V((2, ipd, TALL, 3 * half), BF16), dsh=V((2, ipd, TALL, 3 * width), BF16),
-        wg=V((CH, taps, c.m2), BF16), wf=V((2, taps, width), BF16), wt=V((2, 9 * width, half), BF16),
+        wg=V((CH, taps, c.m2), BF16), wx=V((CH, width, cw), BF16), wf=V((2, taps, width), BF16), wt=V((2, 9 * width, half), BF16),
         sp=V((own, two), F32), slope2=V((own, two), F32), act2=V((own, two), F32), share=V((8, LANES), F32),
         gate_x=V((D * 8, LANES), F32), squeezed=V((D * 8, LANES), F32), gate_slope=V((D * 8, LANES), F32),
         grad_down=V((D * 8, LANES), F32), grad_summary=V((8, width), F32), att=V((8, two), F32),
@@ -1055,32 +1172,38 @@
         dst=V((2, width, own), BF16),
         eg=V((width, cw), F32), es=V((width, cw), piece_type), ebuf=V((DP, piece, cw), piece_type),
         eo=V((DP, piece, cw), piece_type), rg=V((cw, width), F32),
-        all_send=dma(6), all_recv=dma(6), col_send=dma(2), col_recv=dma(2),
+        all_send=dma(5), all_recv=dma(5), col_send=dma(3), col_recv=dma(3), row_send=dma(2), row_recv=dma(2),
         rs_core_send=dma(2), rs_core_recv=dma(2, X, ipd), rs_chip_send=dma(2), rs_chip_recv=dma(2, X, ipd),
-        ag_core_send=dma(4), ag_core_recv=dma(4, ipd), ag_chip_send=dma(4, X), ag_chip_recv=dma(4, X, ipd),
-        ag_pass_send=dma(4, X), ag_pass_recv=dma(4, X, ipd), par_send=dma(1), par_recv=dma(CH),
-        eg_send=dma(2), eg_recv=dma(2), rg_send=dma(3), rg_recv=dma(2), sg_send=dma(4), sg_recv=dma(4),
+        ag_core_send=dma(3), ag_core_recv=dma(3, ipd), ag_chip_send=dma(3, X), ag_chip_recv=dma(3, X, ipd),
+        ag_pass_send=dma(3, X), ag_pass_recv=dma(3, X, ipd), sh_core_send=dma(2), sh_core_recv=dma(2),
+        sh_chip_send=dma(2, X), sh_chip_recv=dma(2, X), sh_col_send=dma(2, X), sh_col_recv=dma(2, X, DP),
+        sh_pass_send=dma(2, X), sh_pass_recv=dma(2, X), par_send=dma(1), par_recv=dma(CH),
+        eg_send=dma(2), eg_recv=dma(2), rg_send=dma(3), rg_recv=dma(2), sg_send=dma(4, 3), sg_recv=dma(4, 3),
         load=dma(2 + 2 * X), store=dma(2),
     )
     for name, count in (
         ("stage", X), ("inward", X), ("outward", X - 1), ("landed", X - 1), ("inward2", X), ("landed2", X - 1)
     ):
         scratch[name] = V((count, ipd, CELLS, width), BF16)
-    for k in range(1, 7):
+    for k in range(1, 6):
         scratch[f"g{k}"] = V((D, 8, LANES), F32)
-    for k in range(1, 3):
-        scratch[f"c{k}"] = V((DP, 8, LANES), F32)
+    scratch["sums3"] = V((CH, 4, LANES), F32)
+    for k in range(1, 4):
+        scratch[f"c{k}"] = V((DP, 4, LANES), F32)
+    scratch["r1"] = V((CH, 4, LANES), F32)
+    scratch["r3"] = V((CH, 4, LANES), F32)
     if c.reduce_inside:
         scratch.update(
             rs=V((width, cw), piece_type), rbuf=V((DP, piece, cw), piece_type), rsum=V((piece, cw), piece_type),
-            rall=V((DP // CH, CH, piece, cw), piece_type), tall=V((LANES, CH * cw), F32),
+            rall=V((DP // CH, CH, piece, cw), piece_type),
         )
     if c.split_inside:
         slab = c.m2 // DP
         scratch.update(
-            ss=V((X, 2, c.m2, taps), BF16), sin=V((X, c.m2, taps), BF16), sc=V((X, c.m2, taps), BF16),
-            sp1=V((DP, X, slab, taps), BF16), sx=V((X, slab, taps), BF16), sxin=V((X, slab, taps), BF16),
-            so=V((DP, slab, taps), BF16),
+            ss=V((3, 2, X, c.m2, 3 * half), BF16), sin=V((3, X, c.m2, 3 * half), BF16),
+            sc=V((3, DP, X, slab, 3 * half), BF16), sp1=V((3, DP, X, slab, 3 * half), BF16),
+            sx=V((3, X, slab, 3 * half), BF16), sxin=V((3, X, slab, 3 * half), BF16),
+            so=V((3, DP, slab, 3 * half), BF16),
         )
     anywhere = pl.BlockSpec(memory_space=pl.ANY)
     vmem = pl.BlockSpec(memory_space=pltpu.VMEM)
@@ -1100,12 +1223,21 @@
         ),
         name="block",
     )(*[a[name] for name in ARGS])
+    results = pl.pallas_call(
+        hand_over,
+        out_shape=tuple(outs.values()),
+        in_specs=[anywhere] * len(outs),
+        out_specs=tuple(anywhere for _ in outs),
+        scratch_shapes=[V(v.shape, v.dtype) for v in outs.values()] + [dma(4 * len(outs), 2)],
+        compiler_params=pltpu.CompilerParams(vmem_limit_bytes=62 * 2**20),
+        name="results",
+    )(*results)
     o = dict(zip(outs, results))
     if not c.reduce_inside:
         place = lax.axis_index("chan")
         part = lax.psum(o["reduce_part"], "dp")
         part = lax.all_gather(part, "chan", axis=1, tiled=True)
-        o["reduce_grad"] = lax.dynamic_slice_in_dim(part, place * c.m1, c.m1, 0).T
+        o["reduce_grad"] = lax.dynamic_slice_in_dim(part, place * c.m1, c.m1, 0)
     if not c.split_inside:
         place = lax.axis_index("chan")
         part = lax.psum(o["split_part"], ("dp", "chan"))
@@ -1113,8 +1245,8 @@
         o["split_grad"] = part.T.reshape(9, half, c.m2)
     flat = lambda name: o[name].reshape(-1)
     return (
-        o["block_out"], o["inputs_grad"], o["reduce_grad"], flat("first_gain_grad"), flat("first_shift_grad"),
-        o["split_grad"], flat("second_gain_grad"), flat("second_shift_grad"), o["down_grad"],
+        o["block_out"], o["inputs_grad"], o["reduce_grad"].T, flat("first_gain_grad"), flat("first_shift_grad"),
+        o["split_grad"], flat("second_gain_grad"), flat("second_shift_grad"), o["down_grad"].T,
         flat("gate_gain_grad"), flat("gate_shift_grad"), o["up_grad"], flat("bias_grad"), o["expand_grad"],
         flat("third_gain_grad"), flat("third_shift_grad"),
     )

time: 168 us -> 142 us (0.85)
  local copies, waits for them, and re-layouts: 14.9 us -> 0 us
  Pallas kernels: 152 us -> 141 us
    pallas_call x1, Pallas kernels: 152 us -> 135 us  [per_device(): pl.pallas_call(functools.partial(kernel, c, names), out_shape=tuple(outs....]
    unnamed x42 -> x0, local copies, waits for them, and re-layouts: 14.9 us -> none
    pallas_call x0 -> x1, Pallas kernels: none -> 5.58 us  [per_device(): pl.pallas_call(hand_over, out_shape=tuple(outs.values()), in_specs=[anywh...]
where the time goes in v2:
time: 142 us
  Pallas kernels  141 us (99%)
    pallas_call x1, Pallas kernels, per_device(): pl.pallas_call(functools.partial(kernel, c, names), out_shape=tuple(outs....  135 us
    pallas_call x1, Pallas kernels, per_device(): pl.pallas_call(hand_over, out_shape=tuple(outs.values()), in_specs=[anywh...  5.58 us

profile of v2, /device:TPU:0, one launch (start us, length us, event | category | flops | bytes accessed | tf_op | source)
XLA Modules:
  0.0 141.6 jit_solution(14976488931685815851)
XLA Ops:
  0.7 135.3 %block.1 = (bf16[4096,256]{1,0:T(8,128)(2,1)}, bf16[4096,256]{1,0:T(8,128)(2,1)}, f32[1,64]{1,0:T(1,128)}, f32[1,64]{1,0:T(1,128)}, f32[1,128]{1,0:T(1,128)}, /*...) custom-call(bf16[4096,256]{1,0:T(8,128)(2,1)} %refs_0_.1, ...), custom_call_target="tpu_custom_call" | custom-call | tf_op jit(solution)/shard_map/block/pallas_call | solution.py:1215
  136.0 5.6 %results.1 = (bf16[4096,256]{1,0:T(8,128)(2,1)}, bf16[4096,256]{1,0:T(8,128)(2,1)}, f32[1,64]{1,0:T(1,128)}, f32[1,64]{1,0:T(1,128)}, f32[1,128]{1,0:T(1,128)}, ...) custom-call(bf16[4096,256]{1,0:T(8,128)(2,1)} %get-tuple-element.48., ...), custom_call_target="tpu_custom_call" | custom-call | tf_op jit(solution)/shard_map/results/pallas_call | solution.py:1226

commit v3 on v2

--- a/solution.py
+++ b/solution.py
@@ -137,6 +137,9 @@
     def everyone_wait(buf, k):
         drain(buf.at[pl.ds(1, D - 1)], r.all_recv.at[k])
 
+    def everyone_wait_on(buf, sem):
+        drain(buf.at[pl.ds(1, D - 1)], sem)
+
     def everyone_done(buf, k):
         drain(buf.at[pl.ds(1, D - 1)], r.all_send.at[k])
 
@@ -182,27 +185,38 @@
 
             loop(ipd, body)
 
+        def mate_one(self, t, i, part):
+            self.stage[t, i] = part(block_of(t, False), i).astype(BF16)
+            remote(
+                self.stage.at[t, i], self.inward.at[t, i],
+                r.rs_core_send.at[self.k], r.rs_core_recv.at[self.k, t, i], mate,
+            ).start()
+
         def to_mate(self, t, part):
-            def body(i):
-                self.stage[t, i] = part(block_of(t, False), i).astype(BF16)
-                remote(
-                    self.stage.at[t, i], self.inward.at[t, i],
-                    r.rs_core_send.at[self.k], r.rs_core_recv.at[self.k, t, i], mate,
-                ).start()
-
-            loop(ipd, body)
+            loop(ipd, lambda i: self.mate_one(t, i, part))
+
+        def peer_one(self, t, i, part):
+            value = part(block_of(t, True), i)
+            drain(self.inward.at[t, i], r.rs_core_recv.at[self.k, t, i])
+            self.outward[t - 1, i] = (value + self.inward[t, i].astype(F32)).astype(BF16)
+            remote(
+                self.outward.at[t - 1, i], self.landed.at[X - t - 1, i],
+                r.rs_chip_send.at[self.k], r.rs_chip_recv.at[self.k, X - t, i], peer(t),
+            ).start()
 
         def to_peer(self, t, part):
-            def body(i):
-                value = part(block_of(t, True), i)
-                drain(self.inward.at[t, i], r.rs_core_recv.at[self.k, t, i])
-                self.outward[t - 1, i] = (value + self.inward[t, i].astype(F32)).astype(BF16)
-                remote(
-                    self.outward.at[t - 1, i], self.landed.at[X - t - 1, i],
-                    r.rs_chip_send.at[self.k], r.rs_chip_recv.at[self.k, X - t, i], peer(t),
-                ).start()
-
-            loop(ipd, body)
+            loop(ipd, lambda i: self.peer_one(t, i, part))
+
+        def both(self, t, part):
+            self.mate_one(t, 0, part)
+
+            def body(i, carry):
+                self.mate_one(t, i, part)
+                self.peer_one(t, i - 1, part)
+                return carry
+
+            lax.fori_loop(1, ipd, body, 0)
+            self.peer_one(t, ipd - 1, part)
 
         def own(self, part):
             def body(i):
@@ -499,6 +513,7 @@
         put(r.g2, g * (width // LANES), total(state[g][0]))
         put(r.g2, (2 + g) * (width // LANES), total(state[g][1]))
     everyone(r.g2, 1)
+    loop(ipd // 2, gx.send)
 
     for g in range(2):
         for tap in range(9):
@@ -538,6 +553,8 @@
 
     loop(ipd, second_act)
     everyone(r.g3, 2)
+    lax.fori_loop(ipd // 2, ipd, lambda i, carry: (gx.send(i), carry)[1], 0)
+
 
     gate_rows = min(D * 8, 2 * LANES)
     gate_blocks = D * 8 // gate_rows
@@ -620,6 +637,43 @@
     r.acc[...] = jnp.zeros((16, cw), F32)
     row_sum(r.r1, 0, r.c1)
     column(r.c1, 0)
+
+    def slope_guess():
+        root = 3.0**0.5
+        points = []
+        for z in (-root, 0.0, root):
+            h = shift2 + z * gain2
+            s = sigmoid(h)
+            points.append(s + h * s - h * s * s)
+        low, mid, high = points
+        return (low + 4.0 * mid + high) * (1.0 / 6.0), (high - low) * (root / 6.0)
+
+    guess = slope_guess()
+
+    def slope_sums(i):
+        share = r.share[pl.ds(i, 1), :]
+        zero = jnp.zeros((8, LANES), F32)
+        n = width // LANES
+
+        def body(at, k, state):
+            new = []
+            for q in range(2 * n):
+                lanes = slice(q * LANES, (q + 1) * LANES)
+                slope = r.slope2[at, lanes]
+                new.append((state[q][0] + fold(slope), state[q][1] + fold(slope * r.sp[at, lanes])))
+            return tuple(new)
+
+        state = strips(i * CELLS, body, ((zero, zero),) * (2 * n))
+        for q in range(2 * n):
+            for stat in range(2):
+                row_at = (stat * n + q % n) * 8 + 4 * (q // n)
+                r.slopes[pl.ds(row_at + i, 1), :] = (
+                    total(state[q][stat]) * share - guess[stat][:, q * LANES : (q + 1) * LANES]
+                )
+
+    r.slopes[...] = jnp.zeros_like(r.slopes)
+    loop(ipd, slope_sums)
+    r.g5[0] = r.slopes[...].astype(BF16)
 
     def turn_own(j):
         r.mt[ch * ipd + j] = flip(r.merged[rows_of(ch, j), :])
@@ -666,7 +720,7 @@
             outputs(block_of(t, True), i)
 
         loop(ipd, outputs_peer)
-    lax.fori_loop(1, ipd, lambda i, carry: (gx.send(i), carry)[1], 0)
+    everyone(r.g5, 4)
     for t in range(1, X):
 
         def outputs_pass(i):
@@ -705,11 +759,9 @@
     rs1.done()
     rs2 = Scatter(1, r.stage, r.inward2, r.outward, r.landed2, r.dm)
     for t in range(1, X):
-        rs2.to_mate(t, part_merged)
-        rs2.to_peer(t, part_merged)
+        rs2.both(t, part_merged)
     rs2.to_mate(0, part_merged)
     rs2.own(part_merged)
-    gx.send(0)
 
     def grow(j):
         r.eg[...] += dot(r.mt[j], r.de[image(j), :])
@@ -726,25 +778,128 @@
     for d in range(1, DP):
         remote(r.es.at[piece_rows(d)], r.ebuf.at[DP - d], r.eg_send.at[0], r.eg_recv.at[0], across(d)).start()
 
-    r.g4[0] = jnp.zeros((8, LANES), F32)
+    r.told[...] = jnp.zeros((16, LANES), F32)
 
     def finish_merged(i):
         rs2.arrive(i)
 
         def body(at, k, state):
-            here = pl.ds(pl.multiple_of(k * STRIP, STRIP), STRIP)
+            here = pl.ds(pl.multiple_of(k * SIDE, SIDE), SIDE)
             value = r.dm[at, :] + rs2.extra(i, here, slice(None))
             r.dm[at, :] = value
-            return state + fold(value * (r.act2[at, 0:width] - r.act2[at, width:two]))
-
-        gap = total(strips(i * CELLS, body, zero8))
+            new = [state[0] + fold(value * (r.act2[at, 0:width] - r.act2[at, width:two]))]
+            for g in range(2):
+                lanes = slice(g * width, (g + 1) * width)
+                part = value * r.slope2[at, lanes]
+                new += [state[1 + 2 * g] + fold(part), state[2 + 2 * g] + fold(part * r.sp[at, lanes])]
+            return tuple(new)
+
+        gap, *parts = strips(i * CELLS, body, (zero8,) * 5, SIDE)
         att = r.att[pl.ds(i, 1), :]
-        grad = att[:, 0:width] * att[:, width:two] * gap
-        for q in range(width // LANES):
-            r.g4[0, pl.ds(4 * q + i, 1), :] = grad[:, q * LANES : (q + 1) * LANES]
+        grad = att[:, 0:width] * att[:, width:two] * total(gap)
+        n = width // LANES
+        for q in range(n):
+            r.told[pl.ds(4 * q + i, 1), :] = grad[:, q * LANES : (q + 1) * LANES]
+        for g in range(2):
+            for stat in range(2):
+                part = total(parts[2 * g + stat]) * att[:, g * width : (g + 1) * width]
+                for q in range(n):
+                    at = 8 + (2 * stat + g) * n + q
+                    r.told[at : at + 1, :] += part[:, q * LANES : (q + 1) * LANES]
 
     loop(ipd, finish_merged)
+    r.r4[0] = r.told[8:16, :]
+    row(r.r4, 2)
+    r.g4[0] = r.told[0:8, :]
     everyone(r.g4, 3)
+    row_sum(r.r4, 2, r.c4)
+    column(r.c4, 3)
+    everyone_wait(r.g5, 4)
+    everyone_wait(r.g4, 3)
+    up_gap = r.gate_up[:, 0:width] - r.gate_up[:, width:two]
+
+    def gate_back(n, state):
+        at = gate_block(n)
+        grad_lo, grad_hi = lower_upper(r.g4, n)
+        grad = exact_nt(grad_lo, up_gap[:, 0:LANES]) + exact_nt(grad_hi, up_gap[:, LANES:width])
+        grad = grad * r.gate_slope[at, :]
+        r.grad_down[at, :] = grad
+        return state[0] + total(grad), state[1] + total(grad * r.gate_x[at, :])
+
+    gate_shift_all, gate_gain_all = lax.fori_loop(0, gate_blocks, gate_back, (zero1, zero1))
+    lead = r.gate_gain[...] * gate_scale
+
+    def gate_norm_back(n, state):
+        at = gate_block(n)
+        grad = r.grad_down[at, :] - gate_shift_all * every - r.gate_x[at, :] * (gate_gain_all * every)
+        grad = jnp.where(valid, lead * grad, 0.0)
+        r.grad_down[at, :] = grad
+        summary = exact_nt(grad, r.gate_down[...])
+        slots = gate_rows // 8
+
+        @pl.when(n == 0)
+        def _():
+            r.grad_summary[...] = summary[0:8, :]
+
+        slopes = r.g5[pl.ds(n * slots, slots)].astype(F32)
+        new = []
+        for stat in range(2):
+            for p in range(width // LANES):
+                part = summary[:, p * LANES : (p + 1) * LANES]
+                part = (part + pltpu.roll(part, 4, 0)).reshape(slots, 8, LANES)
+                k = stat * (width // LANES) + p
+                new.append(state[k] + jnp.sum(part * slopes[:, 8 * k : 8 * k + 8, :], axis=0))
+        new.append(state[-1] + total(summary))
+        return tuple(new)
+
+    n_half = width // LANES
+    zero = jnp.zeros((8, LANES), F32)
+    *flats, summed = lax.fori_loop(
+        0, gate_blocks, gate_norm_back, (zero,) * (2 * n_half) + (jnp.zeros((1, width), F32),)
+    )
+    guess = slope_guess()
+    column_wait(r.c4, 3)
+    told = jnp.sum(r.c4[...], axis=0)
+
+    def second_sum(stat):
+        parts = []
+        for q in range(2 * n_half):
+            flat = flats[stat * n_half + q % n_half]
+            flat = total(flat[4 * (q // n_half) : 4 * (q // n_half) + 4, :])
+            at = 2 * n_half * stat + q
+            lanes = slice(q % n_half * LANES, (q % n_half + 1) * LANES)
+            flat = flat + guess[stat][:, q * LANES : (q + 1) * LANES] * summed[:, lanes]
+            parts.append(flat + told[at : at + 1, :])
+        return jnp.concatenate(parts, axis=1)
+
+    shift_grad2, gain_grad2 = second_sum(0), second_sum(1)
+    lead2, base2, slant2 = gain2 * scale2, shift_grad2 * inverse, gain_grad2 * inverse
+
+    def splits_back(i):
+        att = r.att[pl.ds(i, 1), :]
+        flat = r.grad_summary[pl.ds(i, 1), :] * wide(r.share[pl.ds(i, 1), :], width)
+
+        def body(at, k, carry):
+            there = pl.ds(pl.multiple_of((ch * ipd + i) * CELLS + k * STRIP, STRIP), STRIP)
+            put_at = pl.ds(pl.multiple_of(SIDE + k * STRIP, SIDE), STRIP)
+            mask = r.maskf[there, :]
+            for q in range(two // LANES):
+                g, p = q // n_half, q % n_half
+                lanes = slice(q * LANES, (q + 1) * LANES)
+                here = slice(p * LANES, (p + 1) * LANES)
+                d = (r.dm[at, here] * att[:, lanes] + flat[:, here]) * r.slope2[at, lanes]
+                d = mask * lead2[:, lanes] * (d - base2[:, lanes] - r.sp[at, lanes] * slant2[:, lanes])
+                r.act2[at, lanes] = d
+                before = jnp.where(not_first, pltpu.roll(d, 1, 0), 0.0)
+                after = jnp.where(not_last, pltpu.roll(d, STRIP - 1, 0), 0.0)
+                for n, value in enumerate((after, d, before)):
+                    start = n * width + p * LANES
+                    r.dsh[g, i, put_at, start : start + LANES] = value.astype(BF16)
+            return carry
+
+        strips(i * CELLS, body, 0)
+
+    loop(ipd, splits_back)
 
     drain(r.ebuf.at[pl.ds(1, DP - 1)], r.eg_recv.at[0])
     value = r.eg[piece_rows(0), :]
@@ -753,102 +908,6 @@
     r.eo[0] = value.astype(et)
     for d in range(1, DP):
         remote(r.eo.at[0], r.eo.at[DP - d], r.eg_send.at[1], r.eg_recv.at[1], across(d)).start()
-
-    everyone_wait(r.g4, 3)
-    up_gap = r.gate_up[:, 0:width] - r.gate_up[:, width:two]
-
-    def gate_back(n, state):
-        at = gate_block(n)
-        grad_lo, grad_hi = lower_upper(r.g4, n)
-        grad = exact_nt(grad_lo, up_gap[:, 0:LANES]) + exact_nt(grad_hi, up_gap[:, LANES:width])
-        grad = grad * r.gate_slope[at, :]
-        r.grad_down[at, :] = grad
-        return state[0] + total(grad), state[1] + total(grad * r.gate_x[at, :])
-
-    gate_shift_all, gate_gain_all = lax.fori_loop(0, gate_blocks, gate_back, (zero1, zero1))
-    lead = r.gate_gain[...] * gate_scale
-
-    def gate_norm_back(n):
-        at = gate_block(n)
-        grad = r.grad_down[at, :] - gate_shift_all * every - r.gate_x[at, :] * (gate_gain_all * every)
-        r.grad_down[at, :] = jnp.where(valid, lead * grad, 0.0)
-
-    loop(gate_blocks, gate_norm_back)
-    r.grad_summary[...] = exact_nt(r.grad_down[0:8, :], r.gate_down[...])
-
-    def second_back(i, state):
-        att = r.att[pl.ds(i, 1), :]
-        flat = r.grad_summary[pl.ds(i, 1), :] * wide(r.share[pl.ds(i, 1), :], width)
-
-        def body(at, k, state):
-            d = r.dm[at, :]
-            new = []
-            for g in range(2):
-                lanes = slice(g * width, (g + 1) * width)
-                value = (d * att[:, lanes] + flat) * r.slope2[at, lanes]
-                r.act2[at, lanes] = value
-                new.append((state[g][0] + fold(value), state[g][1] + fold(value * r.sp[at, lanes])))
-            return tuple(new)
-
-        return strips(i * CELLS, body, state, 16)
-
-    state = lax.fori_loop(0, ipd, second_back, ((zero8, zero8), (zero8, zero8)))
-    for g in range(2):
-        put(r.g5, g * (width // LANES), total(state[g][0]))
-        put(r.g5, (2 + g) * (width // LANES), total(state[g][1]))
-    everyone(r.g5, 4)
-
-    r.gate_gain_grad[...] = exact_nt(gate_gain_all, pickg)
-    r.gate_shift_grad[...] = exact_nt(gate_shift_all, pickg)
-
-    def gate_grads(n, state):
-        at = gate_block(n)
-        sum_lo, sum_hi = lower_upper(r.g3, n)
-        grad_lo, grad_hi = lower_upper(r.g4, n)
-        picked = exact_nt(r.grad_down[at, :], pickg)
-        down = jnp.concatenate([exact_tn(picked, sum_lo), exact_tn(picked, sum_hi)], axis=1)
-        squeezed = r.squeezed[at, :]
-        up = jnp.concatenate([exact_tn(squeezed, grad_lo), exact_tn(squeezed, grad_hi)], axis=1)
-        bias = jnp.concatenate([total(grad_lo), total(grad_hi)], axis=1)
-        return state[0] + down, state[1] + up, state[2] + bias
-
-    down, up, bias = lax.fori_loop(
-        0, gate_blocks, gate_grads,
-        (jnp.zeros((mg, width), F32), jnp.zeros((inner, width), F32), jnp.zeros((1, width), F32)),
-    )
-    r.down_grad[...] = down
-    r.up_grad[...] = exact_nt(jnp.concatenate([up, -up], axis=1), pick2)
-    r.bias_grad[...] = exact_nt(jnp.concatenate([bias, -bias], axis=1), pick2)
-
-    everyone_wait(r.g5, 4)
-    sums = jnp.sum(r.g5[...], axis=0)
-    shift_grad, gain_grad = get(sums, 0, two), get(sums, two // LANES, two)
-    r.second_gain_grad[...] = exact_nt(gain_grad, pick2)
-    r.second_shift_grad[...] = exact_nt(shift_grad, pick2)
-    lead2, base2, slant2 = gain2 * scale2, shift_grad * inverse, gain_grad * inverse
-
-    def splits_back(i):
-        def body(at, k, carry):
-            there = pl.ds(pl.multiple_of((ch * ipd + i) * CELLS + k * STRIP, STRIP), STRIP)
-            put_at = pl.ds(pl.multiple_of(SIDE + k * STRIP, SIDE), STRIP)
-            mask = r.maskf[there, :]
-            for q in range(two // LANES):
-                g, p = q // (width // LANES), q % (width // LANES)
-                lanes = slice(q * LANES, (q + 1) * LANES)
-                d = mask * lead2[:, lanes] * (
-                    r.act2[at, lanes] - base2[:, lanes] - r.sp[at, lanes] * slant2[:, lanes]
-                )
-                r.act2[at, lanes] = d
-                before = jnp.where(not_first, pltpu.roll(d, 1, 0), 0.0)
-                after = jnp.where(not_last, pltpu.roll(d, STRIP - 1, 0), 0.0)
-                for n, value in enumerate((after, d, before)):
-                    start = n * width + p * LANES
-                    r.dsh[g, i, put_at, start : start + LANES] = value.astype(BF16)
-            return carry
-
-        strips(i * CELLS, body, 0)
-
-    loop(ipd, splits_back)
 
     def first_back(i, state):
         out = []
@@ -863,13 +922,20 @@
         return tuple(out)
 
     zero_h = jnp.zeros((8, half), F32)
-    state = lax.fori_loop(0, ipd, first_back, ((zero_h, zero_h), (zero_h, zero_h)))
+    gd = Gather(2, lambda b, i: r.dh1.at[rows_of(b, i)], lambda b: r.dh1.at[block_rows(b)], ipd)
+
+    def first_back_send(i, state):
+        state = first_back(i, state)
+        gd.send(i)
+        return state
+
+    state = lax.fori_loop(0, ipd // 2, first_back_send, ((zero_h, zero_h), (zero_h, zero_h)))
+    state = lax.fori_loop(ipd // 2, ipd, first_back, state)
     for g in range(2):
-        r.r3[0, g : g + 1, :] = total(state[g][0])
-        r.r3[0, 2 + g : 3 + g, :] = total(state[g][1])
-    row(r.r3, 1)
-    gd = Gather(2, lambda b, i: r.dh1.at[rows_of(b, i)], lambda b: r.dh1.at[block_rows(b)], ipd)
-    loop(ipd, gd.send)
+        r.g6[0, g : g + 1, :] = total(state[g][0])
+        r.g6[0, 2 + g : 3 + g, :] = total(state[g][1])
+    everyone(r.g6, 5)
+    lax.fori_loop(ipd // 2, ipd, lambda i, carry: (gd.send(i), carry)[1], 0)
 
     def pass_x(i):
         for t in range(1, X):
@@ -896,48 +962,60 @@
                 r.split_part[g * width : (g + 1) * width, k * wide3 : (k + 1) * wide3] = value
         if c.split_inside:
             remote(r.ss.at[k, 1 - core], r.sin.at[k], r.sg_send.at[0, k], r.sg_recv.at[0, k], mate).start()
-    row_sum(r.r3, 1, r.c3)
-    column(r.c3, 2)
     slab = m2 // DP
-
-    def split_spread(k):
+    Z = DP // 2
+    turn, side = dp // 2, dp % 2
+
+    def ring(e):
+        return (((turn + e) % Z) * 2 + side, ch)
+
+    other = (dp + 1 - 2 * side, ch)
+
+    def split_cores(k):
         drain(r.sin.at[k], r.sg_recv.at[0, k])
         for t in range(X):
             value = (r.ss[k, core, t].astype(F32) + r.sin[k, t].astype(F32)).astype(BF16)
-            r.sc[k, :, t] = value.reshape(DP, slab, wide3)
-        for d in range(1, DP):
+            value = value.reshape(Z, 2, slab, wide3)
+            for p in range(2):
+                r.sc[k, p, :, t] = value[:, p]
+        remote(r.sc.at[k, 1 - side], r.sp1.at[k], r.sg_send.at[1, k], r.sg_recv.at[1, k], other).start()
+
+    def split_pairs(k):
+        drain(r.sp1.at[k], r.sg_recv.at[1, k])
+        r.sy[k] = (r.sc[k, side].astype(F32) + r.sp1[k].astype(F32)).astype(BF16)
+        for e in range(1, Z):
             remote(
-                r.sc.at[k, (dp + d) % DP], r.sp1.at[k, DP - d], r.sg_send.at[1, k], r.sg_recv.at[1, k], across(d)
+                r.sy.at[k, (turn + e) % Z], r.sz.at[k, Z - e], r.sg_send.at[2, k], r.sg_recv.at[2, k], ring(e)
             ).start()
 
     def split_chips(k):
-        drain(r.sp1.at[k, pl.ds(1, DP - 1)], r.sg_recv.at[1, k])
+        drain(r.sz.at[k, pl.ds(1, Z - 1)], r.sg_recv.at[2, k])
         for t in range(X):
             there = (chip + t) % X
-            value = r.sc[k, dp, there].astype(F32)
-            for d in range(1, DP):
-                value = value + r.sp1[k, d, there].astype(F32)
+            value = r.sy[k, turn, there].astype(F32)
+            for e in range(1, Z):
+                value = value + r.sz[k, e, there].astype(F32)
             r.sx[k, t] = value.astype(BF16)
             if t:
-                remote(r.sx.at[k, t], r.sxin.at[k, X - t], r.sg_send.at[2, k], r.sg_recv.at[2, k], peer(t)).start()
+                remote(r.sx.at[k, t], r.sxin.at[k, X - t], r.sg_send.at[3, k], r.sg_recv.at[3, k], peer(t)).start()
 
     def split_out(k):
-        drain(r.sxin.at[k, pl.ds(1, X - 1)], r.sg_recv.at[2, k])
+        drain(r.sxin.at[k, pl.ds(1, X - 1)], r.sg_recv.at[3, k])
         value = r.sx[k, 0].astype(F32)
         for t in range(1, X):
             value = value + r.sxin[k, t].astype(F32)
         r.so[k, 0] = value.astype(BF16)
         for d in range(1, DP):
-            remote(r.so.at[k, 0], r.so.at[k, DP - d], r.sg_send.at[3, k], r.sg_recv.at[3, k], across(d)).start()
+            remote(r.so.at[k, 0], r.so.at[k, DP - d], r.sg_send.at[4, k], r.sg_recv.at[4, k], across(d)).start()
 
     def split_step(step, k):
         if c.split_inside:
             step(k)
 
     for k in range(3):
-        split_step(split_spread, k)
-    column_wait(r.c3, 2)
-    sums = jnp.sum(r.c3[...], axis=0)
+        split_step(split_cores, k)
+    everyone_wait(r.g6, 5)
+    sums = jnp.sum(r.g6[...], axis=0)
     shift_grad, gain_grad = get(sums, 0, width), get(sums, 2, width)
     lead1, base1, slant1 = gain1 * scale1, shift_grad * inverse, gain_grad * inverse
 
@@ -973,8 +1051,7 @@
         reduced_back(block_of(0, False), i)
 
     loop(ipd, from_mate)
-    loop(ipd, lambda i: input_back(ch, i))
-    loop(ipd, lambda i: input_back(block_of(0, False), i))
+    split_step(split_pairs, 0)
     for t in range(1, X):
 
         def from_peer(i):
@@ -982,7 +1059,7 @@
             reduced_back(block_of(t, True), i)
 
         loop(ipd, from_peer)
-    split_step(split_chips, 0)
+    split_step(split_pairs, 1)
     for t in range(1, X):
 
         def from_pass(i):
@@ -997,10 +1074,13 @@
             remote(r.rs.at[piece_rows(d)], r.rbuf.at[DP - d], r.rg_send.at[0], r.rg_recv.at[0], across(d)).start()
     else:
         r.reduce_part[...] = r.rg[...].T
+    split_step(split_pairs, 2)
+    split_step(split_chips, 0)
+    loop(ipd, lambda i: input_back(ch, i))
     split_step(split_chips, 1)
-    for t in range(1, X):
-        loop(ipd, lambda i: input_back(block_of(t, True), i))
+    loop(ipd, lambda i: input_back(block_of(0, False), i))
     split_step(split_out, 0)
+    split_step(split_chips, 2)
     if c.reduce_inside:
         groups = DP // CH
         goal = dp // groups
@@ -1021,13 +1101,37 @@
         def _():
             remote(r.rsum, slot, r.rg_send.at[2], r.rg_recv.at[1], (dp, goal)).start()
 
-    split_step(split_chips, 2)
     split_step(split_out, 1)
     for t in range(1, X):
+        loop(ipd, lambda i: input_back(block_of(t, True), i))
+    split_step(split_out, 2)
+    for t in range(1, X):
         loop(ipd, lambda i: input_back(block_of(t, False), i))
+    r.second_gain_grad[...] = exact_nt(gain_grad2, pick2)
+    r.second_shift_grad[...] = exact_nt(shift_grad2, pick2)
     r.first_gain_grad[...] = exact_nt(gain_grad, pick1)
     r.first_shift_grad[...] = exact_nt(shift_grad, pick1)
-    split_step(split_out, 2)
+    r.gate_gain_grad[...] = exact_nt(gate_gain_all, pickg)
+    r.gate_shift_grad[...] = exact_nt(gate_shift_all, pickg)
+
+    def gate_grads(n, state):
+        at = gate_block(n)
+        sum_lo, sum_hi = lower_upper(r.g3, n)
+        grad_lo, grad_hi = lower_upper(r.g4, n)
+        picked = exact_nt(r.grad_down[at, :], pickg)
+        down = jnp.concatenate([exact_tn(picked, sum_lo), exact_tn(picked, sum_hi)], axis=1)
+        squeezed = r.squeezed[at, :]
+        up = jnp.concatenate([exact_tn(squeezed, grad_lo), exact_tn(squeezed, grad_hi)], axis=1)
+        bias = jnp.concatenate([total(grad_lo), total(grad_hi)], axis=1)
+        return state[0] + down, state[1] + up, state[2] + bias
+
+    down, up, bias = lax.fori_loop(
+        0, gate_blocks, gate_grads,
+        (jnp.zeros((mg, width), F32), jnp.zeros((inner, width), F32), jnp.zeros((1, width), F32)),
+    )
+    r.down_grad[...] = down
+    r.up_grad[...] = exact_nt(jnp.concatenate([up, -up], axis=1), pick2)
+    r.bias_grad[...] = exact_nt(jnp.concatenate([bias, -bias], axis=1), pick2)
 
     drain(r.eo.at[pl.ds(1, DP - 1)], r.eg_recv.at[1])
     for d in range(DP):
@@ -1039,7 +1143,7 @@
                 r.reduce_grad[s * piece : (s + 1) * piece, q * cw : (q + 1) * cw] = r.rall[s, q].astype(F32)
     if c.split_inside:
         for k in range(3):
-            drain(r.so.at[k, pl.ds(1, DP - 1)], r.sg_recv.at[3, k])
+            drain(r.so.at[k, pl.ds(1, DP - 1)], r.sg_recv.at[4, k])
             for p in range(3):
                 at = slice(p * half, (p + 1) * half)
                 block = jnp.concatenate(
@@ -1047,12 +1151,12 @@
                 )
                 r.split_grad[3 * k + p] = block.T
 
-    for k, buf in enumerate((r.g1, r.g2, r.g3, r.g4, r.g5)):
+    for k, buf in enumerate((r.g1, r.g2, r.g3, r.g4, r.g5, r.g6)):
         everyone_done(buf, k)
     column_done(r.c1, 0)
-    column_done(r.c3, 2)
     row_done(r.r1, 0)
-    row_done(r.r3, 1)
+    row_done(r.r4, 2)
+    column_done(r.c4, 3)
     column_done(r.c2, 1)
     rs2.done()
     for gather in (gm, gd) + shares:
@@ -1071,9 +1175,10 @@
     if c.split_inside:
         for k in range(3):
             drain(r.sin.at[k], r.sg_send.at[0, k])
-            drain(r.sp1.at[k, pl.ds(1, DP - 1)], r.sg_send.at[1, k])
-            drain(r.sxin.at[k, pl.ds(1, X - 1)], r.sg_send.at[2, k])
-            drain(r.so.at[k, pl.ds(1, DP - 1)], r.sg_send.at[3, k])
+            drain(r.sp1.at[k], r.sg_send.at[1, k])
+            drain(r.sz.at[k, pl.ds(1, Z - 1)], r.sg_send.at[2, k])
+            drain(r.sxin.at[k, pl.ds(1, X - 1)], r.sg_send.at[3, k])
+            drain(r.so.at[k, pl.ds(1, DP - 1)], r.sg_send.at[4, k])
     drain(r.cv, r.store.at[0])
     drain(r.xv, r.store.at[1])
 
@@ -1122,7 +1227,7 @@
     piece_type = BF16 if piece % 16 == 0 else F32
     c.reduce_inside = c.DP % c.CH == 0 and piece % 8 == 0
     c.share = taps % (16 * c.DP) == 0 and c.width % (16 * c.DP) == 0
-    c.split_inside = c.m2 % (16 * c.DP) == 0
+    c.split_inside = c.m2 % (16 * c.DP) == 0 and c.DP % 2 == 0 and c.DP > 2
     own = c.ipd * CELLS
     DP, CH, X, D, ipd, cw, width = c.DP, c.CH, c.X, c.D, c.ipd, c.cw, c.width
     for name in ARGS:
@@ -1172,26 +1277,31 @@
         dst=V((2, width, own), BF16),
         eg=V((width, cw), F32), es=V((width, cw), piece_type), ebuf=V((DP, piece, cw), piece_type),
         eo=V((DP, piece, cw), piece_type), rg=V((cw, width), F32),
-        all_send=dma(5), all_recv=dma(5), col_send=dma(3), col_recv=dma(3), row_send=dma(2), row_recv=dma(2),
+        all_send=dma(6), all_recv=dma(6), col_send=dma(4), col_recv=dma(4), row_send=dma(3), row_recv=dma(3),
         rs_core_send=dma(2), rs_core_recv=dma(2, X, ipd), rs_chip_send=dma(2), rs_chip_recv=dma(2, X, ipd),
         ag_core_send=dma(3), ag_core_recv=dma(3, ipd), ag_chip_send=dma(3, X), ag_chip_recv=dma(3, X, ipd),
         ag_pass_send=dma(3, X), ag_pass_recv=dma(3, X, ipd), sh_core_send=dma(2), sh_core_recv=dma(2),
         sh_chip_send=dma(2, X), sh_chip_recv=dma(2, X), sh_col_send=dma(2, X), sh_col_recv=dma(2, X, DP),
         sh_pass_send=dma(2, X), sh_pass_recv=dma(2, X), par_send=dma(1), par_recv=dma(CH),
-        eg_send=dma(2), eg_recv=dma(2), rg_send=dma(3), rg_recv=dma(2), sg_send=dma(4, 3), sg_recv=dma(4, 3),
+        eg_send=dma(2), eg_recv=dma(2), rg_send=dma(3), rg_recv=dma(2), sg_send=dma(5, 3), sg_recv=dma(5, 3),
         load=dma(2 + 2 * X), store=dma(2),
     )
     for name, count in (
         ("stage", X), ("inward", X), ("outward", X - 1), ("landed", X - 1), ("inward2", X), ("landed2", X - 1)
     ):
         scratch[name] = V((count, ipd, CELLS, width), BF16)
-    for k in range(1, 6):
+    for k in range(1, 5):
         scratch[f"g{k}"] = V((D, 8, LANES), F32)
+    scratch["r4"] = V((CH, 8, LANES), F32)
+    scratch["c4"] = V((DP, 8, LANES), F32)
+    scratch["g5"] = V((D, 16 * width // LANES, LANES), BF16)
+    scratch["told"] = V((16, LANES), F32)
+    scratch["slopes"] = V((16 * width // LANES, LANES), F32)
     scratch["sums3"] = V((CH, 4, LANES), F32)
-    for k in range(1, 4):
-        scratch[f"c{k}"] = V((DP, 4, LANES), F32)
+    scratch["c1"] = V((DP, 4, LANES), F32)
     scratch["r1"] = V((CH, 4, LANES), F32)
-    scratch["r3"] = V((CH, 4, LANES), F32)
+    scratch["c2"] = V((DP, 4, LANES), F32)
+    scratch["g6"] = V((D, 4, LANES), F32)
     if c.reduce_inside:
         scratch.update(
             rs=V((width, cw), piece_type), rbuf=V((DP, piece, cw), piece_type), rsum=V((piece, cw), piece_type),
@@ -1201,9 +1311,10 @@
         slab = c.m2 // DP
         scratch.update(
             ss=V((3, 2, X, c.m2, 3 * half), BF16), sin=V((3, X, c.m2, 3 * half), BF16),
-            sc=V((3, DP, X, slab, 3 * half), BF16), sp1=V((3, DP, X, slab, 3 * half), BF16),
+            sc=V((3, 2, c.DP // 2, X, slab, 3 * half), BF16), sp1=V((3, c.DP // 2, X, slab, 3 * half), BF16),
+            sy=V((3, c.DP // 2, X, slab, 3 * half), BF16), sz=V((3, c.DP // 2, X, slab, 3 * half), BF16),
             sx=V((3, X, slab, 3 * half), BF16), sxin=V((3, X, slab, 3 * half), BF16),
-            so=V((3, DP, slab, 3 * half), BF16),
+            so=V((3, c.DP, slab, 3 * half), BF16),
         )
     anywhere = pl.BlockSpec(memory_space=pl.ANY)
     vmem = pl.BlockSpec(memory_space=pltpu.VMEM)

time: 142 us -> 136 us (0.958)
  Pallas kernels: 141 us -> 136 us
    pallas_call x1, Pallas kernels: 135 us -> 130 us  [per_device(): pl.pallas_call(functools.partial(kernel, c, names), out_shape=tuple(outs....]
where the time goes in v3:
time: 136 us
  Pallas kernels  136 us (100%)
    pallas_call x1, Pallas kernels, per_device(): pl.pallas_call(functools.partial(kernel, c, names), out_shape=tuple(outs....  130 us
    pallas_call x1, Pallas kernels, per_device(): pl.pallas_call(hand_over, out_shape=tuple(outs.values()), in_specs=[anywh...  5.58 us

profile of v3, /device:TPU:0, one launch (start us, length us, event | category | flops | bytes accessed | tf_op | source)
XLA Modules:
  0.0 136.3 jit_solution(16779761737768299961)
XLA Ops:
  0.7 129.9 %block.1 = (bf16[4096,256]{1,0:T(8,128)(2,1)}, bf16[4096,256]{1,0:T(8,128)(2,1)}, f32[1,64]{1,0:T(1,128)}, f32[1,64]{1,0:T(1,128)}, f32[1,128]{1,0:T(1,128)}, /*...) custom-call(bf16[4096,256]{1,0:T(8,128)(2,1)} %refs_0_.1, ...), custom_call_target="tpu_custom_call" | custom-call | tf_op jit(solution)/shard_map/block/pallas_call | solution.py:1326
  130.6 5.6 %results.1 = (bf16[4096,256]{1,0:T(8,128)(2,1)}, bf16[4096,256]{1,0:T(8,128)(2,1)}, f32[1,64]{1,0:T(1,128)}, f32[1,64]{1,0:T(1,128)}, f32[1,128]{1,0:T(1,128)}, ...) custom-call(bf16[4096,256]{1,0:T(8,128)(2,1)} %get-tuple-element.48., ...), custom_call_target="tpu_custom_call" | custom-call | tf_op jit(solution)/shard_map/results/pallas_call | solution.py:1337

commit v4 on v3

--- a/solution.py
+++ b/solution.py
@@ -236,8 +236,9 @@
                 value = value + self.landed[t - 1, i, at, lanes].astype(F32)
             return value
 
-        def done(self):
-            drain(self.stage, r.rs_core_send.at[self.k])
+        def done(self, stage=True):
+            if stage:
+                drain(self.stage, r.rs_core_send.at[self.k])
             drain(self.outward, r.rs_chip_send.at[self.k])
 
     class Gather:
@@ -350,13 +351,12 @@
         mask = jnp.where(jnp.logical_and(spot_r < side, spot_c < side), 1.0, 0.0)
         r.area[pl.ds(j, 1), :] = jnp.full((1, LANES), side * side, jnp.int32).astype(F32)
         r.maskf[image(j), :] = mask
-        r.maskb[image(j), :] = mask.astype(BF16)
 
     loop(images, make_mask)
 
     def part_reduce(b, i):
         at = rows_of(b, i)
-        x = r.xv[at, :] * wide(r.maskb[at, :], cw)
+        x = r.xv[at, :] * wide(r.maskf[at, :].astype(BF16), cw)
         r.xv[at, :] = x
         return dot(x, r.wr[...])
 
@@ -495,20 +495,27 @@
         for q in range(CH // 2):
             r.wf[g, :, q * m2 : (q + 1) * m2] = r.wg[g * (CH // 2) + q]
 
-    def conv(i, state):
-        there = rows_of(ch, i)
+    def two_of(n):
+        return pl.ds(pl.multiple_of(n * 2 * CELLS, 2 * CELLS), 2 * CELLS)
+
+    def conv(n, state):
+        there = pl.ds(pl.multiple_of((ch * ipd + 2 * n) * CELLS, 2 * CELLS), 2 * CELLS)
         out = []
         for g in range(2):
             lanes = slice(g * width, (g + 1) * width)
             left = jnp.concatenate(
-                [r.act[g, i, k * SIDE : k * SIDE + CELLS, :] for k in range(3)], axis=1
+                [
+                    r.act[g, pl.ds(2 * n, 2), k * SIDE : k * SIDE + CELLS, :].reshape(2 * CELLS, 3 * half)
+                    for k in range(3)
+                ],
+                axis=1,
             )
             value = dot(left, r.wf[g]) * wide(r.maskf[there, :], width)
-            r.sp[image(i), lanes] = value
+            r.sp[two_of(n), lanes] = value
             out.append((state[g][0] + fold(value), state[g][1] + fold(value * value)))
         return tuple(out)
 
-    state = lax.fori_loop(0, ipd, conv, ((zero8, zero8), (zero8, zero8)))
+    state = lax.fori_loop(0, ipd // 2, conv, ((zero8, zero8), (zero8, zero8)))
     for g in range(2):
         put(r.g2, g * (width // LANES), total(state[g][0]))
         put(r.g2, (2 + g) * (width // LANES), total(state[g][1]))
@@ -553,7 +560,45 @@
 
     loop(ipd, second_act)
     everyone(r.g3, 2)
-    lax.fori_loop(ipd // 2, ipd, lambda i, carry: (gx.send(i), carry)[1], 0)
+
+    def slope_guess():
+        root = 3.0**0.5
+        points = []
+        for z in (-root, 0.0, root):
+            h = shift2 + z * gain2
+            s = sigmoid(h)
+            points.append(s + h * s - h * s * s)
+        low, mid, high = points
+        return (low + 4.0 * mid + high) * (1.0 / 6.0), (high - low) * (root / 6.0)
+
+    guess = slope_guess()
+
+    def slope_sums(i):
+        share = r.share[pl.ds(i, 1), :]
+        zero = jnp.zeros((8, LANES), F32)
+        n = width // LANES
+
+        def body(at, k, state):
+            new = []
+            for q in range(2 * n):
+                lanes = slice(q * LANES, (q + 1) * LANES)
+                slope = r.slope2[at, lanes]
+                new.append((state[q][0] + fold(slope), state[q][1] + fold(slope * r.sp[at, lanes])))
+            return tuple(new)
+
+        state = strips(i * CELLS, body, ((zero, zero),) * (2 * n))
+        for q in range(2 * n):
+            for stat in range(2):
+                row_at = (stat * n + q % n) * 8 + 4 * (q // n)
+                r.slopes[pl.ds(row_at + i, 1), :] = (
+                    total(state[q][stat]) * share - guess[stat][:, q * LANES : (q + 1) * LANES]
+                )
+
+    r.slopes[...] = jnp.zeros_like(r.slopes)
+    loop(ipd, slope_sums)
+    r.g5[0] = r.slopes[...].astype(BF16)
+
+    everyone(r.g5, 4)
 
 
     gate_rows = min(D * 8, 2 * LANES)
@@ -631,58 +676,35 @@
     zero_c = jnp.zeros((8, cw), F32)
     loop(CH, expand_sums)
     r.r1[0] = r.sums3[ch]
-    row(r.r1, 0, r.sums3)
+    row(r.r1, 1, r.sums3)
     lax.fori_loop(1, ipd, lambda i, carry: (gm.send(i), carry)[1], 0)
     load_c.wait()
     r.acc[...] = jnp.zeros((16, cw), F32)
-    row_sum(r.r1, 0, r.c1)
+    row_sum(r.r1, 1, r.c1)
     column(r.c1, 0)
 
-    def slope_guess():
-        root = 3.0**0.5
-        points = []
-        for z in (-root, 0.0, root):
-            h = shift2 + z * gain2
-            s = sigmoid(h)
-            points.append(s + h * s - h * s * s)
-        low, mid, high = points
-        return (low + 4.0 * mid + high) * (1.0 / 6.0), (high - low) * (root / 6.0)
-
-    guess = slope_guess()
-
-    def slope_sums(i):
-        share = r.share[pl.ds(i, 1), :]
-        zero = jnp.zeros((8, LANES), F32)
-        n = width // LANES
-
-        def body(at, k, state):
-            new = []
-            for q in range(2 * n):
-                lanes = slice(q * LANES, (q + 1) * LANES)
-                slope = r.slope2[at, lanes]
-                new.append((state[q][0] + fold(slope), state[q][1] + fold(slope * r.sp[at, lanes])))
-            return tuple(new)
-
-        state = strips(i * CELLS, body, ((zero, zero),) * (2 * n))
-        for q in range(2 * n):
-            for stat in range(2):
-                row_at = (stat * n + q % n) * 8 + 4 * (q // n)
-                r.slopes[pl.ds(row_at + i, 1), :] = (
-                    total(state[q][stat]) * share - guess[stat][:, q * LANES : (q + 1) * LANES]
-                )
-
-    r.slopes[...] = jnp.zeros_like(r.slopes)
-    loop(ipd, slope_sums)
-    r.g5[0] = r.slopes[...].astype(BF16)
-
+    for t in range(1, X):
+        loop(2, lambda i: gm.from_peer(t, i))
     def turn_own(j):
-        r.mt[ch * ipd + j] = flip(r.merged[rows_of(ch, j), :])
+        r.mt[:, rows_of(ch, j)] = flip(r.merged[rows_of(ch, j), :])
 
     loop(ipd, turn_own)
+
+    def turn_w(k):
+        r.wxt[k] = flip(r.wx[k])
+
+    loop(CH, turn_w)
     column_wait(r.c1, 0)
     sums = jnp.sum(r.c1[...], axis=0)
     mean3, scale3 = moments(get(sums, 0, cw), get(sums, cw // LANES, cw))
     gain3, shift3 = r.third_gain[...], r.third_shift[...]
+    lead3 = gain3 * scale3
+    lift3 = shift3 - mean3 * lead3
+    per3 = cw // LANES
+    put(r.r2, 0, lead3 * scale3)
+    put(r.r2, per3, lead3)
+    put(r.r2, 2 * per3, lead3 * scale3 * mean3)
+    row(r.r2, 0)
 
     def outputs(b, i):
         r.ex[rows_of(b, i), :] = dot(r.merged[rows_of(b, i), :], r.expand_weight[...])
@@ -690,15 +712,15 @@
         def body(at, k, state):
             shift, cross = state
             mask = wide(r.maskf[at, :], cw)
-            xh = (r.ex[at, :] - mean3) * scale3
-            h = gain3 * xh + shift3 + r.xv[at, :].astype(F32)
+            x = r.ex[at, :]
+            h = lead3 * x + lift3 + r.xv[at, :].astype(F32)
             s = sigmoid(h)
             y = h * s
             d = r.cv[at, :].astype(F32) * mask * (s + y - y * s)
             r.cv[at, :] = (mask * y).astype(BF16)
             r.dpre[at, :] = d
-            r.ex[at, :] = xh
-            return (shift + fold(d), cross + fold(d * xh))
+            r.de[at, :] = (lead3 * d).astype(BF16)
+            return (shift + fold(d), cross + fold(d * x))
 
         shift, cross = strips((b * ipd + i) * CELLS, body, (zero_c, zero_c))
         r.acc[0:8, :] += shift
@@ -706,77 +728,77 @@
         at = rows_of(b, i)
         pltpu.make_async_copy(r.cv.at[at], r.block_out.at[at], r.store.at[0]).start()
 
-    loop(ipd, lambda i: outputs(ch, i))
-
-    def outputs_mate(i):
+    def part_merged(b, i):
+        return dot(r.de[rows_of(b, i), :], r.wet[...])
+
+    rs1.done()
+    rs2 = Scatter(1, r.stage, r.inward2, r.outward, r.landed2, r.dm)
+    for t in range(1, X):
+
+        def far(i, ahead):
+            gm.from_pass(t, i)
+            outputs(block_of(t, False), i)
+            rs2.mate_one(t, i, part_merged)
+            outputs(block_of(t, True), i)
+            if ahead:
+                gm.from_peer(t, i + 2)
+            rs2.peer_one(t, i, part_merged)
+
+        loop(ipd - 2, lambda i: far(i, True))
+        lax.fori_loop(ipd - 2, ipd, lambda i, carry: (far(i, False), carry)[1], 0)
+
+    def near(i):
         gm.from_mate(i)
         outputs(block_of(0, False), i)
-
-    loop(ipd, outputs_mate)
-    for t in range(1, X):
-
-        def outputs_peer(i):
-            gm.from_peer(t, i)
-            outputs(block_of(t, True), i)
-
-        loop(ipd, outputs_peer)
-    everyone(r.g5, 4)
-    for t in range(1, X):
-
-        def outputs_pass(i):
-            gm.from_pass(t, i)
-            outputs(block_of(t, False), i)
-
-        loop(ipd, outputs_pass)
-    put(r.c2, 0, total(r.acc[0:8, :]))
-    put(r.c2, cw // LANES, total(r.acc[8:16, :]))
-    column(r.c2, 1)
+        rs2.mate_one(0, i, part_merged)
+
+    loop(ipd, near)
+    loop(ipd, lambda i: outputs(ch, i))
+    shift = total(r.acc[0:8, :])
+    put(r.c2, 0, shift)
+    put(r.c2, cw // LANES, (total(r.acc[8:16, :]) - mean3 * shift) * scale3)
+    everyone(r.c2, 6)
+    rs2.own(part_merged)
 
     def turn_other(j):
         b = j // ipd
         b = jnp.where(b < ch, b, b + 1)
         at = b * ipd + j % ipd
-        r.mt[at] = flip(r.merged[image(at), :])
+        r.mt[:, image(at)] = flip(r.merged[image(at), :])
 
     loop(images - ipd, turn_other)
-    column_wait(r.c2, 1)
-    sums = jnp.sum(r.c2[...], axis=0)
+    everyone_wait(r.c2, 6)
+    drain(r.r2.at[pl.ds(1, CH - 1)], r.row_recv.at[0])
+    r.back3[...] = jnp.sum(r.c2[...].reshape(DP, CH, 4, LANES), axis=0)
+    sums = r.back3[0]
     shift_grad, gain_grad = get(sums, 0, cw), get(sums, cw // LANES, cw)
     r.third_gain_grad[...] = gain_grad
     r.third_shift_grad[...] = shift_grad
-    lead3, base3, slant3 = gain3 * scale3, shift_grad * inverse, gain_grad * inverse
-
-    def part_merged(b, i):
-        def body(at, k, carry):
-            mask = wide(r.maskf[at, :], cw)
-            d = mask * lead3 * (r.dpre[at, :] - base3 - r.ex[at, :] * slant3)
-            r.de[at, :] = d.astype(BF16)
-            return carry
-
-        strips((b * ipd + i) * CELLS, body, 0)
-        return dot(r.de[rows_of(b, i), :], r.wet[...])
-
-    rs1.done()
-    rs2 = Scatter(1, r.stage, r.inward2, r.outward, r.landed2, r.dm)
-    for t in range(1, X):
-        rs2.both(t, part_merged)
-    rs2.to_mate(0, part_merged)
-    rs2.own(part_merged)
-
-    def grow(j):
-        r.eg[...] += dot(r.mt[j], r.de[image(j), :])
-
-    r.eg[...] = dot(r.mt[0], r.de[image(0), :])
-    lax.fori_loop(1, images, lambda j, carry: (grow(j), carry)[1], 0)
-    piece = width // DP
-    et = r.es.dtype
-    r.es[...] = r.eg[...].astype(et)
-
-    def piece_rows(d):
-        return pl.ds(pl.multiple_of(((dp + d) % DP) * piece, piece), piece)
-
-    for d in range(1, DP):
-        remote(r.es.at[piece_rows(d)], r.ebuf.at[DP - d], r.eg_send.at[0], r.eg_recv.at[0], across(d)).start()
+    base3, slant3 = shift_grad * inverse, gain_grad * inverse
+    slope3 = lead3 * scale3 * slant3
+    flat3 = lead3 * base3 - mean3 * slope3
+
+    r.mix[...] = jnp.zeros((width, width), F32)
+    r.offset[...] = jnp.zeros((16, width), F32)
+
+    def mix(q):
+        b = (ch + q) % CH
+        coefs, part = r.r2[q], r.back3[q]
+        base, slant = get(part, 0, cw) * inverse, get(part, per3, cw) * inverse
+        slope = get(coefs, 0, cw) * slant
+        flat = get(coefs, per3, cw) * base - get(coefs, 2 * per3, cw) * slant
+        r.mix[...] += dot((r.wx[b].astype(F32) * slope).astype(BF16), r.wxt[b])
+        high = flat.astype(BF16)
+        low = (flat - high.astype(F32)).astype(BF16)
+        pair = jnp.concatenate([high, low, jnp.zeros((14, cw), BF16)], axis=0)
+        r.offset[...] += dot(pair, r.wxt[b])
+
+    loop(CH, mix)
+    r.mixb[...] = r.mix[...].astype(BF16)
+
+    offset = total(r.offset[...])
+    away = offset + dot(r.merged[block_rows(ch), :], r.mixb[...])
+    r.inward[0] = away.astype(BF16).reshape(ipd, CELLS, width)
 
     r.told[...] = jnp.zeros((16, LANES), F32)
 
@@ -785,7 +807,9 @@
 
         def body(at, k, state):
             here = pl.ds(pl.multiple_of(k * SIDE, SIDE), SIDE)
-            value = r.dm[at, :] + rs2.extra(i, here, slice(None))
+            there = pl.ds(pl.multiple_of((ch * ipd + i) * CELLS + k * SIDE, SIDE), SIDE)
+            away = wide(r.maskf[there, :], width) * r.inward[0, i, here, :].astype(F32)
+            value = r.dm[at, :] + rs2.extra(i, here, slice(None)) - away
             r.dm[at, :] = value
             new = [state[0] + fold(value * (r.act2[at, 0:width] - r.act2[at, width:two]))]
             for g in range(2):
@@ -812,8 +836,34 @@
     row(r.r4, 2)
     r.g4[0] = r.told[0:8, :]
     everyone(r.g4, 3)
+    lax.fori_loop(ipd // 2, ipd, lambda i, carry: (gx.send(i), carry)[1], 0)
     row_sum(r.r4, 2, r.c4)
     column(r.c4, 3)
+
+    piece = width // DP
+    et = r.es.dtype
+    def piece_rows(d):
+        return pl.ds(pl.multiple_of(((dp + d) % DP) * piece, piece), piece)
+
+    def grow(b):
+        def body(at, k, carry):
+            mask = wide(r.maskf[at, :], cw)
+            d = lead3 * r.dpre[at, :] - mask * (flat3 + r.ex[at, :] * slope3)
+            r.de[at, :] = d.astype(BF16)
+            return carry
+
+        for i in range(ipd):
+            strips((b * ipd + i) * CELLS, body, 0)
+        value = dot(r.mt[:, block_rows(b)], r.de[block_rows(b), :])
+        r.eg[...] += value
+
+    r.eg[...] = jnp.zeros((width, cw), F32)
+    loop(CH, grow)
+    r.es[...] = r.eg[...].astype(et)
+
+    for d in range(1, DP):
+        remote(r.es.at[piece_rows(d)], r.ebuf.at[DP - d], r.eg_send.at[0], r.eg_recv.at[0], across(d)).start()
+
     everyone_wait(r.g5, 4)
     everyone_wait(r.g4, 3)
     up_gap = r.gate_up[:, 0:width] - r.gate_up[:, width:two]
@@ -909,33 +959,35 @@
     for d in range(1, DP):
         remote(r.eo.at[0], r.eo.at[DP - d], r.eg_send.at[1], r.eg_recv.at[1], across(d)).start()
 
-    def first_back(i, state):
+    def first_back(n, state):
+        there = pl.ds(pl.multiple_of((ch * ipd + 2 * n) * CELLS, 2 * CELLS), 2 * CELLS)
         out = []
         for g in range(2):
             lanes = slice(g * half, (g + 1) * half)
             left = jnp.concatenate(
-                [r.dsh[g, i, (2 - k) * SIDE : (2 - k) * SIDE + CELLS, :] for k in range(3)], axis=1
+                [
+                    r.dsh[g, pl.ds(2 * n, 2), (2 - k) * SIDE : (2 - k) * SIDE + CELLS, :].reshape(2 * CELLS, 3 * width)
+                    for k in range(3)
+                ],
+                axis=1,
             )
-            value = dot(left, r.wt[g]) * r.slope1[image(i), lanes]
-            r.dh1[rows_of(ch, i), lanes] = value.astype(BF16)
-            out.append((state[g][0] + fold(value), state[g][1] + fold(value * r.red[image(i), lanes])))
+            value = dot(left, r.wt[g]) * r.slope1[two_of(n), lanes]
+            r.dh1[there, lanes] = value.astype(BF16)
+            out.append((state[g][0] + fold(value), state[g][1] + fold(value * r.red[two_of(n), lanes])))
         return tuple(out)
 
     zero_h = jnp.zeros((8, half), F32)
     gd = Gather(2, lambda b, i: r.dh1.at[rows_of(b, i)], lambda b: r.dh1.at[block_rows(b)], ipd)
-
-    def first_back_send(i, state):
-        state = first_back(i, state)
-        gd.send(i)
-        return state
-
-    state = lax.fori_loop(0, ipd // 2, first_back_send, ((zero_h, zero_h), (zero_h, zero_h)))
-    state = lax.fori_loop(ipd // 2, ipd, first_back, state)
+    state = ((zero_h, zero_h), (zero_h, zero_h))
+    for n in range(ipd // 2):
+        state = first_back(n, state)
+        if n == 0:
+            loop(2, gd.send)
     for g in range(2):
         r.g6[0, g : g + 1, :] = total(state[g][0])
         r.g6[0, 2 + g : 3 + g, :] = total(state[g][1])
     everyone(r.g6, 5)
-    lax.fori_loop(ipd // 2, ipd, lambda i, carry: (gd.send(i), carry)[1], 0)
+    lax.fori_loop(2, ipd, lambda i, carry: (gd.send(i), carry)[1], 0)
 
     def pass_x(i):
         for t in range(1, X):
@@ -943,9 +995,11 @@
 
     loop(ipd, pass_x)
 
+    drain(r.stage, r.rs_core_send.at[1])
+
     def turn_d(i):
         for g in range(2):
-            r.dst[g, :, image(i)] = r.act2[image(i), g * width : (g + 1) * width].T.astype(BF16)
+            r.stage[g, i] = r.act2[image(i), g * width : (g + 1) * width].T.astype(BF16)
 
     loop(ipd, turn_d)
     per = CH // 2
@@ -953,7 +1007,7 @@
     for k in range(3):
         for g in range(2):
             right = r.act[g, :, k * SIDE : k * SIDE + CELLS, :].reshape(own_rows, wide3)
-            value = dot(r.dst[g], right)
+            value = dot(jnp.concatenate([r.stage[g, i] for i in range(ipd)], axis=1), right)
             if c.split_inside:
                 for q in range(per):
                     b = g * per + q
@@ -1151,14 +1205,14 @@
                 )
                 r.split_grad[3 * k + p] = block.T
 
-    for k, buf in enumerate((r.g1, r.g2, r.g3, r.g4, r.g5, r.g6)):
+    for k, buf in enumerate((r.g1, r.g2, r.g3, r.g4, r.g5, r.g6, r.c2)):
         everyone_done(buf, k)
     column_done(r.c1, 0)
-    row_done(r.r1, 0)
+    row_done(r.r1, 1)
+    row_done(r.r2, 0)
     row_done(r.r4, 2)
     column_done(r.c4, 3)
-    column_done(r.c2, 1)
-    rs2.done()
+    rs2.done(False)
     for gather in (gm, gd) + shares:
         gather.done()
     drain(r.pbuf.at[pl.ds(1, CH - 1)], r.par_send.at[0])
@@ -1263,8 +1317,8 @@
     dma = lambda *shape: pltpu.SemaphoreType.DMA(shape)
     scratch = dict(
         xv=V((rows, cw), BF16), cv=V((rows, cw), BF16), wr=V((cw, width), BF16), wrt=V((width, cw), BF16),
-        wet=V((cw, width), BF16), xt=V((c.images, cw, CELLS), BF16), mt=V((c.images, width, CELLS), BF16),
-        maskf=V((rows, LANES), F32), area=V((c.images, LANES), F32), maskb=V((rows, LANES), BF16), pbuf=V((CH, 8, two), F32),
+        wet=V((cw, width), BF16), xt=V((c.images, cw, CELLS), BF16), mt=V((width, rows), BF16),
+        maskf=V((rows, LANES), F32), area=V((c.images, LANES), F32), pbuf=V((CH, 8, two), F32),
         red=V((own, width), F32), slope1=V((own, width), F32), xh1=V((rows, width), BF16),
         act=V((2, ipd, TALL, 3 * half), BF16), dsh=V((2, ipd, TALL, 3 * width), BF16),
         wg=V((CH, taps, c.m2), BF16), wx=V((CH, width, cw), BF16), wf=V((2, taps, width), BF16), wt=V((2, 9 * width, half), BF16),
@@ -1274,10 +1328,9 @@
         merged=V((rows, width), BF16), ex=V((rows, cw), F32), acc=V((16, cw), F32),
         dpre=V((rows, cw), F32), de=V((rows, cw), BF16), dm=V((own, width), F32), dh1=V((rows, width), BF16),
 
-        dst=V((2, width, own), BF16),
         eg=V((width, cw), F32), es=V((width, cw), piece_type), ebuf=V((DP, piece, cw), piece_type),
         eo=V((DP, piece, cw), piece_type), rg=V((cw, width), F32),
-        all_send=dma(6), all_recv=dma(6), col_send=dma(4), col_recv=dma(4), row_send=dma(3), row_recv=dma(3),
+        all_send=dma(7), all_recv=dma(7), col_send=dma(4), col_recv=dma(4), row_send=dma(3), row_recv=dma(3),
         rs_core_send=dma(2), rs_core_recv=dma(2, X, ipd), rs_chip_send=dma(2), rs_chip_recv=dma(2, X, ipd),
         ag_core_send=dma(3), ag_core_recv=dma(3, ipd), ag_chip_send=dma(3, X), ag_chip_recv=dma(3, X, ipd),
         ag_pass_send=dma(3, X), ag_pass_recv=dma(3, X, ipd), sh_core_send=dma(2), sh_core_recv=dma(2),
@@ -1297,10 +1350,16 @@
     scratch["g5"] = V((D, 16 * width // LANES, LANES), BF16)
     scratch["told"] = V((16, LANES), F32)
     scratch["slopes"] = V((16 * width // LANES, LANES), F32)
+    scratch["back3"] = V((CH, 4, LANES), F32)
     scratch["sums3"] = V((CH, 4, LANES), F32)
     scratch["c1"] = V((DP, 4, LANES), F32)
     scratch["r1"] = V((CH, 4, LANES), F32)
-    scratch["c2"] = V((DP, 4, LANES), F32)
+    scratch["r2"] = V((CH, 8, LANES), F32)
+    scratch["mix"] = V((width, width), F32)
+    scratch["mixb"] = V((width, width), BF16)
+    scratch["offset"] = V((16, width), F32)
+    scratch["wxt"] = V((CH, cw, width), BF16)
+    scratch["c2"] = V((D, 4, LANES), F32)
     scratch["g6"] = V((D, 4, LANES), F32)
     if c.reduce_inside:
         scratch.update(

time: 136 us -> 133 us (0.978)
  Pallas kernels: 136 us -> 132 us
    pallas_call x1, Pallas kernels: 130 us -> 126 us  [per_device(): pl.pallas_call(functools.partial(kernel, c, names), out_shape=tuple(outs....]
where the time goes in v4:
time: 133 us
  Pallas kernels  132 us (99%)
    pallas_call x1, Pallas kernels, per_device(): pl.pallas_call(functools.partial(kernel, c, names), out_shape=tuple(outs....  126 us
    pallas_call x1, Pallas kernels, per_device(): pl.pallas_call(hand_over, out_shape=tuple(outs.values()), in_specs=[anywh...  5.58 us

profile of v4, /device:TPU:0, one launch (start us, length us, event | category | flops | bytes accessed | tf_op | source)
XLA Modules:
  0.0 132.8 jit_solution(6337278044073610676)
XLA Ops:
  0.7 126.4 %block.1 = (bf16[4096,256]{1,0:T(8,128)(2,1)}, bf16[4096,256]{1,0:T(8,128)(2,1)}, f32[1,64]{1,0:T(1,128)}, f32[1,64]{1,0:T(1,128)}, f32[1,128]{1,0:T(1,128)}, /*...) custom-call(bf16[4096,256]{1,0:T(8,128)(2,1)} %refs_0_.1, ...), custom_call_target="tpu_custom_call" | custom-call | tf_op jit(solution)/shard_map/block/pallas_call | solution.py:1385
  127.1 5.6 %results.1 = (bf16[4096,256]{1,0:T(8,128)(2,1)}, bf16[4096,256]{1,0:T(8,128)(2,1)}, f32[1,64]{1,0:T(1,128)}, f32[1,64]{1,0:T(1,128)}, f32[1,128]{1,0:T(1,128)}, ...) custom-call(bf16[4096,256]{1,0:T(8,128)(2,1)} %get-tuple-element.48., ...), custom_call_target="tpu_custom_call" | custom-call | tf_op jit(solution)/shard_map/results/pallas_call | solution.py:1396

commit v5 on v4

--- a/solution.py
+++ b/solution.py
@@ -401,6 +401,13 @@
     for q in range(1, CH):
         remote(r.pbuf.at[0], r.pbuf.at[CH - q], r.par_send.at[0], r.par_recv.at[CH - q], (dp, (ch + q) % CH)).start()
 
+    pixels = lax.fori_loop(
+        0, ipd, lambda i, count: count + r.area[pl.ds(ch * ipd + i, 1), :], jnp.zeros((1, LANES), F32)
+    )
+    r.g0[0] = jnp.zeros((4, LANES), F32)
+    r.g0[0, 0:1, :] = pixels
+    everyone(r.g0, 7)
+
     r.wrt[...] = flip(r.wr[...])
     r.wet[...] = flip(r.expand_weight[...])
 
@@ -429,19 +436,15 @@
     zero8 = jnp.zeros((8, width), F32)
     first, second = lax.fori_loop(0, ipd, finish_reduce, (zero8, zero8))
 
-    pixels = lax.fori_loop(
-        0, ipd, lambda i, count: count + r.area[pl.ds(ch * ipd + i, 1), :], jnp.zeros((1, LANES), F32)
-    )
-    r.g1[0] = jnp.zeros((8, LANES), F32)
     put(r.g1, 0, total(first))
     put(r.g1, width // LANES, total(second))
-    r.g1[0, 6:7, :] = pixels
     everyone(r.g1, 0)
     for share in shares:
         share.hand()
     everyone_wait(r.g1, 0)
     sums = jnp.sum(r.g1[...], axis=0)
-    count = sums[6:7, 0:1]
+    everyone_wait(r.g0, 7)
+    count = jnp.sum(r.g0[...], axis=0)[0:1, 0:1]
     inverse = 1.0 / count
     params = r.pbuf[0]
     for q in range(1, CH):
@@ -648,30 +651,43 @@
 
     gm = Gather(1, lambda b, i: r.merged.at[rows_of(b, i)], lambda b: r.merged.at[block_rows(b)], ipd)
 
-    def merge(i):
+    def merge(i, state):
         att = r.att[pl.ds(i, 1), :]
 
         def body(at, k, carry):
             there = pl.ds(pl.multiple_of((ch * ipd + i) * CELLS + k * STRIP, STRIP), STRIP)
             left = (r.act2[at, 0:width] * att[:, 0:width]).astype(BF16)
             right = (r.act2[at, width:two] * att[:, width:two]).astype(BF16)
-            r.merged[there, :] = (left.astype(F32) + right.astype(F32)).astype(BF16)
-            return carry
-
-        strips(i * CELLS, body, 0)
-
-    merge(0)
+            both = (left.astype(F32) + right.astype(F32)).astype(BF16)
+            r.merged[there, :] = both
+            return carry + fold(both.astype(F32))
+
+        return strips(i * CELLS, body, state)
+
+    merged_sum = merge(0, zero8)
     gm.send(0)
-    lax.fori_loop(1, ipd, lambda i, carry: (merge(i), carry)[1], 0)
+    merged_sum = lax.fori_loop(1, ipd, merge, merged_sum)
+
+    def turn_own(j):
+        r.mt[:, rows_of(ch, j)] = flip(r.merged[rows_of(ch, j), :])
+
+    loop(ipd, turn_own)
+
+    def halves(value):
+        high = value.astype(BF16)
+        return high, (value - high.astype(F32)).astype(BF16)
+
+    gram = dot(r.mt[:, block_rows(ch)], r.merged[block_rows(ch), :])
+    gram_high, gram_low = halves(gram)
+    high, rest = halves(total(merged_sum))
+    low, last = halves(total(merged_sum) - high.astype(F32))
+    means = jnp.concatenate([high, low, last, jnp.zeros((13, width), BF16)], axis=0)
 
     def expand_sums(k):
-        def body(i, state):
-            value = dot(r.merged[rows_of(ch, i), :], r.wx[k])
-            return (state[0] + fold(value), state[1] + fold(value * value))
-
-        first, second = lax.fori_loop(0, ipd, body, (zero_c, zero_c))
-        put(r.sums3.at[pl.ds(k, 1)], 0, total(first))
-        put(r.sums3.at[pl.ds(k, 1)], cw // LANES, total(second))
+        weight = r.wx[k]
+        square = dot(gram_high, weight) + dot(gram_low, weight)
+        put(r.sums3.at[pl.ds(k, 1)], 0, total(dot(means, weight)))
+        put(r.sums3.at[pl.ds(k, 1)], cw // LANES, total(fold(square * weight.astype(F32))))
 
     zero_c = jnp.zeros((8, cw), F32)
     loop(CH, expand_sums)
@@ -685,15 +701,14 @@
 
     for t in range(1, X):
         loop(2, lambda i: gm.from_peer(t, i))
-    def turn_own(j):
-        r.mt[:, rows_of(ch, j)] = flip(r.merged[rows_of(ch, j), :])
-
-    loop(ipd, turn_own)
-
     def turn_w(k):
         r.wxt[k] = flip(r.wx[k])
 
     loop(CH, turn_w)
+    for p in range(width // LANES):
+        at = slice(p * LANES, (p + 1) * LANES)
+        r.gapt[at, :] = (r.gate_up[:, at] - r.gate_up[:, width + p * LANES : width + (p + 1) * LANES]).T
+        r.downt[:, at] = r.gate_down[at, :].T
     column_wait(r.c1, 0)
     sums = jnp.sum(r.c1[...], axis=0)
     mean3, scale3 = moments(get(sums, 0, cw), get(sums, cw // LANES, cw))
@@ -735,17 +750,21 @@
     rs2 = Scatter(1, r.stage, r.inward2, r.outward, r.landed2, r.dm)
     for t in range(1, X):
 
-        def far(i, ahead):
+        def far(i):
             gm.from_pass(t, i)
             outputs(block_of(t, False), i)
             rs2.mate_one(t, i, part_merged)
+            if i >= 2:
+                rs2.peer_one(t, i - 1, part_merged)
             outputs(block_of(t, True), i)
-            if ahead:
+            if i + 2 < ipd:
                 gm.from_peer(t, i + 2)
-            rs2.peer_one(t, i, part_merged)
-
-        loop(ipd - 2, lambda i: far(i, True))
-        lax.fori_loop(ipd - 2, ipd, lambda i, carry: (far(i, False), carry)[1], 0)
+            if i == 0:
+                rs2.peer_one(t, 0, part_merged)
+
+        for i in range(ipd):
+            far(i)
+        rs2.peer_one(t, ipd - 1, part_merged)
 
     def near(i):
         gm.from_mate(i)
@@ -866,12 +885,11 @@
 
     everyone_wait(r.g5, 4)
     everyone_wait(r.g4, 3)
-    up_gap = r.gate_up[:, 0:width] - r.gate_up[:, width:two]
 
     def gate_back(n, state):
         at = gate_block(n)
         grad_lo, grad_hi = lower_upper(r.g4, n)
-        grad = exact_nt(grad_lo, up_gap[:, 0:LANES]) + exact_nt(grad_hi, up_gap[:, LANES:width])
+        grad = exact(grad_lo, r.gapt[0:LANES, :]) + exact(grad_hi, r.gapt[LANES:width, :])
         grad = grad * r.gate_slope[at, :]
         r.grad_down[at, :] = grad
         return state[0] + total(grad), state[1] + total(grad * r.gate_x[at, :])
@@ -884,7 +902,7 @@
         grad = r.grad_down[at, :] - gate_shift_all * every - r.gate_x[at, :] * (gate_gain_all * every)
         grad = jnp.where(valid, lead * grad, 0.0)
         r.grad_down[at, :] = grad
-        summary = exact_nt(grad, r.gate_down[...])
+        summary = exact(grad, r.downt[...])
         slots = gate_rows // 8
 
         @pl.when(n == 0)
@@ -950,50 +968,6 @@
         strips(i * CELLS, body, 0)
 
     loop(ipd, splits_back)
-
-    drain(r.ebuf.at[pl.ds(1, DP - 1)], r.eg_recv.at[0])
-    value = r.eg[piece_rows(0), :]
-    for d in range(1, DP):
-        value = value + r.ebuf[d].astype(F32)
-    r.eo[0] = value.astype(et)
-    for d in range(1, DP):
-        remote(r.eo.at[0], r.eo.at[DP - d], r.eg_send.at[1], r.eg_recv.at[1], across(d)).start()
-
-    def first_back(n, state):
-        there = pl.ds(pl.multiple_of((ch * ipd + 2 * n) * CELLS, 2 * CELLS), 2 * CELLS)
-        out = []
-        for g in range(2):
-            lanes = slice(g * half, (g + 1) * half)
-            left = jnp.concatenate(
-                [
-                    r.dsh[g, pl.ds(2 * n, 2), (2 - k) * SIDE : (2 - k) * SIDE + CELLS, :].reshape(2 * CELLS, 3 * width)
-                    for k in range(3)
-                ],
-                axis=1,
-            )
-            value = dot(left, r.wt[g]) * r.slope1[two_of(n), lanes]
-            r.dh1[there, lanes] = value.astype(BF16)
-            out.append((state[g][0] + fold(value), state[g][1] + fold(value * r.red[two_of(n), lanes])))
-        return tuple(out)
-
-    zero_h = jnp.zeros((8, half), F32)
-    gd = Gather(2, lambda b, i: r.dh1.at[rows_of(b, i)], lambda b: r.dh1.at[block_rows(b)], ipd)
-    state = ((zero_h, zero_h), (zero_h, zero_h))
-    for n in range(ipd // 2):
-        state = first_back(n, state)
-        if n == 0:
-            loop(2, gd.send)
-    for g in range(2):
-        r.g6[0, g : g + 1, :] = total(state[g][0])
-        r.g6[0, 2 + g : 3 + g, :] = total(state[g][1])
-    everyone(r.g6, 5)
-    lax.fori_loop(2, ipd, lambda i, carry: (gd.send(i), carry)[1], 0)
-
-    def pass_x(i):
-        for t in range(1, X):
-            gx.from_peer(t, i)
-
-    loop(ipd, pass_x)
 
     drain(r.stage, r.rs_core_send.at[1])
 
@@ -1066,8 +1040,57 @@
         if c.split_inside:
             step(k)
 
+    def first_back(i, many, state):
+        size = many * CELLS
+        there = pl.ds(pl.multiple_of((ch * ipd + i) * CELLS, CELLS), size)
+        here = slice(i * CELLS, i * CELLS + size)
+        out = []
+        for g in range(2):
+            lanes = slice(g * half, (g + 1) * half)
+            left = jnp.concatenate(
+                [
+                    r.dsh[g, i : i + many, (2 - k) * SIDE : (2 - k) * SIDE + CELLS, :].reshape(size, 3 * width)
+                    for k in range(3)
+                ],
+                axis=1,
+            )
+            value = dot(left, r.wt[g]) * r.slope1[here, lanes]
+            r.dh1[there, lanes] = value.astype(BF16)
+            out.append((state[g][0] + fold(value), state[g][1] + fold(value * r.red[here, lanes])))
+        return tuple(out)
+
+    zero_h = jnp.zeros((8, half), F32)
+    gd = Gather(2, lambda b, i: r.dh1.at[rows_of(b, i)], lambda b: r.dh1.at[block_rows(b)], ipd)
+    state = ((zero_h, zero_h), (zero_h, zero_h))
+    for i in range(2):
+        state = first_back(i, 1, state)
+        gd.send(i)
+        if i == 0:
+            for k in range(3):
+                split_step(split_cores, k)
+    if ipd > 2:
+        state = first_back(2, ipd - 2, state)
+    for g in range(2):
+        r.g6[0, g : g + 1, :] = total(state[g][0])
+        r.g6[0, 2 + g : 3 + g, :] = total(state[g][1])
+    everyone(r.g6, 5)
+    lax.fori_loop(2, ipd, lambda i, carry: (gd.send(i), carry)[1], 0)
+
+    def pass_x(i):
+        for t in range(1, X):
+            gx.from_peer(t, i)
+
+    loop(ipd, pass_x)
+
+    drain(r.ebuf.at[pl.ds(1, DP - 1)], r.eg_recv.at[0])
+    value = r.eg[piece_rows(0), :]
+    for d in range(1, DP):
+        value = value + r.ebuf[d].astype(F32)
+    r.eo[0] = value.astype(et)
+    for d in range(1, DP):
+        remote(r.eo.at[0], r.eo.at[DP - d], r.eg_send.at[1], r.eg_recv.at[1], across(d)).start()
     for k in range(3):
-        split_step(split_cores, k)
+        split_step(split_pairs, k)
     everyone_wait(r.g6, 5)
     sums = jnp.sum(r.g6[...], axis=0)
     shift_grad, gain_grad = get(sums, 0, width), get(sums, 2, width)
@@ -1105,7 +1128,7 @@
         reduced_back(block_of(0, False), i)
 
     loop(ipd, from_mate)
-    split_step(split_pairs, 0)
+    split_step(split_chips, 0)
     for t in range(1, X):
 
         def from_peer(i):
@@ -1113,7 +1136,7 @@
             reduced_back(block_of(t, True), i)
 
         loop(ipd, from_peer)
-    split_step(split_pairs, 1)
+    split_step(split_chips, 1)
     for t in range(1, X):
 
         def from_pass(i):
@@ -1122,19 +1145,18 @@
 
         loop(ipd, from_pass)
 
+    split_step(split_chips, 2)
     if c.reduce_inside:
         r.rs[...] = r.rg[...].T.astype(r.rs.dtype)
         for d in range(1, DP):
             remote(r.rs.at[piece_rows(d)], r.rbuf.at[DP - d], r.rg_send.at[0], r.rg_recv.at[0], across(d)).start()
     else:
         r.reduce_part[...] = r.rg[...].T
-    split_step(split_pairs, 2)
-    split_step(split_chips, 0)
+    split_step(split_out, 0)
     loop(ipd, lambda i: input_back(ch, i))
-    split_step(split_chips, 1)
+    split_step(split_out, 1)
     loop(ipd, lambda i: input_back(block_of(0, False), i))
-    split_step(split_out, 0)
-    split_step(split_chips, 2)
+    split_step(split_out, 2)
     if c.reduce_inside:
         groups = DP // CH
         goal = dp // groups
@@ -1155,10 +1177,8 @@
         def _():
             remote(r.rsum, slot, r.rg_send.at[2], r.rg_recv.at[1], (dp, goal)).start()
 
-    split_step(split_out, 1)
     for t in range(1, X):
         loop(ipd, lambda i: input_back(block_of(t, True), i))
-    split_step(split_out, 2)
     for t in range(1, X):
         loop(ipd, lambda i: input_back(block_of(t, False), i))
     r.second_gain_grad[...] = exact_nt(gain_grad2, pick2)
@@ -1205,7 +1225,7 @@
                 )
                 r.split_grad[3 * k + p] = block.T
 
-    for k, buf in enumerate((r.g1, r.g2, r.g3, r.g4, r.g5, r.g6, r.c2)):
+    for k, buf in enumerate((r.g1, r.g2, r.g3, r.g4, r.g5, r.g6, r.c2, r.g0)):
         everyone_done(buf, k)
     column_done(r.c1, 0)
     row_done(r.r1, 1)
@@ -1330,7 +1350,7 @@
 
         eg=V((width, cw), F32), es=V((width, cw), piece_type), ebuf=V((DP, piece, cw), piece_type),
         eo=V((DP, piece, cw), piece_type), rg=V((cw, width), F32),
-        all_send=dma(7), all_recv=dma(7), col_send=dma(4), col_recv=dma(4), row_send=dma(3), row_recv=dma(3),
+        all_send=dma(8), all_recv=dma(8), col_send=dma(4), col_recv=dma(4), row_send=dma(3), row_recv=dma(3),
         rs_core_send=dma(2), rs_core_recv=dma(2, X, ipd), rs_chip_send=dma(2), rs_chip_recv=dma(2, X, ipd),
         ag_core_send=dma(3), ag_core_recv=dma(3, ipd), ag_chip_send=dma(3, X), ag_chip_recv=dma(3, X, ipd),
         ag_pass_send=dma(3, X), ag_pass_recv=dma(3, X, ipd), sh_core_send=dma(2), sh_core_recv=dma(2),
@@ -1343,8 +1363,10 @@
         ("stage", X), ("inward", X), ("outward", X - 1), ("landed", X - 1), ("inward2", X), ("landed2", X - 1)
     ):
         scratch[name] = V((count, ipd, CELLS, width), BF16)
-    for k in range(1, 5):
+    for k in range(2, 5):
         scratch[f"g{k}"] = V((D, 8, LANES), F32)
+    scratch["g0"] = V((D, 4, LANES), F32)
+    scratch["g1"] = V((D, 4, LANES), F32)
     scratch["r4"] = V((CH, 8, LANES), F32)
     scratch["c4"] = V((DP, 8, LANES), F32)
     scratch["g5"] = V((D, 16 * width // LANES, LANES), BF16)
@@ -1358,6 +1380,8 @@
     scratch["mix"] = V((width, width), F32)
     scratch["mixb"] = V((width, width), BF16)
     scratch["offset"] = V((16, width), F32)
+    scratch["gapt"] = V((width, LANES), F32)
+    scratch["downt"] = V((LANES, width), F32)
     scratch["wxt"] = V((CH, cw, width), BF16)
     scratch["c2"] = V((D, 4, LANES), F32)
     scratch["g6"] = V((D, 4, LANES), F32)

time: 133 us -> 128 us (0.962)
  Pallas kernels: 132 us -> 127 us
    pallas_call x1, Pallas kernels: 126 us -> 121 us  [per_device(): pl.pallas_call(functools.partial(kernel, c, names), out_shape=tuple(outs....]
where the time goes in v5:
time: 128 us
  Pallas kernels  127 us (99%)
    pallas_call x1, Pallas kernels, per_device(): pl.pallas_call(functools.partial(kernel, c, names), out_shape=tuple(outs....  121 us
    pallas_call x1, Pallas kernels, per_device(): pl.pallas_call(hand_over, out_shape=tuple(outs.values()), in_specs=[anywh...  5.58 us

profile of v5, /device:TPU:0, one launch (start us, length us, event | category | flops | bytes accessed | tf_op | source)
XLA Modules:
  0.0 127.6 jit_solution(14898883652981294789)
XLA Ops:
  0.7 121.2 %block.1 = (bf16[4096,256]{1,0:T(8,128)(2,1)}, bf16[4096,256]{1,0:T(8,128)(2,1)}, f32[1,64]{1,0:T(1,128)}, f32[1,64]{1,0:T(1,128)}, f32[1,128]{1,0:T(1,128)}, /*...) custom-call(bf16[4096,256]{1,0:T(8,128)(2,1)} %refs_0_.1, ...), custom_call_target="tpu_custom_call" | custom-call | tf_op jit(solution)/shard_map/block/pallas_call | solution.py:1409
  121.9 5.6 %results.1 = (bf16[4096,256]{1,0:T(8,128)(2,1)}, bf16[4096,256]{1,0:T(8,128)(2,1)}, f32[1,64]{1,0:T(1,128)}, f32[1,64]{1,0:T(1,128)}, f32[1,128]{1,0:T(1,128)}, ...) custom-call(bf16[4096,256]{1,0:T(8,128)(2,1)} %get-tuple-element.48., ...), custom_call_target="tpu_custom_call" | custom-call | tf_op jit(solution)/shard_map/results/pallas_call | solution.py:1420

commit v6 on v5

--- a/solution.py
+++ b/solution.py
@@ -17,7 +17,7 @@
 F32 = jnp.float32
 BF16 = jnp.bfloat16
 MESH = pl.DeviceIdType.MESH
-STRIP = 32
+STRIP = 64
 
 
 def wide(mask, width):

time: 128 us -> 127 us (level)
  no operation moved by 1% of the time
where the time goes in v6:
time: 127 us
  Pallas kernels  126 us (99%)
    pallas_call x1, Pallas kernels, per_device(): pl.pallas_call(functools.partial(kernel, c, names), out_shape=tuple(outs....  120 us
    pallas_call x1, Pallas kernels, per_device(): pl.pallas_call(hand_over, out_shape=tuple(outs.values()), in_specs=[anywh...  5.58 us

profile of v6, /device:TPU:0, one launch (start us, length us, event | category | flops | bytes accessed | tf_op | source)
XLA Modules:
  0.0 126.7 jit_solution(17112823003899434001)
XLA Ops:
  0.7 120.3 %block.1 = (bf16[4096,256]{1,0:T(8,128)(2,1)}, bf16[4096,256]{1,0:T(8,128)(2,1)}, f32[1,64]{1,0:T(1,128)}, f32[1,64]{1,0:T(1,128)}, f32[1,128]{1,0:T(1,128)}, /*...) custom-call(bf16[4096,256]{1,0:T(8,128)(2,1)} %refs_0_.1, ...), custom_call_target="tpu_custom_call" | custom-call | tf_op jit(solution)/shard_map/block/pallas_call | solution.py:1409
  121.0 5.6 %results.1 = (bf16[4096,256]{1,0:T(8,128)(2,1)}, bf16[4096,256]{1,0:T(8,128)(2,1)}, f32[1,64]{1,0:T(1,128)}, f32[1,64]{1,0:T(1,128)}, f32[1,128]{1,0:T(1,128)}, ...) custom-call(bf16[4096,256]{1,0:T(8,128)(2,1)} %get-tuple-element.48., ...), custom_call_target="tpu_custom_call" | custom-call | tf_op jit(solution)/shard_map/results/pallas_call | solution.py:1420
